TPU v7x, 128 devices: a whole 4x4x4 slice. The times are simulated.
128 devices in a mesh: lat: 16 (over x, z), wave: 8 (over y, core).
Axes of the slice: x: 4, y: 4, z: 4, core: 2. Of those that a mesh axis runs over, the one named last changes fastest.
Arguments:
- spectra: bfloat16 [16, 2, 640, 640], P('lat', None, 'wave'), may hold values from -6 to 6
- legendre: bfloat16 [640, 2560, 640], P('wave', 'lat'), may hold values from -0.25 to 0.25
- wave_order: int32 [640], replicated, may hold values from 0 to 639, as said below
- writer_order: int32 [16], replicated, may hold values from 0 to 15, each once
Outputs:
- coefficients: bfloat16 [16, 2560, 5120], P('wave', 'lat')
Inputs may be any that keep to these rules, and one draw needn't show every extreme that they name: `wave_order`: a permutation of 0 to 639; for every q, slots 2q and 2q+1 hold wavenumbers m and 639-m with m < 320.
All inputs are finite; a program needn't handle non-finite values.
Results may differ from a plain program's by a relative error of at most 0.0056.
Values may be sent and summed in bfloat16 or wider, within the bound.
No kernel may reach another device: no remote copies, remote signals or barrier semaphores. Data moves between devices by JAX's collectives and lax.ppermute only.
A program may use at most 192 MiB of HBM per device.

v0:
```python
import math

import jax
import jax.numpy as jnp
from jax import lax
from jax.sharding import PartitionSpec as P

NLON = 5120
WL = 5


LIFT_ALPHA = -1.586134342059924
LIFT_BETA = -0.052980118572961
LIFT_GAMMA = 0.882911075530934
LIFT_DELTA = 0.443506852043971
LIFT_KAPPA = 1.149604398860241


def trimmed(values, lower, upper, along):
    return lax.slice_in_dim(values, lower, values.shape[along] - upper, 1, along)


def lifting(extended, along):
    length = extended.shape[along]
    even_rows = lax.slice_in_dim(extended, 0, length, 2, along)
    odd_rows = lax.slice_in_dim(extended, 1, length, 2, along)
    first_d = trimmed(odd_rows, 0, 1, along) + LIFT_ALPHA * (
        trimmed(even_rows, 0, 1, along) + trimmed(even_rows, 1, 0, along)
    )
    first_s = trimmed(even_rows, 1, 1, along) + LIFT_BETA * (
        trimmed(first_d, 0, 1, along) + trimmed(first_d, 1, 0, along)
    )
    second_d = trimmed(first_d, 1, 1, along) + LIFT_GAMMA * (
        trimmed(first_s, 0, 1, along) + trimmed(first_s, 1, 0, along)
    )
    second_s = trimmed(first_s, 1, 1, along) + LIFT_DELTA * (
        trimmed(second_d, 0, 1, along) + trimmed(second_d, 1, 0, along)
    )
    return (second_s * LIFT_KAPPA, trimmed(second_d, 1, 0, along) / LIFT_KAPPA)


def pair_up(smooth, detail, along):
    stacked = jnp.stack([smooth, detail], axis=along + 1)
    shape = list(smooth.shape)
    shape[along] = shape[along] * 2
    return stacked.reshape(shape)


def analyze(values, along, levels, extend):
    if levels == 0:
        return values
    smooth, detail = lifting(extend(values), along)
    return pair_up(analyze(smooth, along, levels - 1, extend), detail, along)


def padding(values, along, mode_name):
    widths = [(0, 0)] * values.ndim
    widths[along] = (4, 4)
    return jnp.pad(values, widths, mode=mode_name)


def dft_table(slots, count_lon, count_waves):
    lon_index = jnp.arange(count_lon, dtype=jnp.int32)
    phase = slots[:, None] * lon_index[None, :] % count_lon
    angle = phase.astype(jnp.float32) * (2.0 * math.pi / count_lon)
    weight = jnp.where(slots == 0, 1.0, 2.0).astype(jnp.float32) / math.sqrt(2.0 * count_waves)
    cosine_part = (weight[:, None] * jnp.cos(angle)).astype(jnp.bfloat16)
    sine_part = (-weight[:, None] * jnp.sin(angle)).astype(jnp.bfloat16)
    return jnp.concatenate([cosine_part, sine_part], axis=0)


def on_device(spectra, legendre, wave_order, writer_order):
    slot_count = legendre.shape[0]
    total_n = legendre.shape[2]
    first_slot = lax.axis_index("wave") * slot_count
    local_waves = lax.dynamic_slice_in_dim(wave_order, first_slot, slot_count)
    keep = jnp.arange(total_n, dtype=jnp.int32)[None, :] >= local_waves[:, None]
    piece = lax.all_gather(spectra, "lat", axis=0, tiled=True)
    masked = jnp.where(keep[None, None], piece, jnp.zeros_like(piece))
    partial_sums = jnp.einsum(
        "frmn,mln->flrm", masked, legendre, preferred_element_type=jnp.float32
    )
    legendre_out = partial_sums.astype(jnp.bfloat16)
    ordered = jnp.take(legendre_out, writer_order, axis=0)
    fourier = lax.all_to_all(ordered, "wave", split_axis=0, concat_axis=3, tiled=True)
    fields, band, pairs, waves_all = fourier.shape
    table = dft_table(wave_order, NLON, waves_all)
    grid = jnp.dot(
        fourier.reshape(fields * band, pairs * waves_all), table, preferred_element_type=jnp.float32
    )
    grid = grid.reshape(fields, band, NLON)
    rowwise = analyze(grid, 2, WL, lambda values: padding(values, 2, "wrap"))
    columns = lax.all_to_all(rowwise, "lat", split_axis=2, concat_axis=1, tiled=True)
    finished = analyze(columns, 1, WL, lambda values: padding(values, 1, "reflect")).astype(
        jnp.bfloat16
    )
    return lax.all_to_all(finished, "lat", split_axis=1, concat_axis=2, tiled=True)


def solution(mesh):
    return jax.shard_map(
        on_device,
        mesh=mesh,
        in_specs=(P("lat", None, "wave", None), P("wave", "lat", None), P(), P()),
        out_specs=P("wave", "lat", None),
        check_vma=False,
    )
```

profile of v0, /device:TPU:2, one launch (start us, length us, event | category | flops | bytes accessed | tf_op | source)
XLA Modules:
  0.0 1043.2 jit_solution(16854227844474987930)
XLA Ops:
  10.1 49.4 %all-gather.2.cloned.1.call-done = bf16[16,2,80,640]{3,2,1,0:T(8,128)(2,1)} async-done(((bf16[1,2,80,640]{3,2,1,0:T(8,128)(2,1)}), bf16[16,2,80,640]{3,2,1,0:T(8,128)(2,1)}) %all-gather.2.cloned.1.call-update) | async-done | bytes 3276816 | tf_op jit(solution)/shard_map/all_gather | solution.py:78
  59.6 2.3 broadcast_select_fusion
  61.8 12.7 %fusion.53 = bf16[16,160,2,80]{1,0,2,3:T(8,128)(2,1)} fusion(bf16[80,160,640]{2,1,0:T(8,128)(2,1)} %param.5, bf16[16,2,80,640]{3,2,1,0:T(8,128)(2,1)S(1)} %broadcast_select_fusion), kind=kOutput, calls=%fused_computation.82 | convolution fusion | flops 524697600 | bytes 20480000 | tf_op jit(solution)/shard_map/frmn,mln->flrm/dot_general | solution.py:80
  74.6 2.4 copy.60
  77.8 1.2 broadcast_select_fusion.1
  79.1 4.6 all-to-all-start
  83.7 58.5 %multiply_convert_fusion.1 = (bf16[640,5120]{1,0:T(8,128)(2,1)}, bf16[640,5120]{1,0:T(8,128)(2,1)}) fusion(s32[640]{0:T(1024)S(1)} %copy-done.6, f32[640]{0:T(1024)S(1)} %get-tuple-element.47, f32[640]{0:T(1024)S(1)} %get-tuple-element.48), kind=kLoop, calls=%fused_computation.11 | loop fusion | flops 42598400 | bytes 13114880 | tf_op jit(solution)/shard_map/convert_element_type | solution.py:67
  143.0 1.3 dot_general.9
  144.4 7.5 fusion.4
  151.9 2.8 copy-done.4
  154.8 9.0 concatenate.44
  163.8 110.2 %slice.512 = f32[2,160,2564]{2,1,0:T(8,128)S(1)} slice(f32[2,160,5128]{2,1,0:T(8,128)} %concatenate.44), slice={[0:2:1], [0:160:1], [0:5128:2]} | slice | bytes 6563840 | tf_op jit(solution)/shard_map/slice | solution.py:25
  274.0 110.9 %slice.514 = f32[2,160,2564]{2,1,0:T(8,128)} slice(f32[2,160,5128]{2,1,0:T(8,128)} %concatenate.44), slice={[0:2:1], [0:160:1], [1:5128:2]} | slice | bytes 6563840 | tf_op jit(solution)/shard_map/slice | solution.py:26
  384.9 2.9 fusion.24
  387.8 2.3 fusion.22
  390.2 2.0 fusion.20
  392.2 3.4 fusion.27
  396.4 4.0 concatenate.45
  400.4 58.9 %slice.528 = f32[2,160,1284]{2,1,0:T(8,128)S(1)} slice(f32[2,160,2568]{2,1,0:T(8,128)} %concatenate.45), slice={[0:2:1], [0:160:1], [0:2568:2]} | slice | bytes 3287040 | tf_op jit(solution)/shard_map/slice | solution.py:25
  459.3 59.1 %slice.530 = f32[2,160,1284]{2,1,0:T(8,128)} slice(f32[2,160,2568]{2,1,0:T(8,128)} %concatenate.45), slice={[0:2:1], [0:160:1], [1:2568:2]} | slice | bytes 3287040 | tf_op jit(solution)/shard_map/slice | solution.py:26
  518.4 2.0 fusion.44
  520.4 1.2 fusion.42
  522.6 2.1 fusion.47
  525.5 1.9 concatenate.46
  527.4 28.0 %slice.544 = f32[2,160,644]{2,1,0:T(8,128)S(1)} slice(f32[2,160,1288]{2,1,0:T(8,128)S(1)} %concatenate.46), slice={[0:2:1], [0:160:1], [0:1288:2]} | slice | bytes 1648640 | tf_op jit(solution)/shard_map/slice | solution.py:25
  555.4 28.3 %slice.546 = f32[2,160,644]{2,1,0:T(8,128)} slice(f32[2,160,1288]{2,1,0:T(8,128)S(1)} %concatenate.46), slice={[0:2:1], [0:160:1], [1:1288:2]} | slice | bytes 1648640 | tf_op jit(solution)/shard_map/slice | solution.py:26
  583.7 1.5 fusion.73
  587.4 14.0 %slice.560 = f32[2,160,324]{2,1,0:T(8,128)S(1)} slice(f32[2,160,648]{2,1,0:T(8,128)S(1)} %pad_maximum_fusion.7), slice={[0:2:1], [0:160:1], [0:648:2]} | slice | bytes 829440 | tf_op jit(solution)/shard_map/slice | solution.py:25
  601.4 14.4 %slice.562 = f32[2,160,324]{2,1,0:T(8,128)S(1)} slice(f32[2,160,648]{2,1,0:T(8,128)S(1)} %pad_maximum_fusion.7), slice={[0:2:1], [0:160:1], [1:648:2]} | slice | bytes 829440 | tf_op jit(solution)/shard_map/slice | solution.py:26
  616.7 1.1 fusion.89
  618.2 7.1 slice.576
  625.3 7.1 slice.578
  634.2 1.1 pad_maximum_fusion.8
  637.0 1.3 pad_maximum_fusion.5
  638.3 3.7 copy.66
  642.0 3.2 copy.67
  645.2 2.2 pad_maximum_fusion.2
  647.4 5.4 copy.68
  652.8 6.4 copy.69
  659.2 5.2 pad_maximum_fusion
  664.5 15.2 %copy.70 = f32[2,160,2560,2]{1,0,3,2:T(2,128)} copy(f32[2,160,2560,2]{2,1,0,3:T(8,128)} %pad_maximum_fusion) | data formatting | bytes 13107200 | tf_op jit(solution)/shard_map/stack | solution.py:43
  679.7 122.9 %all_to_all.51 = f32[2,160,5120]{1,0,2:T(2,128)} all-to-all(f32[2,160,5120]{1,0,2:T(2,128)} %bitcast.64), channel_id=1, replica_groups=mesh['lat'=16,'wave'=8] {'lat'}, dimensions={2} | all-to-all | bytes 13107200 | tf_op jit(solution)/shard_map/all_to_all | solution.py:93
  802.5 13.9 %copy.85 = f32[2,160,16,320]{3,1,2,0:T(8,128)} copy(f32[2,160,16,320]{1,0,3,2:T(2,128)} %bitcast.65) | data formatting | bytes 13107200 | tf_op jit(solution)/shard_map/all_to_all | solution.py:93
  817.4 22.5 %concatenate.49 = f32[2,2568,320]{2,1,0:T(8,128)} concatenate(f32[2,4,320]{2,1,0:T(4,128)S(1)} %rev.41, f32[2,2560,320]{2,1,0:T(8,128)} %bitcast.67, f32[2,4,320]{2,1,0:T(4,128)S(1)} %rev.42), dimensions={1} | concatenate | bytes 13148160 | tf_op jit(solution)/shard_map/jit(_pad)/concatenate | solution.py:59
  839.9 19.4 %slice.592 = f32[2,1284,320]{2,1,0:T(8,128)} slice(f32[2,2568,320]{2,1,0:T(8,128)} %concatenate.49), slice={[0:2:1], [0:2568:2], [0:320:1]} | slice | bytes 6574080 | tf_op jit(solution)/shard_map/slice | solution.py:25
  859.2 19.4 %slice.594 = f32[2,1284,320]{2,1,0:T(8,128)} slice(f32[2,2568,320]{2,1,0:T(8,128)} %concatenate.49), slice={[0:2:1], [1:2568:2], [0:320:1]} | slice | bytes 6574080 | tf_op jit(solution)/shard_map/slice | solution.py:26
  878.6 5.2 fusion.15
  886.0 2.6 fusion.18
  888.6 1.9 copy-done.1
  890.7 13.3 %concatenate.50 = f32[2,1288,320]{2,1,0:T(8,128)} concatenate(f32[2,4,320]{2,1,0:T(4,128)S(1)} %rev.43, f32[2,1280,320]{2,1,0:T(8,128)} %copy-done.1, f32[2,4,320]{2,1,0:T(4,128)S(1)} %rev.44), dimensions={1} | concatenate | bytes 6594560 | tf_op jit(solution)/shard_map/jit(_pad)/concatenate | solution.py:59
  904.0 9.1 slice.608
  913.1 10.6 %slice.610 = f32[2,644,320]{2,1,0:T(8,128)} slice(f32[2,1288,320]{2,1,0:T(8,128)} %concatenate.50), slice={[0:2:1], [1:1288:2], [0:320:1]} | slice | bytes 3297280 | tf_op jit(solution)/shard_map/slice | solution.py:26
  923.7 1.9 fusion.34
  926.5 1.6 fusion.38
  928.1 1.3 copy-done.2
  929.6 1.7 pad_maximum_fusion.3
  932.2 3.6 slice.626
  935.8 1.4 fusion.63
  942.7 1.0 copy.76
  944.2 2.0 copy.78
  947.3 25.3 %copy.80 = bf16[2,1280,2,320]{3,0,2,1:T(2,128)(2,1)S(1)} copy(bf16[2,1280,2,320]{3,1,0,2:T(8,128)(2,1)S(1)} %pad_maximum_fusion.1) | data formatting | bytes 6553600 | tf_op jit(solution)/shard_map/stack | solution.py:43
  972.6 52.3 %all_to_all.52 = bf16[2,2560,320]{2,0,1:T(2,128)(2,1)S(1)} all-to-all(bf16[2,2560,320]{2,0,1:T(2,128)(2,1)S(1)} %bitcast.69), channel_id=1, replica_groups=mesh['lat'=16,'wave'=8] {'lat'}, dimensions={1} | all-to-all | bytes 6553600 | tf_op jit(solution)/shard_map/all_to_all | solution.py:97
  1025.4 3.4 copy.82
  1028.8 7.3 all_to_all.47
  (94 shorter events, 27.4 us)
Async XLA Ops:
  6.5 53.0 %all-gather.2.cloned.1.call-start = ((), (), s32[]{:S(2)}) async-start(), calls=%async_computation.3 | async-start | bytes 3481600 | tf_op jit(solution)/shard_map/all_gather | solution.py:78
  77.8 5.9 copy-start.6
  79.1 63.1 %all-to-all-start = ((bf16[16,160,2,80]{3,1,2,0:T(8,128)(2,1)}), bf16[16,160,2,80]{3,1,2,0:T(8,128)(2,1)S(1)}, u32[]{:S(2)}, u32[]{:S(2)}) async-start(bf16[16,160,2,80]{3,1,2,0:T(8,128)(2,1)} %broadcast_select_fusion.1), calls=%async_computation | async-start | bytes 2621440 | tf_op jit(solution)/shard_map/all_to_all | solution.py:85
  151.9 2.8 copy-start.4
  878.6 5.6 copy-start
  888.6 1.9 copy-start.1
  928.1 1.3 copy-start.2
  942.4 1.4 copy-start.5
  944.2 2.3 copy-start.3
Sparse Core Ops, SparseCore 0:
  9.5 49.9 all-gather.1
where the time goes:
time: 1050 us; the launch traced here: 1040 us
  local copies, waits for them, and re-layouts  661 us (63%)
  blocking collectives  175 us (17%)
  other arithmetic  118 us (11%)
  waiting for transfers between devices  50.1 us (5%)
  matrix products  20.3 us (2%)
  between operations  14.4 us (1%)
    slice x10, local copies, waits for them, and re-layouts, lifting(): odd_rows = lax.slice_in_dim(extended, 1, length, 2, along)  254 us
    slice x10, local copies, waits for them, and re-layouts, lifting(): even_rows = lax.slice_in_dim(extended, 0, length, 2, along)  248 us
    all_to_all x1, blocking collectives, on_device(): lax.all_to_all(rowwise, 'lat', split_axis=2, concat_axis=1, tiled=True)  123 us
    another operation x18, local copies, waits for them, and re-layouts, pair_up(): stacked = jnp.stack([smooth, detail], axis=along + 1)  66 us
    convert_element_type x1, other arithmetic, dft_table(): cosine_part = (weight[:, None] * jnp.cos(angle)).astype(jnp.bfloat16)  58.5 us
    all_to_all x1, blocking collectives, on_device(): lax.all_to_all(finished, 'lat', split_axis=1, concat_axis=2, tiled=True)  52.3 us
    concatenate x5, local copies, waits for them, and re-layouts, padding(): return jnp.pad(values, widths, mode=mode_name)  50.6 us
    all_gather x1, waiting for transfers between devices, on_device(): piece = lax.all_gather(spectra, 'lat', axis=0, tiled=True)  49.4 us
  transfers between devices with their start and end apart: 2, of which 1 were waited for; matrix products, arithmetic and copies ran while one was open for 6% of the time, Pallas kernels for 0%

commit v1 on v0

v1 whole, which is shorter than its diff:
```python
import math

import jax
import jax.numpy as jnp
import ml_dtypes
import numpy as np
from jax import lax
from jax.experimental import pallas as pl
from jax.experimental.pallas import tpu as pltpu
from jax.sharding import PartitionSpec as P

NLAT = 2560
NLON = 5120
NWAVE = 640
WL = 5
BANDS = 16
OWNERS = 8
BAND = NLAT // BANDS
SLOTS = NWAVE // OWNERS
PAIRS = SLOTS // 2
FIELDS = 16
BLOCKS = 6
LANE = 128
EDGE = 32
TILE = 512

LIFT_ALPHA = -1.586134342059924
LIFT_BETA = -0.052980118572961
LIFT_GAMMA = 0.882911075530934
LIFT_DELTA = 0.443506852043971
LIFT_KAPPA = 1.149604398860241


def analyze(values, levels, mode_name):
    if levels == 0:
        return values
    widths = [(4, 4)] + [(0, 0)] * (values.ndim - 1)
    extended = np.pad(values, widths, mode=mode_name)
    even, odd = extended[0::2], extended[1::2]
    first_d = odd[:-1] + LIFT_ALPHA * (even[:-1] + even[1:])
    first_s = even[1:-1] + LIFT_BETA * (first_d[:-1] + first_d[1:])
    second_d = first_d[1:-1] + LIFT_GAMMA * (first_s[:-1] + first_s[1:])
    second_s = first_s[1:-1] + LIFT_DELTA * (second_d[:-1] + second_d[1:])
    result = np.empty_like(values)
    result[0::2] = analyze(second_s * LIFT_KAPPA, levels - 1, mode_name)
    result[1::2] = second_d[1:] / LIFT_KAPPA
    return result


def longitude_matrix():
    waves = np.arange(NWAVE)
    phase = waves[:, None] * np.arange(NLON)[None, :] % NLON
    angle = phase * (2.0 * math.pi / NLON)
    weight = np.where(waves == 0, 1.0, 2.0)[:, None] / math.sqrt(2.0 * NWAVE)
    table = np.concatenate([weight * np.cos(angle), -weight * np.sin(angle)], axis=0)
    table = table.astype(np.float32).astype(ml_dtypes.bfloat16).astype(np.float64)
    return analyze(table.T, WL, "wrap").T.astype(np.float32).astype(ml_dtypes.bfloat16)


def latitude_matrices():
    whole = analyze(np.eye(NLAT), WL, "reflect")
    inner = whole[:, 7 * BAND : 8 * BAND]
    touched = np.nonzero((inner != 0).any(axis=1))[0]
    above = touched[touched < 7 * BAND] - 6 * BAND
    below = touched[touched >= 8 * BAND] - 8 * BAND
    out = np.zeros((3, 4, BAND, 4 * BAND + 8 * EDGE))
    for variant, band in enumerate((0, 7, BANDS - 1)):
        columns = whole[:, band * BAND : (band + 1) * BAND]
        own = columns[band * BAND : (band + 1) * BAND]
        for part in range(4):
            out[variant, part, :, part * BAND : (part + 1) * BAND] = own.T
            start = 4 * BAND + part * EDGE
            if band > 0:
                out[variant, part, :, start : start + len(above)] = columns[(band - 1) * BAND + above].T
            start += 4 * EDGE
            if band < BANDS - 1:
                out[variant, part, :, start : start + len(below)] = columns[(band + 1) * BAND + below].T
    place = np.zeros((2, 4 * EDGE, 4 * BAND))
    for part in range(4):
        place[0, part * EDGE + np.arange(len(above)), part * BAND + above] = 1.0
        place[1, part * EDGE + np.arange(len(below)), part * BAND + below] = 1.0
    return (
        out.astype(np.float32).astype(ml_dtypes.bfloat16),
        place.astype(ml_dtypes.bfloat16),
    )


def pack_kernel(order_ref, spectra_ref, real_ref, imag_ref, wide, low, high):
    first = lax.axis_index("wave") * SLOTS
    for pair in range(PAIRS):
        low[pl.ds(pair, 1), :] = jnp.full((1, LANE), order_ref[first + 2 * pair], jnp.int32)
        high[pl.ds(pair, 1), :] = jnp.full((1, LANE), order_ref[first + 2 * pair + 1], jnp.int32)
    waves_a, waves_b = low[...], high[...]
    lane = lax.broadcasted_iota(jnp.int32, (PAIRS, LANE), 1)
    for part, out in enumerate((real_ref, imag_ref)):
        for block in range(5):
            wide[block] = spectra_ref[0, part, :, block * LANE : (block + 1) * LANE].astype(jnp.float32)
        for block in range(BLOCKS):
            taken = jnp.zeros((PAIRS, LANE), jnp.float32)
            if block <= 4:
                values = wide[4 - block, pl.ds(1, PAIRS, stride=2), :]
                taken = jnp.where(lane + (4 - block) * LANE >= waves_b, values, taken)
            if block >= 1:
                values = wide[block - 1, pl.ds(0, PAIRS, stride=2), :]
                values = jnp.where(lane + (block - 1) * LANE >= waves_a, values, jnp.zeros_like(values))
                taken = jnp.where(waves_a < block * LANE, values, taken)
            out[:, block * LANE : (block + 1) * LANE] = taken.astype(jnp.bfloat16)


def legendre_kernel(order_ref, writer_ref, *refs):
    parts = refs[:8]
    legendre_ref, matrix_ref, own_ref, above_ref, below_ref = refs[8:13]
    held, spread, rows, matrix, sems, matrix_sem = refs[13:]
    first = lax.axis_index("wave") * SLOTS
    band = lax.axis_index("lat")
    variant = jnp.where(band == 0, 0, jnp.where(band == BANDS - 1, 2, 1))
    matrix_copy = pltpu.make_async_copy(matrix_ref.at[variant], matrix, matrix_sem)
    matrix_copy.start()

    def fetch(pair, carry):
        wave = order_ref[first + 2 * pair]
        for block in range(BLOCKS):
            from_a = wave < block * LANE
            slot = jnp.where(from_a, 2 * pair, 2 * pair + 1)
            source = jnp.where(from_a, block - 1, 4 - block)
            pltpu.make_async_copy(
                legendre_ref.at[slot, :, pl.ds(pl.multiple_of(source * LANE, LANE), LANE)],
                held.at[pair, :, pl.ds(block * LANE, LANE)],
                sems.at[pair],
            ).start()
        return carry

    lax.fori_loop(0, PAIRS, fetch, 0)

    band_x, band_z = band // 4, lax.rem(band, 4)
    steps = (0, 3, 1, 2)
    for outer in range(4):
        for inner in range(4):
            for part in range(2):
                along_x, along_z = (outer, inner) if part == 0 else (inner, outer)
                field = 4 * lax.rem(band_x + steps[along_x], 4) + lax.rem(band_z + steps[along_z], 4)
                start = pl.multiple_of((2 * field + part) * PAIRS, 8)
                for block in range(BLOCKS):
                    values = parts[4 * part + outer][inner, :, block * LANE : (block + 1) * LANE]
                    spread[block, pl.ds(start, PAIRS), :] = values.astype(jnp.float32)

    def contract(pair, carry):
        pltpu.make_async_copy(held.at[pair], held.at[pair], sems.at[pair]).wait()
        wave = order_ref[first + 2 * pair]
        lower, upper = [], []
        for block in range(BLOCKS):
            values = spread[block, pl.ds(pair, 2 * FIELDS, stride=PAIRS), :]
            from_a = wave < block * LANE
            lower.append(jnp.where(from_a, values, 0.0).astype(jnp.bfloat16))
            upper.append(jnp.where(from_a, 0.0, values).astype(jnp.bfloat16))
        left = jnp.concatenate(
            [jnp.concatenate(lower, axis=1), jnp.concatenate(upper, axis=1)], axis=0
        )
        sums = lax.dot_general(
            left, held[pair], (((1,), (1,)), ((), ())), preferred_element_type=jnp.float32
        )
        for which in range(2):
            piece = sums[which * 2 * FIELDS : (which + 1) * 2 * FIELDS]
            where = pl.ds(2 * pair + which, 2 * FIELDS, stride=SLOTS)
            rows[0, where, :] = piece[:, :LANE]
            rows[1, where, : BAND - LANE] = piece[:, LANE:]
        return carry

    lax.fori_loop(0, PAIRS, contract, 0)
    matrix_copy.wait()

    def lift(owner, carry):
        total = jnp.zeros((SLOTS, 4 * BAND + 8 * EDGE), jnp.float32)
        for part in range(4):
            field = writer_ref[2 * owner + part // 2]
            start = pl.multiple_of((2 * field + part % 2) * SLOTS, 8)
            left = jnp.concatenate(
                [rows[0, pl.ds(start, SLOTS), :], rows[1, pl.ds(start, SLOTS), : BAND - LANE]], axis=1
            ).astype(jnp.bfloat16)
            total += jnp.dot(left, matrix[part], preferred_element_type=jnp.float32)
        own_ref[owner] = total[:, : 4 * BAND]
        above_ref[owner] = total[:, 4 * BAND : 4 * BAND + 4 * EDGE].astype(jnp.bfloat16)
        below_ref[owner] = total[:, 4 * BAND + 4 * EDGE :].astype(jnp.bfloat16)
        return carry

    lax.fori_loop(0, OWNERS, lift, 0)


def join_kernel(own_ref, above_ref, below_ref, place_ref, out_ref):
    for owner in range(OWNERS):
        total = own_ref[owner]
        total += jnp.dot(above_ref[owner], place_ref[0], preferred_element_type=jnp.float32)
        total += jnp.dot(below_ref[owner], place_ref[1], preferred_element_type=jnp.float32)
        out_ref[owner] = total.astype(jnp.bfloat16)


def synthesis_kernel(order_ref, waves_ref, table_ref, out_ref, left):
    @pl.when(pl.program_id(0) == 0)
    def _():
        row = lax.broadcasted_iota(jnp.int32, (NWAVE, NWAVE), 0)
        chosen = jnp.where(row == order_ref[...], 1.0, 0.0).astype(jnp.bfloat16)
        ordered = jnp.dot(chosen, waves_ref[...], preferred_element_type=jnp.float32)
        turned = ordered.T.astype(jnp.bfloat16)
        for field in range(2):
            for part in range(2):
                left[field * BAND : (field + 1) * BAND, part * NWAVE : (part + 1) * NWAVE] = turned[
                    (2 * field + part) * BAND : (2 * field + part + 1) * BAND
                ]

    sums = jnp.dot(left[...], table_ref[...], preferred_element_type=jnp.float32)
    out_ref[0] = sums[:BAND].astype(jnp.bfloat16)
    out_ref[1] = sums[BAND:].astype(jnp.bfloat16)


def along_z(step):
    return [(4 * x + z, 4 * x + (z + step) % 4) for x in range(4) for z in range(4)]


def along_x(step):
    return [(4 * x + z, 4 * ((x + step) % 4) + z) for x in range(4) for z in range(4)]


def neighbour(step):
    return [(band, (band + step) % BANDS) for band in range(BANDS)]


SMEM = pl.BlockSpec(memory_space=pltpu.SMEM)
VMEM = pl.BlockSpec(memory_space=pltpu.VMEM)
ANY = pl.BlockSpec(memory_space=pl.ANY)


def make_on_device(table, matrices, place):
    def on_device(spectra, legendre, wave_order, writer_order):
        real, imag = pl.pallas_call(
            pack_kernel,
            out_shape=[jax.ShapeDtypeStruct((PAIRS, BLOCKS * LANE), jnp.bfloat16)] * 2,
            in_specs=[SMEM, VMEM],
            out_specs=[VMEM, VMEM],
            scratch_shapes=[
                pltpu.VMEM((5, SLOTS, LANE), jnp.float32),
                pltpu.VMEM((PAIRS, LANE), jnp.int32),
                pltpu.VMEM((PAIRS, LANE), jnp.int32),
            ],
            name="pack",
        )(wave_order, spectra)
        firsts = [[real], [imag]]
        for step in (1, 3, 2):
            firsts[0].append(lax.ppermute(real, "lat", along_z(step)))
            firsts[1].append(lax.ppermute(imag, "lat", along_x(step)))
        firsts = [jnp.stack(blocks) for blocks in firsts]
        seconds = [[firsts[0]], [firsts[1]]]
        for step in (1, 3, 2):
            seconds[0].append(lax.ppermute(firsts[0], "lat", along_x(step)))
            seconds[1].append(lax.ppermute(firsts[1], "lat", along_z(step)))

        width = 4 * BAND
        own, above, below = pl.pallas_call(
            legendre_kernel,
            out_shape=[
                jax.ShapeDtypeStruct((OWNERS, SLOTS, width), jnp.float32),
                jax.ShapeDtypeStruct((OWNERS, SLOTS, 4 * EDGE), jnp.bfloat16),
                jax.ShapeDtypeStruct((OWNERS, SLOTS, 4 * EDGE), jnp.bfloat16),
            ],
            in_specs=[SMEM, SMEM] + [VMEM] * 8 + [ANY, ANY],
            out_specs=[VMEM] * 3,
            scratch_shapes=[
                pltpu.VMEM((PAIRS, BAND, BLOCKS * LANE), jnp.bfloat16),
                pltpu.VMEM((BLOCKS, 2 * FIELDS * PAIRS, LANE), jnp.float32),
                pltpu.VMEM((2, 2 * FIELDS * SLOTS, LANE), jnp.float32),
                pltpu.VMEM((4, BAND, width + 8 * EDGE), jnp.bfloat16),
                pltpu.SemaphoreType.DMA((PAIRS,)),
                pltpu.SemaphoreType.DMA,
            ],
            compiler_params=pltpu.CompilerParams(vmem_limit_bytes=40 * 2**20),
            cost_estimate=pl.CostEstimate(flops=800_000_000, bytes_accessed=14_000_000, transcendentals=0),
            name="legendre",
        )(wave_order, writer_order, *seconds[0], *seconds[1], legendre, matrices)

        above = lax.ppermute(above, "lat", neighbour(-1))
        below = lax.ppermute(below, "lat", neighbour(1))
        joined = pl.pallas_call(
            join_kernel,
            out_shape=jax.ShapeDtypeStruct((OWNERS, SLOTS, width), jnp.bfloat16),
            in_specs=[VMEM] * 4,
            out_specs=VMEM,
            name="join",
        )(own, above, below, place)

        waves = lax.all_to_all(joined, "wave", split_axis=0, concat_axis=0, tiled=True)
        return pl.pallas_call(
            synthesis_kernel,
            grid=(NLON // TILE,),
            out_shape=jax.ShapeDtypeStruct((2, BAND, NLON), jnp.bfloat16),
            in_specs=[
                pl.BlockSpec((1, NWAVE), lambda j: (0, 0)),
                pl.BlockSpec((NWAVE, width), lambda j: (0, 0)),
                pl.BlockSpec((2 * NWAVE, TILE), lambda j: (0, j)),
            ],
            out_specs=pl.BlockSpec((2, BAND, TILE), lambda j: (0, 0, j)),
            scratch_shapes=[pltpu.VMEM((2 * BAND, 2 * NWAVE), jnp.bfloat16)],
            compiler_params=pltpu.CompilerParams(vmem_limit_bytes=40 * 2**20),
            cost_estimate=pl.CostEstimate(flops=4_400_000_000, bytes_accessed=18_000_000, transcendentals=0),
            name="synthesis",
        )(wave_order.reshape(1, NWAVE), waves.reshape(NWAVE, width), table)

    return on_device


def solution(mesh):
    table = longitude_matrix()
    matrices, place = latitude_matrices()
    return jax.shard_map(
        make_on_device(jnp.asarray(table), jnp.asarray(matrices), jnp.asarray(place)),
        mesh=mesh,
        in_specs=(P("lat", None, "wave", None), P("wave", "lat", None), P(), P()),
        out_specs=P("wave", "lat", None),
        check_vma=False,
    )
```

time: 1050 us -> 105 us (0.10)
  the two profiles are of different devices: /device:TPU:2 before, /device:TPU:1 now
where the time goes in v1:
time: 105 us
  waiting for transfers between devices  34.1 us (32%)
  starting transfers between devices  30.5 us (29%)
  Pallas kernels  28.6 us (27%)
  local copies, waits for them, and re-layouts  9.87 us (9%)
  other arithmetic  1.72 us (2%)
    pallas_call x1, Pallas kernels, on_device(): pl.pallas_call(legendre_kernel, out_shape=[jax.ShapeDtypeStruct((OWNERS,...  15 us
    all_to_all x1, waiting for transfers between devices, on_device(): lax.all_to_all(joined, 'wave', split_axis=0, concat_axis=0, tiled=True)  12.6 us
    unnamed x16, local copies, waits for them, and re-layouts  9.87 us
    pallas_call x1, Pallas kernels, on_device(): pl.pallas_call(synthesis_kernel, grid=(NLON // TILE,), out_shape=jax.Shap...  8.72 us
    all_to_all x1, starting transfers between devices, on_device(): lax.all_to_all(joined, 'wave', split_axis=0, concat_axis=0, tiled=True)  8.17 us
    ppermute x3, waiting for transfers between devices, on_device(): seconds[0].append(lax.ppermute(firsts[0], 'lat', along_x(step)))  7.02 us
    ppermute x3, starting transfers between devices, on_device(): seconds[1].append(lax.ppermute(firsts[1], 'lat', along_z(step)))  7.01 us
    ppermute x1, waiting for transfers between devices, on_device(): below = lax.ppermute(below, 'lat', neighbour(1))  5.22 us
  transfers between devices with their start and end apart: 15, of which 12 were waited for; matrix products, arithmetic and copies ran while one was open for 1% of the time, Pallas kernels for 0%

profile of v1, /device:TPU:1, one launch (start us, length us, event | category | flops | bytes accessed | tf_op | source)
XLA Modules:
  0.0 104.9 jit_solution(4592962376758726791)
XLA Ops:
  0.0 1.7 %pack.1 = (bf16[40,768]{1,0:T(8,128)(2,1)}, bf16[40,768]{1,0:T(8,128)(2,1)}) custom-call(s32[640]{0:T(1024)} %order_ref.3, bf16[1,2,80,640]{3,2,1,0:T(8,128)(2,1)} %spectra_ref.1), custom_call_target="tpu_custom_call" | custom-call | tf_op jit(solution)/shard_map/pack/pallas_call | solution.py:234
  1.7 3.6 %collective-permute-start.8 = (bf16[40,768]{1,0:T(8,128)(2,1)}, bf16[40,768]{1,0:T(8,128)(2,1)S(1)}, u32[]{:S(2)}, u32[]{:S(2)}) collective-permute-start(bf16[40,768]{1,0:T(8,128)(2,1)} %get-tuple-element.11), channel_id=1, source_target_pairs={{0,64},{8,72},{16,80},{24,88},{32,96},{40,104},{48,112},{56,120},{... | collective-permute-start | bytes 184328 | tf_op jit(solution)/shard_map/ppermute | solution.py:249
  5.2 0.9 collective-permute-start.7
  6.1 0.6 collective-permute-start.6
  6.7 0.4 collective-permute-done.8
  7.1 2.1 %collective-permute-done.7 = bf16[40,768]{1,0:T(8,128)(2,1)S(1)} collective-permute-done((bf16[40,768]{1,0:T(8,128)(2,1)}, bf16[40,768]{1,0:T(8,128)(2,1)S(1)}, u32[]{:S(2)}, u32[]{:S(2)}) %collective-permute-start.7) | collective-permute-done | bytes 61472 | tf_op jit(solution)/shard_map/ppermute | solution.py:249
  9.2 1.4 %collective-permute-done.6 = bf16[40,768]{1,0:T(8,128)(2,1)S(1)} collective-permute-done((bf16[40,768]{1,0:T(8,128)(2,1)}, bf16[40,768]{1,0:T(8,128)(2,1)S(1)}, u32[]{:S(2)}, u32[]{:S(2)}) %collective-permute-start.6) | collective-permute-done | bytes 61472 | tf_op jit(solution)/shard_map/ppermute | solution.py:249
  10.6 0.9 pad_maximum_fusion.1.refs_4_
  11.5 3.7 %collective-permute-start.11 = (bf16[4,40,768]{2,1,0:T(8,128)(2,1)S(1)}, bf16[4,40,768]{2,1,0:T(8,128)(2,1)S(1)}, u32[]{:S(2)}, u32[]{:S(2)}) collective-permute-start(bf16[4,40,768]{2,1,0:T(8,128)(2,1)S(1)} %pad_maximum_fusion.1.refs_4_), channel_id=1, source_target_pairs={{0,16},{8,24},{16,0},{24,8},{32,48},{40,56},{48,32},{56,40},{64,80... | collective-permute-start | bytes 737288 | tf_op jit(solution)/shard_map/ppermute | solution.py:254
  15.1 0.1 collective-permute-start.2
  15.2 3.0 %collective-permute-start.1 = (bf16[40,768]{1,0:T(8,128)(2,1)}, bf16[40,768]{1,0:T(8,128)(2,1)S(1)}, u32[]{:S(2)}, u32[]{:S(2)}) collective-permute-start(bf16[40,768]{1,0:T(8,128)(2,1)} %get-tuple-element.10), channel_id=1, source_target_pairs={{0,24},{8,0},{16,8},{24,16},{32,56},{40,32},{48,40},{56,48},{64,88... | collective-permute-start | bytes 184328 | tf_op jit(solution)/shard_map/ppermute | solution.py:248
  18.3 0.0 collective-permute-start
  18.3 2.7 %collective-permute-start.10 = (bf16[4,40,768]{2,1,0:T(8,128)(2,1)S(1)}, bf16[4,40,768]{2,1,0:T(8,128)(2,1)S(1)}, u32[]{:S(2)}, u32[]{:S(2)}) collective-permute-start(bf16[4,40,768]{2,1,0:T(8,128)(2,1)S(1)} %pad_maximum_fusion.1.refs_4_), channel_id=1, source_target_pairs={{0,24},{8,0},{16,8},{24,16},{32,56},{40,32},{48,40},{56,48},{64,88... | collective-permute-start | bytes 737288 | tf_op jit(solution)/shard_map/ppermute | solution.py:254
  20.9 0.0 collective-permute-done.2
  20.9 0.7 collective-permute-start.9
  21.6 0.5 collective-permute-done.1
  22.1 1.9 %collective-permute-done = bf16[40,768]{1,0:T(8,128)(2,1)S(1)} collective-permute-done((bf16[40,768]{1,0:T(8,128)(2,1)}, bf16[40,768]{1,0:T(8,128)(2,1)S(1)}, u32[]{:S(2)}, u32[]{:S(2)}) %collective-permute-start) | collective-permute-done | bytes 61472 | tf_op jit(solution)/shard_map/ppermute | solution.py:248
  24.0 0.9 pad_maximum_fusion.refs_0_
  24.8 0.9 collective-permute-start.5
  25.8 1.6 %collective-permute-start.4 = (bf16[4,40,768]{2,1,0:T(8,128)(2,1)S(1)}, bf16[4,40,768]{2,1,0:T(8,128)(2,1)S(1)}, u32[]{:S(2)}, u32[]{:S(2)}) collective-permute-start(bf16[4,40,768]{2,1,0:T(8,128)(2,1)S(1)} %pad_maximum_fusion.refs_0_), channel_id=1, source_target_pairs={{0,96},{8,104},{16,112},{24,120},{32,0},{40,8},{48,16},{56,24},{64... | collective-permute-start | bytes 737288 | tf_op jit(solution)/shard_map/ppermute | solution.py:253
  27.3 0.0 collective-permute-done.11.refs_7_
  27.3 0.0 collective-permute-start.3
  27.3 0.7 collective-permute-done.10.refs_6_
  28.1 0.0 collective-permute-done.9.refs_5_
  28.1 3.5 %collective-permute-done.5.refs_3_ = bf16[4,40,768]{2,1,0:T(8,128)(2,1)S(1)} collective-permute-done((bf16[4,40,768]{2,1,0:T(8,128)(2,1)S(1)}, bf16[4,40,768]{2,1,0:T(8,128)(2,1)S(1)}, u32[]{:S(2)}, u32[]{:S(2)}) %collective-permute-start.5) | collective-permute-done | bytes 245792 | tf_op jit(solution)/shard_map/ppermute | solution.py:253
  31.5 2.3 %collective-permute-done.4.refs_2_ = bf16[4,40,768]{2,1,0:T(8,128)(2,1)S(1)} collective-permute-done((bf16[4,40,768]{2,1,0:T(8,128)(2,1)S(1)}, bf16[4,40,768]{2,1,0:T(8,128)(2,1)S(1)}, u32[]{:S(2)}, u32[]{:S(2)}) %collective-permute-start.4) | collective-permute-done | bytes 245792 | tf_op jit(solution)/shard_map/ppermute | solution.py:253
  33.8 1.3 %collective-permute-done.3.refs_1_ = bf16[4,40,768]{2,1,0:T(8,128)(2,1)S(1)} collective-permute-done((bf16[4,40,768]{2,1,0:T(8,128)(2,1)S(1)}, bf16[4,40,768]{2,1,0:T(8,128)(2,1)S(1)}, u32[]{:S(2)}, u32[]{:S(2)}) %collective-permute-start.3) | collective-permute-done | bytes 245792 | tf_op jit(solution)/shard_map/ppermute | solution.py:253
  35.1 0.0 copy-start.1
  35.1 2.0 %copy-done.1 = bf16[3,4,160,896]{3,2,1,0:T(8,128)(2,1)S(1)} copy-done((bf16[3,4,160,896]{3,2,1,0:T(8,128)(2,1)S(1)}, bf16[3,4,160,896]{3,2,1,0:T(8,128)(2,1)}, u32[]{:S(2)}) %copy-start.1) | copy-done | bytes 3440664
  37.1 0.0 copy-start.3
  37.1 0.7 copy-done.3
  37.7 0.0 copy-start.5
  37.7 0.7 copy-done.5
  38.4 15.0 %legendre.1 = (f32[8,80,640]{2,1,0:T(8,128)S(1)}, bf16[8,80,128]{2,1,0:T(8,128)(2,1)S(1)}, bf16[8,80,128]{2,1,0:T(8,128)(2,1)S(1)}) custom-call(s32[640]{0:T(1024)S(1)} %copy-done.3, s32[16]{0:T(128)S(1)} %copy-done.5, bf16[4,40,768]{2,1,0:T(8,128)(2,1)S(1)} %pad_maximum_fusion.refs_0_, bf16[4,40,768]{2,1,0:T(8,128)(2,1)S(1)} %collective-permute-done.3.refs_1_, ...), custom_call_target="tpu_custom_call" | custom-call | flops 800000000 | bytes 14000000 | tf_op jit(solution)/shard_map/legendre/pallas_call | solution.py:257
  53.4 0.0 copy-start.2
  53.5 1.2 %copy-done.2 = f32[8,80,640]{2,1,0:T(8,128)} copy-done((f32[8,80,640]{2,1,0:T(8,128)}, f32[8,80,640]{2,1,0:T(8,128)S(1)}, u32[]{:S(2)}) %copy-start.2) | copy-done | bytes 1638424
  54.6 0.0 copy-start.4
  54.6 4.7 %collective-permute-start.12 = (bf16[8,80,128]{2,1,0:T(8,128)(2,1)S(1)}, bf16[8,80,128]{2,1,0:T(8,128)(2,1)S(1)}, u32[]{:S(2)}, u32[]{:S(2)}) collective-permute-start(bf16[8,80,128]{2,1,0:T(8,128)(2,1)S(1)} %get-tuple-element.13), channel_id=1, source_target_pairs={{0,120},{8,0},{16,8},{24,16},{32,24},{40,32},{48,40},{56,48},{64,5... | collective-permute-start | bytes 491528 | tf_op jit(solution)/shard_map/ppermute | solution.py:279
  59.3 0.0 collective-permute-start.13
  59.3 2.3 %collective-permute-done.12.above_ref = bf16[8,80,128]{2,1,0:T(8,128)(2,1)S(1)} collective-permute-done((bf16[8,80,128]{2,1,0:T(8,128)(2,1)S(1)}, bf16[8,80,128]{2,1,0:T(8,128)(2,1)S(1)}, u32[]{:S(2)}, u32[]{:S(2)}) %collective-permute-start.12) | collective-permute-done | bytes 163872 | tf_op jit(solution)/shard_map/ppermute | solution.py:279
  61.6 0.0 copy-start.6
  61.6 5.2 %collective-permute-done.13.below_ref = bf16[8,80,128]{2,1,0:T(8,128)(2,1)S(1)} collective-permute-done((bf16[8,80,128]{2,1,0:T(8,128)(2,1)S(1)}, bf16[8,80,128]{2,1,0:T(8,128)(2,1)S(1)}, u32[]{:S(2)}, u32[]{:S(2)}) %collective-permute-start.13) | collective-permute-done | bytes 163872 | tf_op jit(solution)/shard_map/ppermute | solution.py:280
  66.8 0.0 copy-start.7
  66.8 0.0 copy-done.6
  66.8 0.7 copy-done.7
  67.5 3.2 %join.1 = bf16[8,80,640]{2,1,0:T(8,128)(2,1)} custom-call(f32[8,80,640]{2,1,0:T(8,128)} %copy-done.2, bf16[8,80,128]{2,1,0:T(8,128)(2,1)} %copy-done.6, bf16[8,80,128]{2,1,0:T(8,128)(2,1)} %copy-done.7, bf16[2,128,640]{2,1,0:T(8,128)(2,1)} %constant.7.clone.place_ref), custom_call_target="tpu_custom_call" | custom-call | tf_op jit(solution)/shard_map/join/pallas_call | solution.py:281
  70.6 8.2 %all-to-all-start = ((bf16[8,80,640]{2,1,0:T(8,128)(2,1)}), bf16[8,80,640]{2,1,0:T(8,128)(2,1)S(1)}, u32[]{:S(2)}, u32[]{:S(2)}) async-start(bf16[8,80,640]{2,1,0:T(8,128)(2,1)} %join.1), calls=%async_computation | async-start | bytes 1638400 | tf_op jit(solution)/shard_map/all_to_all | solution.py:289
  78.8 0.0 copy-done.4
  78.8 12.6 %all-to-all-done = bf16[8,80,640]{2,1,0:T(8,128)(2,1)S(1)} async-done(((bf16[8,80,640]{2,1,0:T(8,128)(2,1)}), bf16[8,80,640]{2,1,0:T(8,128)(2,1)S(1)}, u32[]{:S(2)}, u32[]{:S(2)}) %all-to-all-start) | async-done | bytes 819232 | tf_op jit(solution)/shard_map/all_to_all | solution.py:289
  91.4 0.0 copy-start
  91.4 4.7 %copy-done = bf16[1280,5120]{1,0:T(8,128)(2,1)S(1)} copy-done((bf16[1280,5120]{1,0:T(8,128)(2,1)S(1)}, bf16[1280,5120]{1,0:T(8,128)(2,1)}, u32[]{:S(2)}) %copy-start) | copy-done | bytes 13107224
  96.2 8.7 %synthesis.1 = bf16[2,160,5120]{2,1,0:T(8,128)(2,1)} custom-call(s32[1,640]{1,0:T(1,128)S(1)} %reshape.6.order_ref, bf16[640,640]{1,0:T(8,128)(2,1)S(1)} %bitcast.9, bf16[1280,5120]{1,0:T(8,128)(2,1)S(1)} %copy-done), custom_call_target="tpu_custom_call" | custom-call | flops 4400000000 | bytes 18000000 | tf_op jit(solution)/shard_map/synthesis/pallas_call | solution.py:290
  (1 shorter events, 0.0 us)
Async XLA Ops:
  1.7 5.4 %collective-permute-start.8 = (bf16[40,768]{1,0:T(8,128)(2,1)}, bf16[40,768]{1,0:T(8,128)(2,1)S(1)}, u32[]{:S(2)}, u32[]{:S(2)}) collective-permute-start(bf16[40,768]{1,0:T(8,128)(2,1)} %get-tuple-element.11), channel_id=1, source_target_pairs={{0,64},{8,72},{16,80},{24,88},{32,96},{40,104},{48,112},{56,120},{... | collective-permute-start | bytes 184328 | tf_op jit(solution)/shard_map/ppermute | solution.py:249
  5.2 3.9 %collective-permute-start.7 = (bf16[40,768]{1,0:T(8,128)(2,1)}, bf16[40,768]{1,0:T(8,128)(2,1)S(1)}, u32[]{:S(2)}, u32[]{:S(2)}) collective-permute-start(bf16[40,768]{1,0:T(8,128)(2,1)} %get-tuple-element.11), channel_id=1, source_target_pairs={{0,96},{8,104},{16,112},{24,120},{32,0},{40,8},{48,16},{56,24},{64... | collective-permute-start | bytes 184328 | tf_op jit(solution)/shard_map/ppermute | solution.py:249
  6.1 4.5 %collective-permute-start.6 = (bf16[40,768]{1,0:T(8,128)(2,1)}, bf16[40,768]{1,0:T(8,128)(2,1)S(1)}, u32[]{:S(2)}, u32[]{:S(2)}) collective-permute-start(bf16[40,768]{1,0:T(8,128)(2,1)} %get-tuple-element.11), channel_id=1, source_target_pairs={{0,32},{8,40},{16,48},{24,56},{32,64},{40,72},{48,80},{56,88},{64,... | collective-permute-start | bytes 184328 | tf_op jit(solution)/shard_map/ppermute | solution.py:249
  11.5 15.9 %collective-permute-start.11 = (bf16[4,40,768]{2,1,0:T(8,128)(2,1)S(1)}, bf16[4,40,768]{2,1,0:T(8,128)(2,1)S(1)}, u32[]{:S(2)}, u32[]{:S(2)}) collective-permute-start(bf16[4,40,768]{2,1,0:T(8,128)(2,1)S(1)} %pad_maximum_fusion.1.refs_4_), channel_id=1, source_target_pairs={{0,16},{8,24},{16,0},{24,8},{32,48},{40,56},{48,32},{56,40},{64,80... | collective-permute-start | bytes 737288 | tf_op jit(solution)/shard_map/ppermute | solution.py:254
  15.1 5.8 %collective-permute-start.2 = (bf16[40,768]{1,0:T(8,128)(2,1)}, bf16[40,768]{1,0:T(8,128)(2,1)S(1)}, u32[]{:S(2)}, u32[]{:S(2)}) collective-permute-start(bf16[40,768]{1,0:T(8,128)(2,1)} %get-tuple-element.10), channel_id=1, source_target_pairs={{0,16},{8,24},{16,0},{24,8},{32,48},{40,56},{48,32},{56,40},{64,80... | collective-permute-start | bytes 184328 | tf_op jit(solution)/shard_map/ppermute | solution.py:248
  15.2 6.9 %collective-permute-start.1 = (bf16[40,768]{1,0:T(8,128)(2,1)}, bf16[40,768]{1,0:T(8,128)(2,1)S(1)}, u32[]{:S(2)}, u32[]{:S(2)}) collective-permute-start(bf16[40,768]{1,0:T(8,128)(2,1)} %get-tuple-element.10), channel_id=1, source_target_pairs={{0,24},{8,0},{16,8},{24,16},{32,56},{40,32},{48,40},{56,48},{64,88... | collective-permute-start | bytes 184328 | tf_op jit(solution)/shard_map/ppermute | solution.py:248
  18.3 5.7 %collective-permute-start = (bf16[40,768]{1,0:T(8,128)(2,1)}, bf16[40,768]{1,0:T(8,128)(2,1)S(1)}, u32[]{:S(2)}, u32[]{:S(2)}) collective-permute-start(bf16[40,768]{1,0:T(8,128)(2,1)} %get-tuple-element.10), channel_id=1, source_target_pairs={{0,8},{8,16},{16,24},{24,0},{32,40},{40,48},{48,56},{56,32},{64,72... | collective-permute-start | bytes 184328 | tf_op jit(solution)/shard_map/ppermute | solution.py:248
  18.3 9.8 %collective-permute-start.10 = (bf16[4,40,768]{2,1,0:T(8,128)(2,1)S(1)}, bf16[4,40,768]{2,1,0:T(8,128)(2,1)S(1)}, u32[]{:S(2)}, u32[]{:S(2)}) collective-permute-start(bf16[4,40,768]{2,1,0:T(8,128)(2,1)S(1)} %pad_maximum_fusion.1.refs_4_), channel_id=1, source_target_pairs={{0,24},{8,0},{16,8},{24,16},{32,56},{40,32},{48,40},{56,48},{64,88... | collective-permute-start | bytes 737288 | tf_op jit(solution)/shard_map/ppermute | solution.py:254
  20.9 7.1 %collective-permute-start.9 = (bf16[4,40,768]{2,1,0:T(8,128)(2,1)S(1)}, bf16[4,40,768]{2,1,0:T(8,128)(2,1)S(1)}, u32[]{:S(2)}, u32[]{:S(2)}) collective-permute-start(bf16[4,40,768]{2,1,0:T(8,128)(2,1)S(1)} %pad_maximum_fusion.1.refs_4_), channel_id=1, source_target_pairs={{0,8},{8,16},{16,24},{24,0},{32,40},{40,48},{48,56},{56,32},{64,72... | collective-permute-start | bytes 737288 | tf_op jit(solution)/shard_map/ppermute | solution.py:254
  24.8 6.7 %collective-permute-start.5 = (bf16[4,40,768]{2,1,0:T(8,128)(2,1)S(1)}, bf16[4,40,768]{2,1,0:T(8,128)(2,1)S(1)}, u32[]{:S(2)}, u32[]{:S(2)}) collective-permute-start(bf16[4,40,768]{2,1,0:T(8,128)(2,1)S(1)} %pad_maximum_fusion.refs_0_), channel_id=1, source_target_pairs={{0,64},{8,72},{16,80},{24,88},{32,96},{40,104},{48,112},{56,120},{... | collective-permute-start | bytes 737288 | tf_op jit(solution)/shard_map/ppermute | solution.py:253
  25.8 8.0 %collective-permute-start.4 = (bf16[4,40,768]{2,1,0:T(8,128)(2,1)S(1)}, bf16[4,40,768]{2,1,0:T(8,128)(2,1)S(1)}, u32[]{:S(2)}, u32[]{:S(2)}) collective-permute-start(bf16[4,40,768]{2,1,0:T(8,128)(2,1)S(1)} %pad_maximum_fusion.refs_0_), channel_id=1, source_target_pairs={{0,96},{8,104},{16,112},{24,120},{32,0},{40,8},{48,16},{56,24},{64... | collective-permute-start | bytes 737288 | tf_op jit(solution)/shard_map/ppermute | solution.py:253
  27.3 7.7 %collective-permute-start.3 = (bf16[4,40,768]{2,1,0:T(8,128)(2,1)S(1)}, bf16[4,40,768]{2,1,0:T(8,128)(2,1)S(1)}, u32[]{:S(2)}, u32[]{:S(2)}) collective-permute-start(bf16[4,40,768]{2,1,0:T(8,128)(2,1)S(1)} %pad_maximum_fusion.refs_0_), channel_id=1, source_target_pairs={{0,32},{8,40},{16,48},{24,56},{32,64},{40,72},{48,80},{56,88},{64,... | collective-permute-start | bytes 737288 | tf_op jit(solution)/shard_map/ppermute | solution.py:253
  35.1 2.0 %copy-start.1 = (bf16[3,4,160,896]{3,2,1,0:T(8,128)(2,1)S(1)}, bf16[3,4,160,896]{3,2,1,0:T(8,128)(2,1)}, u32[]{:S(2)}) copy-start(bf16[3,4,160,896]{3,2,1,0:T(8,128)(2,1)} %constant.6.clone.refs_9_) | copy-start | bytes 10321924
  37.1 0.7 copy-start.3
  37.7 0.7 copy-start.5
  53.4 1.2 %copy-start.2 = (f32[8,80,640]{2,1,0:T(8,128)}, f32[8,80,640]{2,1,0:T(8,128)S(1)}, u32[]{:S(2)}) copy-start(f32[8,80,640]{2,1,0:T(8,128)S(1)} %get-tuple-element.12.own_ref) | copy-start | bytes 4915204
  54.6 24.2 %copy-start.4 = (s32[640]{0:T(1024)S(1)}, s32[640]{0:T(1024)}, u32[]{:S(2)}) copy-start(s32[640]{0:T(1024)} %order_ref.3) | copy-start | bytes 7684
  54.6 7.0 %collective-permute-start.12 = (bf16[8,80,128]{2,1,0:T(8,128)(2,1)S(1)}, bf16[8,80,128]{2,1,0:T(8,128)(2,1)S(1)}, u32[]{:S(2)}, u32[]{:S(2)}) collective-permute-start(bf16[8,80,128]{2,1,0:T(8,128)(2,1)S(1)} %get-tuple-element.13), channel_id=1, source_target_pairs={{0,120},{8,0},{16,8},{24,16},{32,24},{40,32},{48,40},{56,48},{64,5... | collective-permute-start | bytes 491528 | tf_op jit(solution)/shard_map/ppermute | solution.py:279
  59.3 7.5 %collective-permute-start.13 = (bf16[8,80,128]{2,1,0:T(8,128)(2,1)S(1)}, bf16[8,80,128]{2,1,0:T(8,128)(2,1)S(1)}, u32[]{:S(2)}, u32[]{:S(2)}) collective-permute-start(bf16[8,80,128]{2,1,0:T(8,128)(2,1)S(1)} %get-tuple-element.14), channel_id=1, source_target_pairs={{0,8},{8,16},{16,24},{24,32},{32,40},{40,48},{48,56},{56,64},{64,7... | collective-permute-start | bytes 491528 | tf_op jit(solution)/shard_map/ppermute | solution.py:280
  61.6 5.2 %copy-start.6 = (bf16[8,80,128]{2,1,0:T(8,128)(2,1)}, bf16[8,80,128]{2,1,0:T(8,128)(2,1)S(1)}, u32[]{:S(2)}) copy-start(bf16[8,80,128]{2,1,0:T(8,128)(2,1)S(1)} %collective-permute-done.12.above_ref) | copy-start | bytes 491524
  66.8 0.7 copy-start.7
  70.6 20.8 %all-to-all-start = ((bf16[8,80,640]{2,1,0:T(8,128)(2,1)}), bf16[8,80,640]{2,1,0:T(8,128)(2,1)S(1)}, u32[]{:S(2)}, u32[]{:S(2)}) async-start(bf16[8,80,640]{2,1,0:T(8,128)(2,1)} %join.1), calls=%async_computation | async-start | bytes 1638400 | tf_op jit(solution)/shard_map/all_to_all | solution.py:289
  91.4 4.7 %copy-start = (bf16[1280,5120]{1,0:T(8,128)(2,1)S(1)}, bf16[1280,5120]{1,0:T(8,128)(2,1)}, u32[]{:S(2)}) copy-start(bf16[1280,5120]{1,0:T(8,128)(2,1)} %constant.8.clone.table_ref) | copy-start | bytes 39321604

commit v2 on v1

v2 whole, which is shorter than its diff:
```python
import math

import jax
import jax.numpy as jnp
import ml_dtypes
import numpy as np
from jax import lax
from jax.experimental import pallas as pl
from jax.experimental.pallas import tpu as pltpu
from jax.sharding import PartitionSpec as P

NLAT = 2560
NLON = 5120
NWAVE = 640
WL = 5
BANDS = 16
OWNERS = 8
BAND = NLAT // BANDS
SLOTS = NWAVE // OWNERS
PAIRS = SLOTS // 2
FIELDS = 16
BLOCKS = 6
LANE = 128
HALVES = 2
PART_PAIRS = PAIRS // HALVES
PART_SLOTS = SLOTS // HALVES
RANK = 16
WIDTH = 4 * LANE + 4 * (BAND - LANE + 2 * RANK)
TILE = 512
GROUP = 4
SMALL_BYTES = 48 * 2**20
LARGE_BYTES = 52 * 2**20

LIFT_ALPHA = -1.586134342059924
LIFT_BETA = -0.052980118572961
LIFT_GAMMA = 0.882911075530934
LIFT_DELTA = 0.443506852043971
LIFT_KAPPA = 1.149604398860241


def analyze(values, levels, mode_name):
    if levels == 0:
        return values
    widths = [(4, 4)] + [(0, 0)] * (values.ndim - 1)
    extended = np.pad(values, widths, mode=mode_name)
    even, odd = extended[0::2], extended[1::2]
    first_d = odd[:-1] + LIFT_ALPHA * (even[:-1] + even[1:])
    first_s = even[1:-1] + LIFT_BETA * (first_d[:-1] + first_d[1:])
    second_d = first_d[1:-1] + LIFT_GAMMA * (first_s[:-1] + first_s[1:])
    second_s = first_s[1:-1] + LIFT_DELTA * (second_d[:-1] + second_d[1:])
    result = np.empty_like(values)
    result[0::2] = analyze(second_s * LIFT_KAPPA, levels - 1, mode_name)
    result[1::2] = second_d[1:] / LIFT_KAPPA
    return result


def longitude_matrix():
    waves = np.arange(NWAVE)
    phase = waves[:, None] * np.arange(NLON)[None, :] % NLON
    angle = phase * (2.0 * math.pi / NLON)
    weight = np.where(waves == 0, 1.0, 2.0)[:, None] / math.sqrt(2.0 * NWAVE)
    table = np.concatenate([weight * np.cos(angle), -weight * np.sin(angle)], axis=0)
    table = table.astype(np.float32).astype(ml_dtypes.bfloat16).astype(np.float64)
    return analyze(table.T, WL, "wrap").T.astype(np.float32).astype(ml_dtypes.bfloat16)


def latitude_matrices():
    whole = analyze(np.eye(NLAT), WL, "reflect")

    def block(row_band, column_band):
        return whole[row_band * BAND : (row_band + 1) * BAND, column_band * BAND : (column_band + 1) * BAND]

    assert all(np.abs(block(band - 1, band) - block(6, 7)).max() < 1e-12 for band in range(1, BANDS))
    assert all(np.abs(block(band, band - 1) - block(8, 7)).max() < 1e-12 for band in range(1, BANDS))
    inner = whole[:, 7 * BAND : 8 * BAND]
    assert np.abs(inner[: 6 * BAND]).max() == 0 and np.abs(inner[9 * BAND :]).max() == 0
    assert all(np.abs(block(band, band) - block(7, 7)).max() < 1e-12 for band in range(1, BANDS - 1))
    expand = np.zeros((BAND, 2 * RANK))
    project = np.zeros((BAND, 2 * RANK))
    for side, part in enumerate((block(6, 7), block(8, 7))):
        left, sizes, right = np.linalg.svd(part)
        rank = int((sizes > 1e-12).sum())
        assert rank <= RANK
        expand[:, side * RANK : side * RANK + rank] = left[:, :rank] * sizes[:rank]
        project[:, side * RANK : side * RANK + rank] = right[:rank].T
    out = np.zeros((3, BAND, 2 * LANE))
    for variant, band in enumerate((0, 7, BANDS - 1)):
        own = block(band, band).T
        tail = np.concatenate([own[:, LANE:], project], axis=1)
        out[variant] = np.concatenate([own[:, :LANE], tail, tail], axis=1)
    return (
        out.astype(np.float32).astype(ml_dtypes.bfloat16),
        expand.astype(np.float32).astype(ml_dtypes.bfloat16),
    )


def pack_kernel(order_ref, spectra_ref, *refs):
    outs, (wide, low, high, packed) = refs[:HALVES], refs[HALVES:]
    first = lax.axis_index("wave") * SLOTS
    for pair in range(PAIRS):
        low[pl.ds(pair, 1), :] = jnp.full((1, LANE), order_ref[first + 2 * pair], jnp.int32)
        high[pl.ds(pair, 1), :] = jnp.full((1, LANE), order_ref[first + 2 * pair + 1], jnp.int32)
    waves_a, waves_b = low[...], high[...]
    lane = lax.broadcasted_iota(jnp.int32, (PAIRS, LANE), 1)
    for part in range(2):
        for block in range(5):
            wide[block] = spectra_ref[0, part, :, block * LANE : (block + 1) * LANE].astype(jnp.float32)
        for block in range(BLOCKS):
            taken = jnp.zeros((PAIRS, LANE), jnp.float32)
            if block <= 4:
                values = wide[4 - block, pl.ds(1, PAIRS, stride=2), :]
                taken = jnp.where(lane + (4 - block) * LANE >= waves_b, values, taken)
            if block >= 1:
                values = wide[block - 1, pl.ds(0, PAIRS, stride=2), :]
                values = jnp.where(lane + (block - 1) * LANE >= waves_a, values, jnp.zeros_like(values))
                taken = jnp.where(waves_a < block * LANE, values, taken)
            for half in range(HALVES):
                packed[half, pl.ds(part * PART_PAIRS, PART_PAIRS), block * LANE : (block + 1) * LANE] = taken[
                    half * PART_PAIRS : (half + 1) * PART_PAIRS
                ]
    for half in range(HALVES):
        outs[half][...] = packed[half].astype(jnp.bfloat16)


def legendre_kernel(half, order_ref, writer_ref, *refs):
    parts = refs[:4]
    legendre_ref, matrix_ref, out_ref = refs[4:7]
    held, staged, spread, rows, results, matrix, sems, staged_sems, matrix_sem = refs[7:]
    base = half * PART_PAIRS
    first = lax.axis_index("wave") * SLOTS + 2 * base
    band = lax.axis_index("lat")
    variant = jnp.where(band == 0, 0, jnp.where(band == BANDS - 1, 2, 1))
    copies = [pltpu.make_async_copy(parts[i], staged.at[i], staged_sems.at[i]) for i in range(4)]
    for copy in copies:
        copy.start()

    def fetch(pair, carry):
        wave = order_ref[first + 2 * pair]
        for block in range(BLOCKS):
            from_a = wave < block * LANE
            slot = 2 * (base + pair) + jnp.where(from_a, 0, 1)
            source = jnp.where(from_a, block - 1, 4 - block)
            pltpu.make_async_copy(
                legendre_ref.at[slot, :, pl.ds(pl.multiple_of(source * LANE, LANE), LANE)],
                held.at[pair, :, pl.ds(block * LANE, LANE)],
                sems.at[pair],
            ).start()
        return carry

    lax.fori_loop(0, PART_PAIRS, fetch, 0)
    matrix_copy = pltpu.make_async_copy(matrix_ref.at[variant], matrix, matrix_sem)
    matrix_copy.start()

    band_x, band_z = band // 4, lax.rem(band, 4)
    steps = (0, 3, 1, 2)
    for outer in range(4):
        copies[outer].wait()
        for inner in range(4):
            along_x, along_z = (outer, inner) if half == 0 else (inner, outer)
            field = 4 * lax.rem(band_x + steps[along_x], 4) + lax.rem(band_z + steps[along_z], 4)
            start = pl.multiple_of(field * 2 * PART_PAIRS, 8)
            for block in range(BLOCKS):
                values = staged[outer, inner, :, block * LANE : (block + 1) * LANE]
                spread[block, pl.ds(start, 2 * PART_PAIRS), :] = values.astype(jnp.float32)

    def contract(group, carry):
        for member in range(GROUP):
            pair = group * GROUP + member
            pltpu.make_async_copy(held.at[pair], held.at[pair], sems.at[pair]).wait()
            wave = order_ref[first + 2 * pair]
            lower, upper = [], []
            for block in range(BLOCKS):
                values = spread[block, pl.ds(pair, 2 * FIELDS, stride=PART_PAIRS), :].astype(jnp.bfloat16)
                from_a = wave < block * LANE
                lower.append(jnp.where(from_a, values, jnp.zeros_like(values)))
                upper.append(jnp.where(from_a, jnp.zeros_like(values), values))
            left = jnp.concatenate(
                [jnp.concatenate(lower, axis=1), jnp.concatenate(upper, axis=1)], axis=0
            )
            sums = lax.dot_general(
                left, held[pair], (((1,), (1,)), ((), ())), preferred_element_type=jnp.float32
            )
            for which in range(2):
                piece = sums[which * 2 * FIELDS : (which + 1) * 2 * FIELDS]
                where = pl.ds(2 * pair + which, 2 * FIELDS, stride=PART_SLOTS)
                rows[0, where, :] = piece[:, :LANE]
                rows[1, where, : BAND - LANE] = piece[:, LANE:]
        return carry

    lax.fori_loop(0, PART_PAIRS // GROUP, contract, 0)
    matrix_copy.wait()

    chunk = 2 * FIELDS * PART_SLOTS // 4
    for index in range(4):
        picked = slice(index * chunk, (index + 1) * chunk)
        left = jnp.concatenate([rows[0, picked, :], rows[1, picked, : BAND - LANE]], axis=1).astype(jnp.bfloat16)
        sums = jnp.dot(left, matrix[...], preferred_element_type=jnp.float32)
        results[0, picked, :] = sums[:, :LANE]
        results[1, picked, :] = sums[:, LANE:]

    lane = lax.broadcasted_iota(jnp.int32, (PART_SLOTS, LANE), 1)
    for owner in range(OWNERS):
        for member in range(2):
            field = writer_ref[2 * owner + member]
            tails = []
            for part in range(2):
                start = pl.multiple_of((2 * field + part) * PART_SLOTS, 8)
                place = (2 * member + part) * LANE
                out_ref[owner, :, place : place + LANE] = results[0, pl.ds(start, PART_SLOTS), :].astype(jnp.bfloat16)
                tails.append(results[1, pl.ds(start, PART_SLOTS), :])
            place = (4 + member) * LANE
            out_ref[owner, :, place : place + LANE] = jnp.where(lane < LANE // 2, *tails).astype(jnp.bfloat16)


def edge_kernel(order_ref, *refs):
    waves = refs[:HALVES]
    chosen_ref, rest_ref, above_ref, below_ref = refs[HALVES:]
    row = lax.broadcasted_iota(jnp.int32, (NWAVE, NWAVE), 0)
    chosen_ref[...] = jnp.where(row == order_ref[...], 1.0, 0.0).astype(jnp.bfloat16)
    count = NWAVE // HALVES
    ordered = sum(
        jnp.dot(
            chosen_ref[:, half * count : (half + 1) * count],
            waves[half][...],
            preferred_element_type=jnp.float32,
        )
        for half in range(HALVES)
    )
    turned = ordered.T.astype(jnp.bfloat16)
    rest = BAND - LANE
    for part in range(4):
        start = part * (rest + 2 * RANK)
        rest_ref[part * rest : (part + 1) * rest] = turned[start : start + rest]
        above_ref[part * RANK : (part + 1) * RANK] = turned[start + rest : start + rest + RANK]
        below_ref[part * RANK : (part + 1) * RANK] = turned[start + rest + RANK : start + rest + 2 * RANK]


def order_kernel(chosen_ref, *refs):
    waves, out_ref = refs[:HALVES], refs[HALVES]
    count = NWAVE // HALVES
    ordered = sum(
        jnp.dot(
            chosen_ref[:, half * count : (half + 1) * count],
            waves[half][...],
            preferred_element_type=jnp.float32,
        )
        for half in range(HALVES)
    )
    out_ref[...] = ordered.T.astype(jnp.bfloat16)


def synthesis_kernel(main_ref, rest_ref, above_ref, below_ref, expand_ref, table_ref, out_ref, left):
    @pl.when(pl.program_id(0) == 0)
    def _():
        rest = BAND - LANE
        for field in range(2):
            for part in range(2):
                which = 2 * field + part
                edges = slice(which * RANK, (which + 1) * RANK)
                added = jnp.dot(
                    expand_ref[...],
                    jnp.concatenate([above_ref[edges], below_ref[edges]], axis=0),
                    preferred_element_type=jnp.float32,
                )
                lanes = slice(part * NWAVE, (part + 1) * NWAVE)
                own = main_ref[which * LANE : (which + 1) * LANE].astype(jnp.float32)
                left[field * BAND : field * BAND + LANE, lanes] = (own + added[:LANE]).astype(jnp.bfloat16)
                own = rest_ref[which * rest : (which + 1) * rest].astype(jnp.float32)
                left[field * BAND + LANE : (field + 1) * BAND, lanes] = (own + added[LANE:]).astype(jnp.bfloat16)

    sums = jnp.dot(left[...], table_ref[...], preferred_element_type=jnp.float32)
    out_ref[0] = sums[:BAND].astype(jnp.bfloat16)
    out_ref[1] = sums[BAND:].astype(jnp.bfloat16)


def along_z(step):
    return [(4 * x + z, 4 * x + (z + step) % 4) for x in range(4) for z in range(4)]


def along_x(step):
    return [(4 * x + z, 4 * ((x + step) % 4) + z) for x in range(4) for z in range(4)]


def neighbour(step):
    return [(band, band + step) for band in range(BANDS) if 0 <= band + step < BANDS]


SMEM = pl.BlockSpec(memory_space=pltpu.SMEM)
VMEM = pl.BlockSpec(memory_space=pltpu.VMEM)
ANY = pl.BlockSpec(memory_space=pl.ANY)
SMALL = pltpu.CompilerParams(vmem_limit_bytes=SMALL_BYTES)
LARGE = pltpu.CompilerParams(vmem_limit_bytes=LARGE_BYTES)


def bf16(*shape):
    return jax.ShapeDtypeStruct(shape, jnp.bfloat16)


def make_on_device(table, matrices, expand):
    def on_device(spectra, legendre, wave_order, writer_order):
        halves = pl.pallas_call(
            pack_kernel,
            out_shape=[bf16(2 * PART_PAIRS, BLOCKS * LANE)] * HALVES,
            in_specs=[SMEM, VMEM],
            out_specs=[VMEM] * HALVES,
            scratch_shapes=[
                pltpu.VMEM((5, SLOTS, LANE), jnp.float32),
                pltpu.VMEM((PAIRS, LANE), jnp.int32),
                pltpu.VMEM((PAIRS, LANE), jnp.int32),
                pltpu.VMEM((HALVES, 2 * PART_PAIRS, BLOCKS * LANE), jnp.float32),
            ],
            name="pack",
        )(wave_order, spectra)
        order = wave_order.reshape(OWNERS, HALVES, PART_SLOTS).swapaxes(0, 1).reshape(1, NWAVE)

        axes = ((along_z, along_x), (along_x, along_z))
        gathered = halves
        for stage in range(2):
            arrived = [
                [values] + [lax.ppermute(values, "lat", axes[half][stage](step)) for step in (1, 3, 2)]
                for half, values in enumerate(gathered)
            ]
            gathered = lax.optimization_barrier([jnp.stack(blocks) for blocks in arrived]) if stage == 0 else arrived

        waves = []
        for half in range(HALVES):
            lifted = pl.pallas_call(
                lambda *refs, half=half: legendre_kernel(half, *refs),
                out_shape=bf16(OWNERS, PART_SLOTS, WIDTH),
                in_specs=[SMEM, SMEM] + [ANY] * 6,
                out_specs=VMEM,
                scratch_shapes=[
                    pltpu.VMEM((PART_PAIRS, BAND, BLOCKS * LANE), jnp.bfloat16),
                    pltpu.VMEM((4, 4, 2 * PART_PAIRS, BLOCKS * LANE), jnp.bfloat16),
                    pltpu.VMEM((BLOCKS, 2 * FIELDS * PART_PAIRS, LANE), jnp.float32),
                    pltpu.VMEM((2, 2 * FIELDS * PART_SLOTS, LANE), jnp.float32),
                    pltpu.VMEM((2, 2 * FIELDS * PART_SLOTS, LANE), jnp.float32),
                    pltpu.VMEM((BAND, 2 * LANE), jnp.bfloat16),
                    pltpu.SemaphoreType.DMA((PART_PAIRS,)),
                    pltpu.SemaphoreType.DMA((4,)),
                    pltpu.SemaphoreType.DMA,
                ],
                compiler_params=SMALL,
                cost_estimate=pl.CostEstimate(flops=400_000_000, bytes_accessed=8_000_000, transcendentals=0),
                name=f"legendre{half}",
            )(wave_order, writer_order, *gathered[half], legendre, matrices)
            if half + 1 < HALVES:
                lifted, gathered[half + 1] = lax.optimization_barrier((lifted, gathered[half + 1]))
            received = lax.all_to_all(lifted, "wave", split_axis=0, concat_axis=0, tiled=True)
            waves.append(received.reshape(OWNERS * PART_SLOTS, WIDTH))

        main, rest = 4 * LANE, 4 * (BAND - LANE)
        count = NWAVE // HALVES
        chosen, tail, above, below = pl.pallas_call(
            edge_kernel,
            grid=(1,),
            out_shape=[bf16(NWAVE, NWAVE), bf16(rest, NWAVE), bf16(4 * RANK, NWAVE), bf16(4 * RANK, NWAVE)],
            in_specs=[pl.BlockSpec((1, NWAVE), lambda i: (0, 0))]
            + [pl.BlockSpec((count, WIDTH - main), lambda i: (0, main // (WIDTH - main)))] * HALVES,
            out_specs=[VMEM] * 4,
            compiler_params=SMALL,
            name="edges",
        )(order, *waves)
        above = lax.ppermute(above, "lat", neighbour(-1))
        below = lax.ppermute(below, "lat", neighbour(1))
        ordered = pl.pallas_call(
            order_kernel,
            grid=(1,),
            out_shape=bf16(main, NWAVE),
            in_specs=[pl.BlockSpec((NWAVE, NWAVE), lambda i: (0, 0))]
            + [pl.BlockSpec((count, main), lambda i: (0, 0))] * HALVES,
            out_specs=VMEM,
            compiler_params=SMALL,
            cost_estimate=pl.CostEstimate(flops=800_000_000, bytes_accessed=4_000_000, transcendentals=0),
            name="order",
        )(chosen, *waves)
        return pl.pallas_call(
            synthesis_kernel,
            grid=(NLON // TILE,),
            out_shape=bf16(2, BAND, NLON),
            in_specs=[VMEM] * 5 + [pl.BlockSpec((2 * NWAVE, TILE), lambda j: (0, j))],
            out_specs=pl.BlockSpec((2, BAND, TILE), lambda j: (0, 0, j)),
            scratch_shapes=[pltpu.VMEM((2 * BAND, 2 * NWAVE), jnp.bfloat16)],
            compiler_params=LARGE,
            cost_estimate=pl.CostEstimate(flops=4_400_000_000, bytes_accessed=18_000_000, transcendentals=0),
            name="synthesis",
        )(ordered, tail, above, below, expand, table)

    return on_device


def solution(mesh):
    table = longitude_matrix()
    matrices, expand = latitude_matrices()
    return jax.shard_map(
        make_on_device(jnp.asarray(table), jnp.asarray(matrices), jnp.asarray(expand)),
        mesh=mesh,
        in_specs=(P("lat", None, "wave", None), P("wave", "lat", None), P(), P()),
        out_specs=P("wave", "lat", None),
        check_vma=False,
    )
```

time: 105 us -> 96.7 us (0.921)
  the two profiles are of different devices: /device:TPU:1 before, /device:TPU:2 now
where the time goes in v2:
time: 96.7 us; the launch traced here: 95.8 us
  starting transfers between devices  34.7 us (36%)
  Pallas kernels  34.3 us (35%)
  waiting for transfers between devices  22.5 us (23%)
  local copies, waits for them, and re-layouts  2.49 us (3%)
  other arithmetic  1.72 us (2%)
    pallas_call x2, Pallas kernels, on_device(): pl.pallas_call(lambda *refs, half=half: legendre_kernel(half, *refs), out...  18.8 us
    ppermute x12, starting transfers between devices, on_device(): lax.ppermute(values, 'lat', axes[half][stage](step))  18.7 us
    pallas_call x1, Pallas kernels, on_device(): pl.pallas_call(synthesis_kernel, grid=(NLON // TILE,), out_shape=bf16(2,...  12.1 us
    all_to_all x2, waiting for transfers between devices, on_device(): lax.all_to_all(lifted, 'wave', split_axis=0, concat_axis=0, tiled=True)  10.3 us
    all_to_all x2, starting transfers between devices, on_device(): lax.all_to_all(lifted, 'wave', split_axis=0, concat_axis=0, tiled=True)  8.79 us
    ppermute x12, waiting for transfers between devices, on_device(): lax.ppermute(values, 'lat', axes[half][stage](step))  6.66 us
    ppermute x1, waiting for transfers between devices, on_device(): below = lax.ppermute(below, 'lat', neighbour(1))  5.54 us
    ppermute x1, starting transfers between devices, on_device(): above = lax.ppermute(above, 'lat', neighbour(-1))  5.33 us
  transfers between devices with their start and end apart: 16, of which 9 were waited for; matrix products, arithmetic and copies ran while one was open for 1% of the time, Pallas kernels for 21%

profile of v2, /device:TPU:2, one launch (start us, length us, event | category | flops | bytes accessed | tf_op | source)
XLA Modules:
  0.0 95.8 jit_solution(8465312773729859523)
XLA Ops:
  0.0 0.0 copy-start.1
  0.0 0.0 copy-start.3
  0.0 0.0 copy-start.6
  0.0 1.7 %pack.1 = (bf16[40,768]{1,0:T(8,128)(2,1)}, bf16[40,768]{1,0:T(8,128)(2,1)}) custom-call(s32[640]{0:T(1024)} %refs_0_.3, bf16[1,2,80,640]{3,2,1,0:T(8,128)(2,1)} %spectra_ref.1), custom_call_target="tpu_custom_call" | custom-call | tf_op jit(solution)/shard_map/pack/pallas_call | solution.py:301
  1.8 3.9 %collective-permute-start.2 = (bf16[40,768]{1,0:T(8,128)(2,1)}, bf16[40,768]{1,0:T(8,128)(2,1)S(1)}, u32[]{:S(2)}, u32[]{:S(2)}) collective-permute-start(bf16[40,768]{1,0:T(8,128)(2,1)} %get-tuple-element.18), channel_id=1, source_target_pairs={{0,16},{8,24},{16,0},{24,8},{32,48},{40,56},{48,32},{56,40},{64,80... | collective-permute-start | bytes 184328 | tf_op jit(solution)/shard_map/ppermute | solution.py:320
  5.6 0.7 collective-permute-start.1
  6.3 1.3 %collective-permute-start = (bf16[40,768]{1,0:T(8,128)(2,1)}, bf16[40,768]{1,0:T(8,128)(2,1)S(1)}, u32[]{:S(2)}, u32[]{:S(2)}) collective-permute-start(bf16[40,768]{1,0:T(8,128)(2,1)} %get-tuple-element.18), channel_id=1, source_target_pairs={{0,8},{8,16},{16,24},{24,0},{32,40},{40,48},{48,56},{56,32},{64,72... | collective-permute-start | bytes 184328 | tf_op jit(solution)/shard_map/ppermute | solution.py:320
  7.7 2.1 %collective-permute-start.5 = (bf16[40,768]{1,0:T(8,128)(2,1)}, bf16[40,768]{1,0:T(8,128)(2,1)S(1)}, u32[]{:S(2)}, u32[]{:S(2)}) collective-permute-start(bf16[40,768]{1,0:T(8,128)(2,1)} %get-tuple-element.19), channel_id=1, source_target_pairs={{0,64},{8,72},{16,80},{24,88},{32,96},{40,104},{48,112},{56,120},{... | collective-permute-start | bytes 184328 | tf_op jit(solution)/shard_map/ppermute | solution.py:320
  9.8 1.4 %collective-permute-start.4 = (bf16[40,768]{1,0:T(8,128)(2,1)}, bf16[40,768]{1,0:T(8,128)(2,1)S(1)}, u32[]{:S(2)}, u32[]{:S(2)}) collective-permute-start(bf16[40,768]{1,0:T(8,128)(2,1)} %get-tuple-element.19), channel_id=1, source_target_pairs={{0,96},{8,104},{16,112},{24,120},{32,0},{40,8},{48,16},{56,24},{64... | collective-permute-start | bytes 184328 | tf_op jit(solution)/shard_map/ppermute | solution.py:320
  11.2 0.0 collective-permute-done.2
  11.2 0.6 collective-permute-start.3
  11.8 0.0 collective-permute-done.1
  11.8 0.2 collective-permute-done
  12.0 0.9 pad_maximum_fusion.refs_2_
  12.9 0.7 collective-permute-done.5
  13.6 0.7 collective-permute-done.4
  14.3 1.4 %collective-permute-done.3 = bf16[40,768]{1,0:T(8,128)(2,1)S(1)} collective-permute-done((bf16[40,768]{1,0:T(8,128)(2,1)}, bf16[40,768]{1,0:T(8,128)(2,1)S(1)}, u32[]{:S(2)}, u32[]{:S(2)}) %collective-permute-start.3) | collective-permute-done | bytes 61472 | tf_op jit(solution)/shard_map/ppermute | solution.py:320
  15.7 0.9 pad_maximum_fusion.1.refs_2_
  16.5 1.3 %collective-permute-start.8 = (bf16[4,40,768]{2,1,0:T(8,128)(2,1)S(1)}, bf16[4,40,768]{2,1,0:T(8,128)(2,1)S(1)}, u32[]{:S(2)}, u32[]{:S(2)}) collective-permute-start(bf16[4,40,768]{2,1,0:T(8,128)(2,1)S(1)} %pad_maximum_fusion.refs_2_), channel_id=1, source_target_pairs={{0,64},{8,72},{16,80},{24,88},{32,96},{40,104},{48,112},{56,120},{... | collective-permute-start | bytes 737288 | tf_op jit(solution)/shard_map/ppermute | solution.py:320
  17.8 1.5 %collective-permute-start.7 = (bf16[4,40,768]{2,1,0:T(8,128)(2,1)S(1)}, bf16[4,40,768]{2,1,0:T(8,128)(2,1)S(1)}, u32[]{:S(2)}, u32[]{:S(2)}) collective-permute-start(bf16[4,40,768]{2,1,0:T(8,128)(2,1)S(1)} %pad_maximum_fusion.refs_2_), channel_id=1, source_target_pairs={{0,96},{8,104},{16,112},{24,120},{32,0},{40,8},{48,16},{56,24},{64... | collective-permute-start | bytes 737288 | tf_op jit(solution)/shard_map/ppermute | solution.py:320
  19.3 1.2 %collective-permute-start.6 = (bf16[4,40,768]{2,1,0:T(8,128)(2,1)S(1)}, bf16[4,40,768]{2,1,0:T(8,128)(2,1)S(1)}, u32[]{:S(2)}, u32[]{:S(2)}) collective-permute-start(bf16[4,40,768]{2,1,0:T(8,128)(2,1)S(1)} %pad_maximum_fusion.refs_2_), channel_id=1, source_target_pairs={{0,32},{8,40},{16,48},{24,56},{32,64},{40,72},{48,80},{56,88},{64,... | collective-permute-start | bytes 737288 | tf_op jit(solution)/shard_map/ppermute | solution.py:320
  20.4 1.1 %collective-permute-start.11 = (bf16[4,40,768]{2,1,0:T(8,128)(2,1)S(1)}, bf16[4,40,768]{2,1,0:T(8,128)(2,1)S(1)}, u32[]{:S(2)}, u32[]{:S(2)}) collective-permute-start(bf16[4,40,768]{2,1,0:T(8,128)(2,1)S(1)} %pad_maximum_fusion.1.refs_2_), channel_id=1, source_target_pairs={{0,16},{8,24},{16,0},{24,8},{32,48},{40,56},{48,32},{56,40},{64,80... | collective-permute-start | bytes 737288 | tf_op jit(solution)/shard_map/ppermute | solution.py:320
  21.5 2.6 %collective-permute-start.10 = (bf16[4,40,768]{2,1,0:T(8,128)(2,1)S(1)}, bf16[4,40,768]{2,1,0:T(8,128)(2,1)S(1)}, u32[]{:S(2)}, u32[]{:S(2)}) collective-permute-start(bf16[4,40,768]{2,1,0:T(8,128)(2,1)S(1)} %pad_maximum_fusion.1.refs_2_), channel_id=1, source_target_pairs={{0,24},{8,0},{16,8},{24,16},{32,56},{40,32},{48,40},{56,48},{64,88... | collective-permute-start | bytes 737288 | tf_op jit(solution)/shard_map/ppermute | solution.py:320
  24.1 2.4 %collective-permute-done.8.refs_5_ = bf16[4,40,768]{2,1,0:T(8,128)(2,1)S(1)} collective-permute-done((bf16[4,40,768]{2,1,0:T(8,128)(2,1)S(1)}, bf16[4,40,768]{2,1,0:T(8,128)(2,1)S(1)}, u32[]{:S(2)}, u32[]{:S(2)}) %collective-permute-start.8) | collective-permute-done | bytes 245792 | tf_op jit(solution)/shard_map/ppermute | solution.py:320
  26.5 1.0 %collective-permute-start.9 = (bf16[4,40,768]{2,1,0:T(8,128)(2,1)S(1)}, bf16[4,40,768]{2,1,0:T(8,128)(2,1)S(1)}, u32[]{:S(2)}, u32[]{:S(2)}) collective-permute-start(bf16[4,40,768]{2,1,0:T(8,128)(2,1)S(1)} %pad_maximum_fusion.1.refs_2_), channel_id=1, source_target_pairs={{0,8},{8,16},{16,24},{24,0},{32,40},{40,48},{48,56},{56,32},{64,72... | collective-permute-start | bytes 737288 | tf_op jit(solution)/shard_map/ppermute | solution.py:320
  27.6 1.2 %collective-permute-done.7.refs_4_ = bf16[4,40,768]{2,1,0:T(8,128)(2,1)S(1)} collective-permute-done((bf16[4,40,768]{2,1,0:T(8,128)(2,1)S(1)}, bf16[4,40,768]{2,1,0:T(8,128)(2,1)S(1)}, u32[]{:S(2)}, u32[]{:S(2)}) %collective-permute-start.7) | collective-permute-done | bytes 245792 | tf_op jit(solution)/shard_map/ppermute | solution.py:320
  28.8 0.0 collective-permute-done.6.refs_3_
  28.8 0.0 copy-start
  28.8 0.9 copy-done
  29.7 0.0 copy-start.2
  29.8 0.7 copy-done.2
  30.4 0.0 copy-start.5
  30.4 0.7 copy-done.5
  31.1 9.4 %legendre0.1 = bf16[8,40,768]{2,1,0:T(8,128)(2,1)} custom-call(s32[640]{0:T(1024)S(1)} %copy-done.2, s32[16]{0:T(128)S(1)} %copy-done.5, bf16[4,40,768]{2,1,0:T(8,128)(2,1)S(1)} %pad_maximum_fusion.refs_2_, bf16[4,40,768]{2,1,0:T(8,128)(2,1)S(1)} %collective-permute-done.6.refs_3_, bf16[4,40,768]{2,1,0:T(8,128)(2,1)S(1)} %collective-permute-done.7.refs_4_, ...), custom_call_target="tpu_custom_call" | custom-call | flops 400000000 | bytes 8000000 | tf_op jit(solution)/shard_map/legendre0/pallas_call | solution.py:327
  40.5 0.0 copy-start.4
  40.5 0.0 collective-permute-done.11.refs_5_
  40.5 0.0 collective-permute-done.10.refs_4_
  40.5 0.0 collective-permute-done.9.refs_3_
  40.5 4.5 %all-to-all-start = ((bf16[8,40,768]{2,1,0:T(8,128)(2,1)}), bf16[8,40,768]{2,1,0:T(8,128)(2,1)S(1)}, u32[]{:S(2)}, u32[]{:S(2)}) async-start(bf16[8,40,768]{2,1,0:T(8,128)(2,1)} %legendre0.1), calls=%async_computation | async-start | bytes 983040 | tf_op jit(solution)/shard_map/all_to_all | solution.py:349
  45.0 0.0 copy-done.1
  45.0 0.0 copy-done.3
  45.0 0.0 copy-done.6
  45.0 9.5 %legendre1.1 = bf16[8,40,768]{2,1,0:T(8,128)(2,1)} custom-call(s32[640]{0:T(1024)S(1)} %copy-done.3, s32[16]{0:T(128)S(1)} %copy-done.6, bf16[4,40,768]{2,1,0:T(8,128)(2,1)S(1)} %pad_maximum_fusion.1.refs_2_, bf16[4,40,768]{2,1,0:T(8,128)(2,1)S(1)} %collective-permute-done.9.refs_3_, bf16[4,40,768]{2,1,0:T(8,128)(2,1)S(1)} %collective-permute-done.10.refs_4_, ...), custom_call_target="tpu_custom_call" | custom-call | flops 400000000 | bytes 8000000 | tf_op jit(solution)/shard_map/legendre1/pallas_call | solution.py:327
  54.5 0.5 all-to-all-done
  55.0 4.3 %all-to-all-start.1 = ((bf16[8,40,768]{2,1,0:T(8,128)(2,1)}), bf16[8,40,768]{2,1,0:T(8,128)(2,1)S(1)}, u32[]{:S(2)}, u32[]{:S(2)}) async-start(bf16[8,40,768]{2,1,0:T(8,128)(2,1)} %legendre1.1), calls=%async_computation.1 | async-start | bytes 983040 | tf_op jit(solution)/shard_map/all_to_all | solution.py:349
  59.3 0.1 reshape.12
  59.4 0.1 reshape.13.order_ref
  59.5 9.8 %all-to-all-done.1 = bf16[8,40,768]{2,1,0:T(8,128)(2,1)S(1)} async-done(((bf16[8,40,768]{2,1,0:T(8,128)(2,1)}), bf16[8,40,768]{2,1,0:T(8,128)(2,1)S(1)}, u32[]{:S(2)}, u32[]{:S(2)}) %all-to-all-start.1) | async-done | bytes 491552 | tf_op jit(solution)/shard_map/all_to_all | solution.py:349
  69.3 0.7 edges.1
  70.0 5.3 %collective-permute-start.12 = (bf16[64,640]{1,0:T(8,128)(2,1)S(1)}, bf16[64,640]{1,0:T(8,128)(2,1)S(1)}, u32[]{:S(2)}, u32[]{:S(2)}) collective-permute-start(bf16[64,640]{1,0:T(8,128)(2,1)S(1)} %get-tuple-element.29), channel_id=1, source_target_pairs={{8,0},{16,8},{24,16},{32,24},{40,32},{48,40},{56,48},{64,56},{72,6... | collective-permute-start | bytes 245768 | tf_op jit(solution)/shard_map/ppermute | solution.py:364
  75.3 1.9 %collective-permute-start.13 = (bf16[64,640]{1,0:T(8,128)(2,1)S(1)}, bf16[64,640]{1,0:T(8,128)(2,1)S(1)}, u32[]{:S(2)}, u32[]{:S(2)}) collective-permute-start(bf16[64,640]{1,0:T(8,128)(2,1)S(1)} %get-tuple-element.30), channel_id=1, source_target_pairs={{0,8},{8,16},{16,24},{24,32},{32,40},{40,48},{48,56},{56,64},{64,7... | collective-permute-start | bytes 245768 | tf_op jit(solution)/shard_map/ppermute | solution.py:365
  77.2 1.0 order.1.main_ref
  78.2 0.0 collective-permute-done.12.above_ref
  78.2 5.5 %collective-permute-done.13.below_ref = bf16[64,640]{1,0:T(8,128)(2,1)S(1)} collective-permute-done((bf16[64,640]{1,0:T(8,128)(2,1)S(1)}, bf16[64,640]{1,0:T(8,128)(2,1)S(1)}, u32[]{:S(2)}, u32[]{:S(2)}) %collective-permute-start.13) | collective-permute-done | bytes 81952 | tf_op jit(solution)/shard_map/ppermute | solution.py:365
  83.7 0.0 copy-done.4
  83.7 12.1 %synthesis.1 = bf16[2,160,5120]{2,1,0:T(8,128)(2,1)} custom-call(bf16[512,640]{1,0:T(8,128)(2,1)S(1)} %order.1.main_ref, bf16[128,640]{1,0:T(8,128)(2,1)S(1)} %get-tuple-element.28.rest_ref, bf16[64,640]{1,0:T(8,128)(2,1)S(1)} %collective-permute-done.12.above_ref, bf16[64,640]{1,0:T(8,128)(2,1)S(1)} %collective-permute-done.13.below_ref, ...), custom_call_target="tpu_custom_call" | custom-call | flops 4400000000 | bytes 18000000 | tf_op jit(solution)/shard_map/synthesis/pallas_call | solution.py:377
  (1 shorter events, 0.0 us)
Async XLA Ops:
  0.0 45.0 %copy-start.1 = (bf16[3,160,256]{2,1,0:T(8,128)(2,1)S(1)}, bf16[3,160,256]{2,1,0:T(8,128)(2,1)}, u32[]{:S(2)}) copy-start(bf16[3,160,256]{2,1,0:T(8,128)(2,1)} %constant.6.clone.refs_7_) | copy-start | bytes 737284
  0.0 45.0 %copy-start.3 = (s32[640]{0:T(1024)S(1)}, s32[640]{0:T(1024)}, u32[]{:S(2)}) copy-start(s32[640]{0:T(1024)} %refs_0_.3) | copy-start | bytes 7684
  0.0 45.0 %copy-start.6 = (s32[16]{0:T(128)S(1)}, s32[16]{0:T(128)}, u32[]{:S(2)}) copy-start(s32[16]{0:T(128)} %refs_1_.3) | copy-start | bytes 196
  1.8 9.5 %collective-permute-start.2 = (bf16[40,768]{1,0:T(8,128)(2,1)}, bf16[40,768]{1,0:T(8,128)(2,1)S(1)}, u32[]{:S(2)}, u32[]{:S(2)}) collective-permute-start(bf16[40,768]{1,0:T(8,128)(2,1)} %get-tuple-element.18), channel_id=1, source_target_pairs={{0,16},{8,24},{16,0},{24,8},{32,48},{40,56},{48,32},{56,40},{64,80... | collective-permute-start | bytes 184328 | tf_op jit(solution)/shard_map/ppermute | solution.py:320
  5.6 6.2 %collective-permute-start.1 = (bf16[40,768]{1,0:T(8,128)(2,1)}, bf16[40,768]{1,0:T(8,128)(2,1)S(1)}, u32[]{:S(2)}, u32[]{:S(2)}) collective-permute-start(bf16[40,768]{1,0:T(8,128)(2,1)} %get-tuple-element.18), channel_id=1, source_target_pairs={{0,24},{8,0},{16,8},{24,16},{32,56},{40,32},{48,40},{56,48},{64,88... | collective-permute-start | bytes 184328 | tf_op jit(solution)/shard_map/ppermute | solution.py:320
  6.3 5.6 %collective-permute-start = (bf16[40,768]{1,0:T(8,128)(2,1)}, bf16[40,768]{1,0:T(8,128)(2,1)S(1)}, u32[]{:S(2)}, u32[]{:S(2)}) collective-permute-start(bf16[40,768]{1,0:T(8,128)(2,1)} %get-tuple-element.18), channel_id=1, source_target_pairs={{0,8},{8,16},{16,24},{24,0},{32,40},{40,48},{48,56},{56,32},{64,72... | collective-permute-start | bytes 184328 | tf_op jit(solution)/shard_map/ppermute | solution.py:320
  7.7 5.9 %collective-permute-start.5 = (bf16[40,768]{1,0:T(8,128)(2,1)}, bf16[40,768]{1,0:T(8,128)(2,1)S(1)}, u32[]{:S(2)}, u32[]{:S(2)}) collective-permute-start(bf16[40,768]{1,0:T(8,128)(2,1)} %get-tuple-element.19), channel_id=1, source_target_pairs={{0,64},{8,72},{16,80},{24,88},{32,96},{40,104},{48,112},{56,120},{... | collective-permute-start | bytes 184328 | tf_op jit(solution)/shard_map/ppermute | solution.py:320
  9.8 4.5 %collective-permute-start.4 = (bf16[40,768]{1,0:T(8,128)(2,1)}, bf16[40,768]{1,0:T(8,128)(2,1)S(1)}, u32[]{:S(2)}, u32[]{:S(2)}) collective-permute-start(bf16[40,768]{1,0:T(8,128)(2,1)} %get-tuple-element.19), channel_id=1, source_target_pairs={{0,96},{8,104},{16,112},{24,120},{32,0},{40,8},{48,16},{56,24},{64... | collective-permute-start | bytes 184328 | tf_op jit(solution)/shard_map/ppermute | solution.py:320
  11.2 4.4 %collective-permute-start.3 = (bf16[40,768]{1,0:T(8,128)(2,1)}, bf16[40,768]{1,0:T(8,128)(2,1)S(1)}, u32[]{:S(2)}, u32[]{:S(2)}) collective-permute-start(bf16[40,768]{1,0:T(8,128)(2,1)} %get-tuple-element.19), channel_id=1, source_target_pairs={{0,32},{8,40},{16,48},{24,56},{32,64},{40,72},{48,80},{56,88},{64,... | collective-permute-start | bytes 184328 | tf_op jit(solution)/shard_map/ppermute | solution.py:320
  16.5 10.0 %collective-permute-start.8 = (bf16[4,40,768]{2,1,0:T(8,128)(2,1)S(1)}, bf16[4,40,768]{2,1,0:T(8,128)(2,1)S(1)}, u32[]{:S(2)}, u32[]{:S(2)}) collective-permute-start(bf16[4,40,768]{2,1,0:T(8,128)(2,1)S(1)} %pad_maximum_fusion.refs_2_), channel_id=1, source_target_pairs={{0,64},{8,72},{16,80},{24,88},{32,96},{40,104},{48,112},{56,120},{... | collective-permute-start | bytes 737288 | tf_op jit(solution)/shard_map/ppermute | solution.py:320
  17.8 11.0 %collective-permute-start.7 = (bf16[4,40,768]{2,1,0:T(8,128)(2,1)S(1)}, bf16[4,40,768]{2,1,0:T(8,128)(2,1)S(1)}, u32[]{:S(2)}, u32[]{:S(2)}) collective-permute-start(bf16[4,40,768]{2,1,0:T(8,128)(2,1)S(1)} %pad_maximum_fusion.refs_2_), channel_id=1, source_target_pairs={{0,96},{8,104},{16,112},{24,120},{32,0},{40,8},{48,16},{56,24},{64... | collective-permute-start | bytes 737288 | tf_op jit(solution)/shard_map/ppermute | solution.py:320
  19.3 9.5 %collective-permute-start.6 = (bf16[4,40,768]{2,1,0:T(8,128)(2,1)S(1)}, bf16[4,40,768]{2,1,0:T(8,128)(2,1)S(1)}, u32[]{:S(2)}, u32[]{:S(2)}) collective-permute-start(bf16[4,40,768]{2,1,0:T(8,128)(2,1)S(1)} %pad_maximum_fusion.refs_2_), channel_id=1, source_target_pairs={{0,32},{8,40},{16,48},{24,56},{32,64},{40,72},{48,80},{56,88},{64,... | collective-permute-start | bytes 737288 | tf_op jit(solution)/shard_map/ppermute | solution.py:320
  20.4 20.1 %collective-permute-start.11 = (bf16[4,40,768]{2,1,0:T(8,128)(2,1)S(1)}, bf16[4,40,768]{2,1,0:T(8,128)(2,1)S(1)}, u32[]{:S(2)}, u32[]{:S(2)}) collective-permute-start(bf16[4,40,768]{2,1,0:T(8,128)(2,1)S(1)} %pad_maximum_fusion.1.refs_2_), channel_id=1, source_target_pairs={{0,16},{8,24},{16,0},{24,8},{32,48},{40,56},{48,32},{56,40},{64,80... | collective-permute-start | bytes 737288 | tf_op jit(solution)/shard_map/ppermute | solution.py:320
  21.5 19.0 %collective-permute-start.10 = (bf16[4,40,768]{2,1,0:T(8,128)(2,1)S(1)}, bf16[4,40,768]{2,1,0:T(8,128)(2,1)S(1)}, u32[]{:S(2)}, u32[]{:S(2)}) collective-permute-start(bf16[4,40,768]{2,1,0:T(8,128)(2,1)S(1)} %pad_maximum_fusion.1.refs_2_), channel_id=1, source_target_pairs={{0,24},{8,0},{16,8},{24,16},{32,56},{40,32},{48,40},{56,48},{64,88... | collective-permute-start | bytes 737288 | tf_op jit(solution)/shard_map/ppermute | solution.py:320
  26.5 14.0 %collective-permute-start.9 = (bf16[4,40,768]{2,1,0:T(8,128)(2,1)S(1)}, bf16[4,40,768]{2,1,0:T(8,128)(2,1)S(1)}, u32[]{:S(2)}, u32[]{:S(2)}) collective-permute-start(bf16[4,40,768]{2,1,0:T(8,128)(2,1)S(1)} %pad_maximum_fusion.1.refs_2_), channel_id=1, source_target_pairs={{0,8},{8,16},{16,24},{24,0},{32,40},{40,48},{48,56},{56,32},{64,72... | collective-permute-start | bytes 737288 | tf_op jit(solution)/shard_map/ppermute | solution.py:320
  28.8 0.9 copy-start
  29.7 0.7 copy-start.2
  30.4 0.7 copy-start.5
  40.5 43.3 %copy-start.4 = (bf16[160,32]{1,0:T(8,128)(2,1)S(1)}, bf16[160,32]{1,0:T(8,128)(2,1)}, u32[]{:S(2)}) copy-start(bf16[160,32]{1,0:T(8,128)(2,1)} %constant.7.clone.expand_ref) | copy-start | bytes 30724
  40.5 14.5 %all-to-all-start = ((bf16[8,40,768]{2,1,0:T(8,128)(2,1)}), bf16[8,40,768]{2,1,0:T(8,128)(2,1)S(1)}, u32[]{:S(2)}, u32[]{:S(2)}) async-start(bf16[8,40,768]{2,1,0:T(8,128)(2,1)} %legendre0.1), calls=%async_computation | async-start | bytes 983040 | tf_op jit(solution)/shard_map/all_to_all | solution.py:349
  55.0 14.3 %all-to-all-start.1 = ((bf16[8,40,768]{2,1,0:T(8,128)(2,1)}), bf16[8,40,768]{2,1,0:T(8,128)(2,1)S(1)}, u32[]{:S(2)}, u32[]{:S(2)}) async-start(bf16[8,40,768]{2,1,0:T(8,128)(2,1)} %legendre1.1), calls=%async_computation.1 | async-start | bytes 983040 | tf_op jit(solution)/shard_map/all_to_all | solution.py:349
  70.0 8.2 %collective-permute-start.12 = (bf16[64,640]{1,0:T(8,128)(2,1)S(1)}, bf16[64,640]{1,0:T(8,128)(2,1)S(1)}, u32[]{:S(2)}, u32[]{:S(2)}) collective-permute-start(bf16[64,640]{1,0:T(8,128)(2,1)S(1)} %get-tuple-element.29), channel_id=1, source_target_pairs={{8,0},{16,8},{24,16},{32,24},{40,32},{48,40},{56,48},{64,56},{72,6... | collective-permute-start | bytes 245768 | tf_op jit(solution)/shard_map/ppermute | solution.py:364
  75.3 8.4 %collective-permute-start.13 = (bf16[64,640]{1,0:T(8,128)(2,1)S(1)}, bf16[64,640]{1,0:T(8,128)(2,1)S(1)}, u32[]{:S(2)}, u32[]{:S(2)}) collective-permute-start(bf16[64,640]{1,0:T(8,128)(2,1)S(1)} %get-tuple-element.30), channel_id=1, source_target_pairs={{0,8},{8,16},{16,24},{24,32},{32,40},{40,48},{48,56},{56,64},{64,7... | collective-permute-start | bytes 245768 | tf_op jit(solution)/shard_map/ppermute | solution.py:365

commit v3 on v2

--- a/solution.py
+++ b/solution.py
@@ -26,10 +26,12 @@
 PART_SLOTS = SLOTS // HALVES
 RANK = 16
 WIDTH = 4 * LANE + 4 * (BAND - LANE + 2 * RANK)
-TILE = 512
+TILE = 256
+STEPS = NLON // 2 // TILE
 GROUP = 4
-SMALL_BYTES = 48 * 2**20
-LARGE_BYTES = 52 * 2**20
+SMALL_BYTES = 16 * 2**20
+FETCH_BYTES = int(45.5 * 2**20)
+LARGE_BYTES = int(50 * 2**20)
 
 LIFT_ALPHA = -1.586134342059924
 LIFT_BETA = -0.052980118572961
@@ -54,14 +56,18 @@
     return result
 
 
-def longitude_matrix():
+def longitude_matrices():
     waves = np.arange(NWAVE)
     phase = waves[:, None] * np.arange(NLON)[None, :] % NLON
     angle = phase * (2.0 * math.pi / NLON)
     weight = np.where(waves == 0, 1.0, 2.0)[:, None] / math.sqrt(2.0 * NWAVE)
     table = np.concatenate([weight * np.cos(angle), -weight * np.sin(angle)], axis=0)
     table = table.astype(np.float32).astype(ml_dtypes.bfloat16).astype(np.float64)
-    return analyze(table.T, WL, "wrap").T.astype(np.float32).astype(ml_dtypes.bfloat16)
+    lifted = analyze(table.T, WL, "wrap").T
+    half = lifted[:, : NLON // 2].reshape(2 * NWAVE, STEPS, TILE).swapaxes(0, 1)
+    middle = np.zeros((NWAVE, LANE))
+    middle[:, 0] = lifted[:NWAVE, NLON // 2]
+    return [values.astype(np.float32).astype(ml_dtypes.bfloat16) for values in (half, middle)]
 
 
 def latitude_matrices():
@@ -94,79 +100,99 @@
     )
 
 
-def pack_kernel(order_ref, spectra_ref, *refs):
-    outs, (wide, low, high, packed) = refs[:HALVES], refs[HALVES:]
+def pack_kernel(order_ref, spectra_ref, order_any, writer_any, matrix_any, *refs):
+    outs, (order_out, writer_out, matrix_out) = refs[:HALVES], refs[HALVES : HALVES + 3]
+    wide, low, high, packed, sems = refs[HALVES + 3 :]
+    band = lax.axis_index("lat")
+    variant = jnp.where(band == 0, 0, jnp.where(band == BANDS - 1, 2, 1))
+    copies = [
+        pltpu.make_async_copy(order_any, order_out, sems.at[0]),
+        pltpu.make_async_copy(writer_any, writer_out, sems.at[1]),
+        pltpu.make_async_copy(matrix_any.at[variant], matrix_out, sems.at[2]),
+    ]
+    for copy in copies:
+        copy.start()
     first = lax.axis_index("wave") * SLOTS
     for pair in range(PAIRS):
         low[pl.ds(pair, 1), :] = jnp.full((1, LANE), order_ref[first + 2 * pair], jnp.int32)
         high[pl.ds(pair, 1), :] = jnp.full((1, LANE), order_ref[first + 2 * pair + 1], jnp.int32)
     waves_a, waves_b = low[...], high[...]
     lane = lax.broadcasted_iota(jnp.int32, (PAIRS, LANE), 1)
+    zero = jnp.zeros((PAIRS, LANE), jnp.float32)
     for part in range(2):
+        firsts, seconds = [], []
         for block in range(5):
             wide[block] = spectra_ref[0, part, :, block * LANE : (block + 1) * LANE].astype(jnp.float32)
+            values = wide[block, pl.ds(0, PAIRS, stride=2), :]
+            firsts.append(jnp.where(lane + block * LANE >= waves_a, values, zero))
+            values = wide[block, pl.ds(1, PAIRS, stride=2), :]
+            seconds.append(jnp.where(lane + block * LANE >= waves_b, values, zero))
         for block in range(BLOCKS):
-            taken = jnp.zeros((PAIRS, LANE), jnp.float32)
-            if block <= 4:
-                values = wide[4 - block, pl.ds(1, PAIRS, stride=2), :]
-                taken = jnp.where(lane + (4 - block) * LANE >= waves_b, values, taken)
-            if block >= 1:
-                values = wide[block - 1, pl.ds(0, PAIRS, stride=2), :]
-                values = jnp.where(lane + (block - 1) * LANE >= waves_a, values, jnp.zeros_like(values))
-                taken = jnp.where(waves_a < block * LANE, values, taken)
+            taken = firsts[block - 1] if block else zero
+            for cut in range(block, 5):
+                inside = (waves_a >= cut * LANE) & (waves_a < (cut + 1) * LANE)
+                taken = jnp.where(inside, seconds[4 - cut + block], taken)
             for half in range(HALVES):
                 packed[half, pl.ds(part * PART_PAIRS, PART_PAIRS), block * LANE : (block + 1) * LANE] = taken[
                     half * PART_PAIRS : (half + 1) * PART_PAIRS
                 ]
     for half in range(HALVES):
         outs[half][...] = packed[half].astype(jnp.bfloat16)
+    for copy in copies:
+        copy.wait()
+
+
+def fetch_kernel(order_ref, legendre_ref, *refs):
+    outs, sems = refs[:HALVES], refs[HALVES]
+    first = lax.axis_index("wave") * SLOTS
+    for half in range(HALVES):
+
+        def fetch(member, carry, half=half):
+            pair = half * PART_PAIRS + member
+            block = order_ref[first + 2 * pair] // LANE
+            for cut in range(5):
+
+                @pl.when(block == cut)
+                def _():
+                    pltpu.make_async_copy(
+                        legendre_ref.at[2 * pair + 1, :, pl.ds((4 - cut) * LANE, (cut + 1) * LANE)],
+                        outs[half].at[member, :, pl.ds(0, (cut + 1) * LANE)],
+                        sems.at[half],
+                    ).start()
+                    pltpu.make_async_copy(
+                        legendre_ref.at[2 * pair, :, pl.ds(cut * LANE, (5 - cut) * LANE)],
+                        outs[half].at[member, :, pl.ds((cut + 1) * LANE, (5 - cut) * LANE)],
+                        sems.at[half],
+                    ).start()
+
+            return carry
+
+        lax.fori_loop(0, PART_PAIRS, fetch, 0)
+    for half in range(HALVES):
+        pltpu.make_async_copy(outs[half], outs[half], sems.at[half]).wait()
 
 
 def legendre_kernel(half, order_ref, writer_ref, *refs):
     parts = refs[:4]
-    legendre_ref, matrix_ref, out_ref = refs[4:7]
-    held, staged, spread, rows, results, matrix, sems, staged_sems, matrix_sem = refs[7:]
+    held, matrix, out_ref = refs[4:7]
+    spread, rows, results = refs[7:]
     base = half * PART_PAIRS
     first = lax.axis_index("wave") * SLOTS + 2 * base
     band = lax.axis_index("lat")
-    variant = jnp.where(band == 0, 0, jnp.where(band == BANDS - 1, 2, 1))
-    copies = [pltpu.make_async_copy(parts[i], staged.at[i], staged_sems.at[i]) for i in range(4)]
-    for copy in copies:
-        copy.start()
-
-    def fetch(pair, carry):
-        wave = order_ref[first + 2 * pair]
-        for block in range(BLOCKS):
-            from_a = wave < block * LANE
-            slot = 2 * (base + pair) + jnp.where(from_a, 0, 1)
-            source = jnp.where(from_a, block - 1, 4 - block)
-            pltpu.make_async_copy(
-                legendre_ref.at[slot, :, pl.ds(pl.multiple_of(source * LANE, LANE), LANE)],
-                held.at[pair, :, pl.ds(block * LANE, LANE)],
-                sems.at[pair],
-            ).start()
-        return carry
-
-    lax.fori_loop(0, PART_PAIRS, fetch, 0)
-    matrix_copy = pltpu.make_async_copy(matrix_ref.at[variant], matrix, matrix_sem)
-    matrix_copy.start()
-
     band_x, band_z = band // 4, lax.rem(band, 4)
     steps = (0, 3, 1, 2)
     for outer in range(4):
-        copies[outer].wait()
         for inner in range(4):
             along_x, along_z = (outer, inner) if half == 0 else (inner, outer)
             field = 4 * lax.rem(band_x + steps[along_x], 4) + lax.rem(band_z + steps[along_z], 4)
             start = pl.multiple_of(field * 2 * PART_PAIRS, 8)
             for block in range(BLOCKS):
-                values = staged[outer, inner, :, block * LANE : (block + 1) * LANE]
+                values = parts[outer][inner, :, block * LANE : (block + 1) * LANE]
                 spread[block, pl.ds(start, 2 * PART_PAIRS), :] = values.astype(jnp.float32)
 
     def contract(group, carry):
         for member in range(GROUP):
             pair = group * GROUP + member
-            pltpu.make_async_copy(held.at[pair], held.at[pair], sems.at[pair]).wait()
             wave = order_ref[first + 2 * pair]
             lower, upper = [], []
             for block in range(BLOCKS):
@@ -188,7 +214,6 @@
         return carry
 
     lax.fori_loop(0, PART_PAIRS // GROUP, contract, 0)
-    matrix_copy.wait()
 
     chunk = 2 * FIELDS * PART_SLOTS // 4
     for index in range(4):
@@ -249,28 +274,66 @@
     out_ref[...] = ordered.T.astype(jnp.bfloat16)
 
 
-def synthesis_kernel(main_ref, rest_ref, above_ref, below_ref, expand_ref, table_ref, out_ref, left):
-    @pl.when(pl.program_id(0) == 0)
-    def _():
-        rest = BAND - LANE
+def synthesis_kernel(main_ref, rest_ref, above_ref, below_ref, expand_ref, middle_ref, table_ref, out_ref, *refs):
+    left, table, tiles, even, flip, table_sems, out_sems = refs
+    tables = [pltpu.make_async_copy(table_ref.at[step], table.at[step], table_sems.at[step]) for step in range(STEPS)]
+    for copy in reversed(tables):
+        copy.start()
+    rest = BAND - LANE
+    for field in range(2):
+        for part in range(2):
+            which = 2 * field + part
+            edges = slice(which * RANK, (which + 1) * RANK)
+            added = jnp.dot(
+                expand_ref[...],
+                jnp.concatenate([above_ref[edges], below_ref[edges]], axis=0),
+                preferred_element_type=jnp.float32,
+            )
+            own = main_ref[which * LANE : (which + 1) * LANE].astype(jnp.float32)
+            left[part, field * BAND : field * BAND + LANE] = (own + added[:LANE]).astype(jnp.bfloat16)
+            own = rest_ref[which * rest : (which + 1) * rest].astype(jnp.float32)
+            left[part, field * BAND + LANE : (field + 1) * BAND] = (own + added[LANE:]).astype(jnp.bfloat16)
+    total = lax.broadcasted_iota(jnp.int32, (TILE, TILE), 0) + lax.broadcasted_iota(jnp.int32, (TILE, TILE), 1)
+    flip[...] = jnp.where(total == TILE, 1.0, 0.0).astype(jnp.bfloat16)
+    even[...] = jnp.dot(left[0], middle_ref[...], preferred_element_type=jnp.float32)
+
+    def place(tile, where):
+        return [
+            pltpu.make_async_copy(
+                tiles.at[tile, field],
+                out_ref.at[field, :, pl.ds(where, TILE)],
+                out_sems.at[tile, field],
+            )
+            for field in range(2)
+        ]
+
+    def step(count, carry):
+        tile = STEPS - 1 - count
+        pltpu.make_async_copy(table_ref.at[tile], table.at[tile], table_sems.at[tile]).wait()
+        cosine = jnp.dot(left[0], table[tile, :NWAVE], preferred_element_type=jnp.float32)
+        sine = jnp.dot(left[1], table[tile, NWAVE:], preferred_element_type=jnp.float32)
+        front = (cosine + sine).astype(jnp.bfloat16)
+        back = cosine - sine
+        turned = jnp.dot(back.astype(jnp.bfloat16), flip[...], preferred_element_type=jnp.float32)
+        lane = lax.broadcasted_iota(jnp.int32, (2 * BAND, LANE), 1)
+        mirror = 2 * STEPS - 1 - tile
+        head = jnp.where(lane == 0, even[...], turned[:, :LANE]).astype(jnp.bfloat16)
+        tail = turned[:, LANE:].astype(jnp.bfloat16)
+        even[...] = back[:, :LANE]
         for field in range(2):
-            for part in range(2):
-                which = 2 * field + part
-                edges = slice(which * RANK, (which + 1) * RANK)
-                added = jnp.dot(
-                    expand_ref[...],
-                    jnp.concatenate([above_ref[edges], below_ref[edges]], axis=0),
-                    preferred_element_type=jnp.float32,
-                )
-                lanes = slice(part * NWAVE, (part + 1) * NWAVE)
-                own = main_ref[which * LANE : (which + 1) * LANE].astype(jnp.float32)
-                left[field * BAND : field * BAND + LANE, lanes] = (own + added[:LANE]).astype(jnp.bfloat16)
-                own = rest_ref[which * rest : (which + 1) * rest].astype(jnp.float32)
-                left[field * BAND + LANE : (field + 1) * BAND, lanes] = (own + added[LANE:]).astype(jnp.bfloat16)
-
-    sums = jnp.dot(left[...], table_ref[...], preferred_element_type=jnp.float32)
-    out_ref[0] = sums[:BAND].astype(jnp.bfloat16)
-    out_ref[1] = sums[BAND:].astype(jnp.bfloat16)
+            rows = slice(field * BAND, (field + 1) * BAND)
+            tiles[tile, field] = front[rows]
+            tiles[mirror, field, :, :LANE] = head[rows]
+            tiles[mirror, field, :, LANE:] = tail[rows]
+        for which in (tile, mirror):
+            for copy in place(which, pl.multiple_of(which * TILE, TILE)):
+                copy.start()
+        return carry
+
+    lax.fori_loop(0, STEPS, step, 0)
+    for tile in range(2 * STEPS):
+        for copy in place(tile, tile * TILE):
+            copy.wait()
 
 
 def along_z(step):
@@ -288,6 +351,7 @@
 SMEM = pl.BlockSpec(memory_space=pltpu.SMEM)
 VMEM = pl.BlockSpec(memory_space=pltpu.VMEM)
 ANY = pl.BlockSpec(memory_space=pl.ANY)
+FETCH = pltpu.CompilerParams(vmem_limit_bytes=FETCH_BYTES)
 SMALL = pltpu.CompilerParams(vmem_limit_bytes=SMALL_BYTES)
 LARGE = pltpu.CompilerParams(vmem_limit_bytes=LARGE_BYTES)
 
@@ -296,22 +360,38 @@
     return jax.ShapeDtypeStruct(shape, jnp.bfloat16)
 
 
-def make_on_device(table, matrices, expand):
+def make_on_device(table, middle, matrices, expand):
     def on_device(spectra, legendre, wave_order, writer_order):
-        halves = pl.pallas_call(
+        *halves, orders, writers, matrix = pl.pallas_call(
             pack_kernel,
-            out_shape=[bf16(2 * PART_PAIRS, BLOCKS * LANE)] * HALVES,
-            in_specs=[SMEM, VMEM],
-            out_specs=[VMEM] * HALVES,
+            out_shape=[bf16(2 * PART_PAIRS, BLOCKS * LANE)] * HALVES
+            + [
+                jax.ShapeDtypeStruct((NWAVE,), jnp.int32),
+                jax.ShapeDtypeStruct((FIELDS,), jnp.int32),
+                bf16(BAND, 2 * LANE),
+            ],
+            in_specs=[SMEM, VMEM, ANY, ANY, ANY],
+            out_specs=[VMEM] * HALVES + [ANY] * 3,
             scratch_shapes=[
                 pltpu.VMEM((5, SLOTS, LANE), jnp.float32),
                 pltpu.VMEM((PAIRS, LANE), jnp.int32),
                 pltpu.VMEM((PAIRS, LANE), jnp.int32),
                 pltpu.VMEM((HALVES, 2 * PART_PAIRS, BLOCKS * LANE), jnp.float32),
+                pltpu.SemaphoreType.DMA((3,)),
             ],
             name="pack",
-        )(wave_order, spectra)
+        )(wave_order, spectra, wave_order, writer_order, matrices)
         order = wave_order.reshape(OWNERS, HALVES, PART_SLOTS).swapaxes(0, 1).reshape(1, NWAVE)
+        held = pl.pallas_call(
+            fetch_kernel,
+            out_shape=[bf16(PART_PAIRS, BAND, BLOCKS * LANE)] * HALVES,
+            in_specs=[SMEM, ANY],
+            out_specs=[VMEM] * HALVES,
+            scratch_shapes=[pltpu.SemaphoreType.DMA((HALVES,))],
+            compiler_params=FETCH,
+            cost_estimate=pl.CostEstimate(flops=0, bytes_accessed=14_000_000, transcendentals=0),
+            name="fetch",
+        )(orders, legendre)
 
         axes = ((along_z, along_x), (along_x, along_z))
         gathered = halves
@@ -320,32 +400,31 @@
                 [values] + [lax.ppermute(values, "lat", axes[half][stage](step)) for step in (1, 3, 2)]
                 for half, values in enumerate(gathered)
             ]
-            gathered = lax.optimization_barrier([jnp.stack(blocks) for blocks in arrived]) if stage == 0 else arrived
+            if stage == 0:
+                gathered, held = lax.optimization_barrier(([jnp.stack(blocks) for blocks in arrived], held))
+            else:
+                gathered = arrived
 
         waves = []
         for half in range(HALVES):
             lifted = pl.pallas_call(
                 lambda *refs, half=half: legendre_kernel(half, *refs),
                 out_shape=bf16(OWNERS, PART_SLOTS, WIDTH),
-                in_specs=[SMEM, SMEM] + [ANY] * 6,
+                in_specs=[SMEM, SMEM] + [VMEM] * 6,
                 out_specs=VMEM,
                 scratch_shapes=[
-                    pltpu.VMEM((PART_PAIRS, BAND, BLOCKS * LANE), jnp.bfloat16),
-                    pltpu.VMEM((4, 4, 2 * PART_PAIRS, BLOCKS * LANE), jnp.bfloat16),
                     pltpu.VMEM((BLOCKS, 2 * FIELDS * PART_PAIRS, LANE), jnp.float32),
                     pltpu.VMEM((2, 2 * FIELDS * PART_SLOTS, LANE), jnp.float32),
                     pltpu.VMEM((2, 2 * FIELDS * PART_SLOTS, LANE), jnp.float32),
-                    pltpu.VMEM((BAND, 2 * LANE), jnp.bfloat16),
-                    pltpu.SemaphoreType.DMA((PART_PAIRS,)),
-                    pltpu.SemaphoreType.DMA((4,)),
-                    pltpu.SemaphoreType.DMA,
                 ],
                 compiler_params=SMALL,
                 cost_estimate=pl.CostEstimate(flops=400_000_000, bytes_accessed=8_000_000, transcendentals=0),
                 name=f"legendre{half}",
-            )(wave_order, writer_order, *gathered[half], legendre, matrices)
+            )(orders, writers, *gathered[half], held[half], matrix)
             if half + 1 < HALVES:
                 lifted, gathered[half + 1] = lax.optimization_barrier((lifted, gathered[half + 1]))
+            if waves:
+                lifted, waves[-1] = lax.optimization_barrier((lifted, waves[-1]))
             received = lax.all_to_all(lifted, "wave", split_axis=0, concat_axis=0, tiled=True)
             waves.append(received.reshape(OWNERS * PART_SLOTS, WIDTH))
 
@@ -376,24 +455,30 @@
         )(chosen, *waves)
         return pl.pallas_call(
             synthesis_kernel,
-            grid=(NLON // TILE,),
             out_shape=bf16(2, BAND, NLON),
-            in_specs=[VMEM] * 5 + [pl.BlockSpec((2 * NWAVE, TILE), lambda j: (0, j))],
-            out_specs=pl.BlockSpec((2, BAND, TILE), lambda j: (0, 0, j)),
-            scratch_shapes=[pltpu.VMEM((2 * BAND, 2 * NWAVE), jnp.bfloat16)],
+            in_specs=[VMEM] * 6 + [ANY],
+            out_specs=ANY,
+            scratch_shapes=[
+                pltpu.VMEM((2, 2 * BAND, NWAVE), jnp.bfloat16),
+                pltpu.VMEM((STEPS, 2 * NWAVE, TILE), jnp.bfloat16),
+                pltpu.VMEM((2 * STEPS, 2, BAND, TILE), jnp.bfloat16),
+                pltpu.VMEM((2 * BAND, LANE), jnp.float32),
+                pltpu.VMEM((TILE, TILE), jnp.bfloat16),
+                pltpu.SemaphoreType.DMA((STEPS,)),
+                pltpu.SemaphoreType.DMA((2 * STEPS, 2)),
+            ],
             compiler_params=LARGE,
-            cost_estimate=pl.CostEstimate(flops=4_400_000_000, bytes_accessed=18_000_000, transcendentals=0),
+            cost_estimate=pl.CostEstimate(flops=2_400_000_000, bytes_accessed=11_000_000, transcendentals=0),
             name="synthesis",
-        )(ordered, tail, above, below, expand, table)
+        )(ordered, tail, above, below, expand, middle, table)
 
     return on_device
 
 
 def solution(mesh):
-    table = longitude_matrix()
-    matrices, expand = latitude_matrices()
+    constants = [*longitude_matrices(), *latitude_matrices()]
     return jax.shard_map(
-        make_on_device(jnp.asarray(table), jnp.asarray(matrices), jnp.asarray(expand)),
+        make_on_device(*[jnp.asarray(values) for values in constants]),
         mesh=mesh,
         in_specs=(P("lat", None, "wave", None), P("wave", "lat", None), P(), P()),
         out_specs=P("wave", "lat", None),

time: 96.7 us -> 96 us (level)
  waiting for transfers between devices: 22.5 us -> 29.5 us
  Pallas kernels: 34.3 us -> 30.3 us
  starting transfers between devices: 34.7 us -> 32.3 us
  other arithmetic: 1.72 us -> 0.07 us
    pallas_call x2, Pallas kernels: 18.8 us -> 8.29 us  [on_device(): pl.pallas_call(lambda *refs, half=half: legendre_kernel(half, *refs), out...]
    ppermute x12, waiting for transfers between devices: 6.66 us -> 10.8 us  [on_device(): lax.ppermute(values, 'lat', axes[half][stage](step))]
    pallas_call x1, Pallas kernels: 1.74 us -> 5.29 us  [on_device(): pl.pallas_call(pack_kernel, out_shape=[bf16(2 * PART_PAIRS, BLOCKS * LANE...]
    pallas_call x1 -> x2, Pallas kernels: 12.1 us -> 15.1 us  [the longest x1 8.22 us: on_device(): pl.pallas_call(synthesis_kernel, out_shape=bf16(2, BAND, NLON), in_specs=...]
    ppermute x12, starting transfers between devices: 18.7 us -> 15.8 us  [on_device(): lax.ppermute(values, 'lat', axes[half][stage](step))]
    all_to_all x2, waiting for transfers between devices: 10.3 us -> 13.2 us  [on_device(): lax.all_to_all(lifted, 'wave', split_axis=0, concat_axis=0, tiled=True)]
    another operation x2, other arithmetic: 1.72 us -> 0.07 us  [on_device(): jnp.stack(blocks)]
    ppermute x1, starting transfers between devices: 5.33 us -> 6.63 us  [on_device(): above = lax.ppermute(above, 'lat', neighbour(-1))]
  transfers between devices with their start and end apart: 16 -> 16, of which waited for: 9 -> 8; matrix products, arithmetic and copies ran while one was open for 1% -> 0% of each run, Pallas kernels for 21% -> 17%
where the time goes in v3:
time: 96 us; the launch traced here: 95.6 us
  starting transfers between devices  32.3 us (34%)
  Pallas kernels  30.3 us (32%)
  waiting for transfers between devices  29.5 us (31%)
  local copies, waits for them, and re-layouts  3.28 us (3%)
    ppermute x12, starting transfers between devices, on_device(): lax.ppermute(values, 'lat', axes[half][stage](step))  15.8 us
    all_to_all x2, waiting for transfers between devices, on_device(): lax.all_to_all(lifted, 'wave', split_axis=0, concat_axis=0, tiled=True)  13.2 us
    ppermute x12, waiting for transfers between devices, on_device(): lax.ppermute(values, 'lat', axes[half][stage](step))  10.8 us
    pallas_call x2, Pallas kernels, on_device(): pl.pallas_call(lambda *refs, half=half: legendre_kernel(half, *refs), out...  8.29 us
    pallas_call x1, Pallas kernels, on_device(): pl.pallas_call(synthesis_kernel, out_shape=bf16(2, BAND, NLON), in_specs=...  8.22 us
    all_to_all x2, starting transfers between devices, on_device(): lax.all_to_all(lifted, 'wave', split_axis=0, concat_axis=0, tiled=True)  7.96 us
    pallas_call x1, Pallas kernels, on_device(): pl.pallas_call(fetch_kernel, out_shape=[bf16(PART_PAIRS, BAND, BLOCKS * L...  6.9 us
    ppermute x1, starting transfers between devices, on_device(): above = lax.ppermute(above, 'lat', neighbour(-1))  6.63 us
  transfers between devices with their start and end apart: 16, of which 8 were waited for; matrix products, arithmetic and copies ran while one was open for 0% of the time, Pallas kernels for 17%

profile of v3, /device:TPU:2, one launch (start us, length us, event | category | flops | bytes accessed | tf_op | source)
XLA Modules:
  0.0 95.6 jit_solution(18178300615533613950)
XLA Ops:
  0.0 5.3 %pack.1 = (bf16[40,768]{1,0:T(8,128)(2,1)}, bf16[40,768]{1,0:T(8,128)(2,1)}, s32[640]{0:T(1024)}, s32[16]{0:T(128)}, bf16[160,256]{1,0:T(8,128)(2,1)}) custom-call(s32[640]{0:T(1024)} %order_any.1, bf16[1,2,80,640]{3,2,1,0:T(8,128)(2,1)} %spectra_ref.1, s32[640]{0:T(1024)} %order_any.1, s32[16]{0:T(128)} %writer_any.1, ...), custom_call_target="tpu_custom_call" | custom-call | tf_op jit(solution)/shard_map/pack/pallas_call | solution.py:365
  5.3 1.6 %collective-permute-start.3 = (bf16[40,768]{1,0:T(8,128)(2,1)}, bf16[40,768]{1,0:T(8,128)(2,1)S(1)}, u32[]{:S(2)}, u32[]{:S(2)}) collective-permute-start(bf16[40,768]{1,0:T(8,128)(2,1)} %get-tuple-element.30), channel_id=1, source_target_pairs={{0,32},{8,40},{16,48},{24,56},{32,64},{40,72},{48,80},{56,88},{64,... | collective-permute-start | bytes 184328 | tf_op jit(solution)/shard_map/ppermute | solution.py:400
  6.9 0.5 collective-permute-start.4
  7.4 2.1 %collective-permute-start.5 = (bf16[40,768]{1,0:T(8,128)(2,1)}, bf16[40,768]{1,0:T(8,128)(2,1)S(1)}, u32[]{:S(2)}, u32[]{:S(2)}) collective-permute-start(bf16[40,768]{1,0:T(8,128)(2,1)} %get-tuple-element.30), channel_id=1, source_target_pairs={{0,64},{8,72},{16,80},{24,88},{32,96},{40,104},{48,112},{56,120},{... | collective-permute-start | bytes 184328 | tf_op jit(solution)/shard_map/ppermute | solution.py:400
  9.5 1.9 %collective-permute-start = (bf16[40,768]{1,0:T(8,128)(2,1)}, bf16[40,768]{1,0:T(8,128)(2,1)S(1)}, u32[]{:S(2)}, u32[]{:S(2)}) collective-permute-start(bf16[40,768]{1,0:T(8,128)(2,1)} %get-tuple-element.29), channel_id=1, source_target_pairs={{0,8},{8,16},{16,24},{24,0},{32,40},{40,48},{48,56},{56,32},{64,72... | collective-permute-start | bytes 184328 | tf_op jit(solution)/shard_map/ppermute | solution.py:400
  11.4 2.1 %collective-permute-start.1 = (bf16[40,768]{1,0:T(8,128)(2,1)}, bf16[40,768]{1,0:T(8,128)(2,1)S(1)}, u32[]{:S(2)}, u32[]{:S(2)}) collective-permute-start(bf16[40,768]{1,0:T(8,128)(2,1)} %get-tuple-element.29), channel_id=1, source_target_pairs={{0,24},{8,0},{16,8},{24,16},{32,56},{40,32},{48,40},{56,48},{64,88... | collective-permute-start | bytes 184328 | tf_op jit(solution)/shard_map/ppermute | solution.py:400
  13.6 0.0 copy-start.4
  13.6 0.7 copy-done.4
  14.2 0.0 copy-start.7
  14.2 0.0 copy-start.8
  14.2 0.0 copy-start.1
  14.2 0.0 copy-start.6
  14.2 6.9 %fetch.1 = (bf16[20,160,768]{2,1,0:T(8,128)(2,1)S(1)}, bf16[20,160,768]{2,1,0:T(8,128)(2,1)}) custom-call(s32[640]{0:T(1024)S(1)} %copy-done.4, bf16[80,160,640]{2,1,0:T(8,128)(2,1)} %legendre_ref.1), custom_call_target="tpu_custom_call" | custom-call | bytes 14000000 | tf_op jit(solution)/shard_map/fetch/pallas_call | solution.py:385
  21.2 0.0 copy-start.5
  21.2 0.0 collective-permute-done.3
  21.2 0.0 copy-done.7
  21.2 1.9 %collective-permute-start.2 = (bf16[40,768]{1,0:T(8,128)(2,1)S(1)}, bf16[40,768]{1,0:T(8,128)(2,1)S(1)}, u32[]{:S(2)}, u32[]{:S(2)}) collective-permute-start(bf16[40,768]{1,0:T(8,128)(2,1)S(1)} %copy-done.7), channel_id=1, source_target_pairs={{0,16},{8,24},{16,0},{24,8},{32,48},{40,56},{48,32},{56,40},{64,80... | collective-permute-start | bytes 184328 | tf_op jit(solution)/shard_map/ppermute | solution.py:400
  23.1 0.0 collective-permute-done.4
  23.1 0.0 collective-permute-done.5
  23.1 0.0 copy-done.8
  23.2 0.0 collective-permute-done
  23.2 0.0 collective-permute-done.1
  23.2 3.8 %collective-permute-done.2 = bf16[40,768]{1,0:T(8,128)(2,1)S(1)} collective-permute-done((bf16[40,768]{1,0:T(8,128)(2,1)S(1)}, bf16[40,768]{1,0:T(8,128)(2,1)S(1)}, u32[]{:S(2)}, u32[]{:S(2)}) %collective-permute-start.2) | collective-permute-done | bytes 61472 | tf_op jit(solution)/shard_map/ppermute | solution.py:400
  27.0 1.2 %collective-permute-start.6 = (bf16[4,40,768]{2,1,0:T(8,128)(2,1)S(1)}, bf16[4,40,768]{2,1,0:T(8,128)(2,1)S(1)}, u32[]{:S(2)}, u32[]{:S(2)}) collective-permute-start(bf16[4,40,768]{2,1,0:T(8,128)(2,1)S(1)} %pad_maximum_fusion.refs_2_), channel_id=1, source_target_pairs={{0,32},{8,40},{16,48},{24,56},{32,64},{40,72},{48,80},{56,88},{64,... | collective-permute-start | bytes 737288 | tf_op jit(solution)/shard_map/ppermute | solution.py:400
  28.2 0.9 collective-permute-start.7
  29.1 1.5 %collective-permute-start.8 = (bf16[4,40,768]{2,1,0:T(8,128)(2,1)S(1)}, bf16[4,40,768]{2,1,0:T(8,128)(2,1)S(1)}, u32[]{:S(2)}, u32[]{:S(2)}) collective-permute-start(bf16[4,40,768]{2,1,0:T(8,128)(2,1)S(1)} %pad_maximum_fusion.refs_2_), channel_id=1, source_target_pairs={{0,64},{8,72},{16,80},{24,88},{32,96},{40,104},{48,112},{56,120},{... | collective-permute-start | bytes 737288 | tf_op jit(solution)/shard_map/ppermute | solution.py:400
  30.6 2.0 %collective-permute-start.10 = (bf16[4,40,768]{2,1,0:T(8,128)(2,1)S(1)}, bf16[4,40,768]{2,1,0:T(8,128)(2,1)S(1)}, u32[]{:S(2)}, u32[]{:S(2)}) collective-permute-start(bf16[4,40,768]{2,1,0:T(8,128)(2,1)S(1)} %pad_maximum_fusion.1.refs_2_), channel_id=1, source_target_pairs={{0,24},{8,0},{16,8},{24,16},{32,56},{40,32},{48,40},{56,48},{64,88... | collective-permute-start | bytes 737288 | tf_op jit(solution)/shard_map/ppermute | solution.py:400
  32.6 0.0 collective-permute-start.11
  32.6 2.5 %collective-permute-done.6.refs_3_ = bf16[4,40,768]{2,1,0:T(8,128)(2,1)S(1)} collective-permute-done((bf16[4,40,768]{2,1,0:T(8,128)(2,1)S(1)}, bf16[4,40,768]{2,1,0:T(8,128)(2,1)S(1)}, u32[]{:S(2)}, u32[]{:S(2)}) %collective-permute-start.6) | collective-permute-done | bytes 245792 | tf_op jit(solution)/shard_map/ppermute | solution.py:400
  35.2 0.0 collective-permute-start.9
  35.2 1.5 %collective-permute-done.7.refs_4_ = bf16[4,40,768]{2,1,0:T(8,128)(2,1)S(1)} collective-permute-done((bf16[4,40,768]{2,1,0:T(8,128)(2,1)S(1)}, bf16[4,40,768]{2,1,0:T(8,128)(2,1)S(1)}, u32[]{:S(2)}, u32[]{:S(2)}) %collective-permute-start.7) | collective-permute-done | bytes 245792 | tf_op jit(solution)/shard_map/ppermute | solution.py:400
  36.6 2.6 %collective-permute-done.8.refs_5_ = bf16[4,40,768]{2,1,0:T(8,128)(2,1)S(1)} collective-permute-done((bf16[4,40,768]{2,1,0:T(8,128)(2,1)S(1)}, bf16[4,40,768]{2,1,0:T(8,128)(2,1)S(1)}, u32[]{:S(2)}, u32[]{:S(2)}) %collective-permute-start.8) | collective-permute-done | bytes 245792 | tf_op jit(solution)/shard_map/ppermute | solution.py:400
  39.3 0.0 copy-done.1
  39.3 0.0 copy-done.6
  39.3 4.1 %legendre0.1 = bf16[8,40,768]{2,1,0:T(8,128)(2,1)} custom-call(s32[640]{0:T(1024)S(1)} %copy-done.4, s32[16]{0:T(128)S(1)} %copy-done.6, bf16[4,40,768]{2,1,0:T(8,128)(2,1)S(1)} %pad_maximum_fusion.refs_2_, bf16[4,40,768]{2,1,0:T(8,128)(2,1)S(1)} %collective-permute-done.6.refs_3_, bf16[4,40,768]{2,1,0:T(8,128)(2,1)S(1)} %collective-permute-done.7.refs_4_, ...), custom_call_target="tpu_custom_call" | custom-call | flops 400000000 | bytes 8000000 | tf_op jit(solution)/shard_map/legendre0/pallas_call | solution.py:410
  43.4 0.0 copy-start.9
  43.4 0.0 collective-permute-done.10.refs_4_
  43.4 0.0 collective-permute-done.11.refs_5_
  43.4 0.3 collective-permute-done.9.refs_3_
  43.7 4.5 %all-to-all-start = ((bf16[8,40,768]{2,1,0:T(8,128)(2,1)}), bf16[8,40,768]{2,1,0:T(8,128)(2,1)S(1)}, u32[]{:S(2)}, u32[]{:S(2)}) async-start(bf16[8,40,768]{2,1,0:T(8,128)(2,1)} %legendre0.1), calls=%async_computation | async-start | bytes 983040 | tf_op jit(solution)/shard_map/all_to_all | solution.py:428
  48.2 0.0 copy-done.5
  48.2 0.0 copy-start
  48.2 2.4 %copy-done = bf16[20,160,768]{2,1,0:T(8,128)(2,1)S(1)} copy-done((bf16[20,160,768]{2,1,0:T(8,128)(2,1)S(1)}, bf16[20,160,768]{2,1,0:T(8,128)(2,1)}, u32[]{:S(2)}) %copy-start) | copy-done | bytes 4915224
  50.6 0.0 copy-start.2
  50.6 0.0 copy-start.3
  50.6 4.1 %legendre1.1 = bf16[8,40,768]{2,1,0:T(8,128)(2,1)} custom-call(s32[640]{0:T(1024)S(1)} %copy-done.5, s32[16]{0:T(128)S(1)} %copy-done.6, bf16[4,40,768]{2,1,0:T(8,128)(2,1)S(1)} %pad_maximum_fusion.1.refs_2_, bf16[4,40,768]{2,1,0:T(8,128)(2,1)S(1)} %collective-permute-done.9.refs_3_, bf16[4,40,768]{2,1,0:T(8,128)(2,1)S(1)} %collective-permute-done.10.refs_4_, ...), custom_call_target="tpu_custom_call" | custom-call | flops 400000000 | bytes 8000000 | tf_op jit(solution)/shard_map/legendre1/pallas_call | solution.py:410
  54.8 3.4 %all-to-all-done = bf16[8,40,768]{2,1,0:T(8,128)(2,1)S(1)} async-done(((bf16[8,40,768]{2,1,0:T(8,128)(2,1)}), bf16[8,40,768]{2,1,0:T(8,128)(2,1)S(1)}, u32[]{:S(2)}, u32[]{:S(2)}) %all-to-all-start) | async-done | bytes 491552 | tf_op jit(solution)/shard_map/all_to_all | solution.py:428
  58.2 3.5 %all-to-all-start.1 = ((bf16[8,40,768]{2,1,0:T(8,128)(2,1)}), bf16[8,40,768]{2,1,0:T(8,128)(2,1)S(1)}, u32[]{:S(2)}, u32[]{:S(2)}) async-start(bf16[8,40,768]{2,1,0:T(8,128)(2,1)} %legendre1.1), calls=%async_computation.1 | async-start | bytes 983040 | tf_op jit(solution)/shard_map/all_to_all | solution.py:428
  61.7 0.0 copy-done.9
  61.7 0.1 reshape.12
  61.8 0.1 reshape.13.order_ref
  61.9 9.7 %all-to-all-done.1 = bf16[8,40,768]{2,1,0:T(8,128)(2,1)S(1)} async-done(((bf16[8,40,768]{2,1,0:T(8,128)(2,1)}), bf16[8,40,768]{2,1,0:T(8,128)(2,1)S(1)}, u32[]{:S(2)}, u32[]{:S(2)}) %all-to-all-start.1) | async-done | bytes 491552 | tf_op jit(solution)/shard_map/all_to_all | solution.py:428
  71.6 0.7 edges.1
  72.3 6.6 %collective-permute-start.12 = (bf16[64,640]{1,0:T(8,128)(2,1)S(1)}, bf16[64,640]{1,0:T(8,128)(2,1)S(1)}, u32[]{:S(2)}, u32[]{:S(2)}) collective-permute-start(bf16[64,640]{1,0:T(8,128)(2,1)S(1)} %get-tuple-element.47), channel_id=1, source_target_pairs={{8,0},{16,8},{24,16},{32,24},{40,32},{48,40},{56,48},{64,56},{72,6... | collective-permute-start | bytes 245768 | tf_op jit(solution)/shard_map/ppermute | solution.py:443
  78.9 1.9 %collective-permute-start.13 = (bf16[64,640]{1,0:T(8,128)(2,1)S(1)}, bf16[64,640]{1,0:T(8,128)(2,1)S(1)}, u32[]{:S(2)}, u32[]{:S(2)}) collective-permute-start(bf16[64,640]{1,0:T(8,128)(2,1)S(1)} %get-tuple-element.48), channel_id=1, source_target_pairs={{0,8},{8,16},{16,24},{24,32},{32,40},{40,48},{48,56},{56,64},{64,7... | collective-permute-start | bytes 245768 | tf_op jit(solution)/shard_map/ppermute | solution.py:444
  80.9 1.0 %order.1.main_ref = bf16[512,640]{1,0:T(8,128)(2,1)S(1)} custom-call(bf16[640,640]{1,0:T(8,128)(2,1)S(1)} %get-tuple-element.45.chosen_ref, bf16[320,768]{1,0:T(8,128)(2,1)S(1)} %bitcast.12, bf16[320,768]{1,0:T(8,128)(2,1)S(1)} %bitcast.14), custom_call_target="tpu_custom_call" | custom-call | flops 800000000 | bytes 4000000 | tf_op jit(solution)/shard_map/order/pallas_call | solution.py:445
  81.8 0.0 collective-permute-done.12.above_ref
  81.8 5.5 %collective-permute-done.13.below_ref = bf16[64,640]{1,0:T(8,128)(2,1)S(1)} collective-permute-done((bf16[64,640]{1,0:T(8,128)(2,1)S(1)}, bf16[64,640]{1,0:T(8,128)(2,1)S(1)}, u32[]{:S(2)}, u32[]{:S(2)}) %collective-permute-start.13) | collective-permute-done | bytes 81952 | tf_op jit(solution)/shard_map/ppermute | solution.py:444
  87.4 0.0 copy-done.2
  87.4 0.0 copy-done.3
  87.4 8.2 %synthesis.1 = bf16[2,160,5120]{2,1,0:T(8,128)(2,1)} custom-call(bf16[512,640]{1,0:T(8,128)(2,1)S(1)} %order.1.main_ref, bf16[128,640]{1,0:T(8,128)(2,1)S(1)} %get-tuple-element.46.rest_ref, bf16[64,640]{1,0:T(8,128)(2,1)S(1)} %collective-permute-done.12.above_ref, bf16[64,640]{1,0:T(8,128)(2,1)S(1)} %collective-permute-done.13.below_ref, ...), custom_call_target="tpu_custom_call" | custom-call | flops 2400000000 | bytes 11000000 | tf_op jit(solution)/shard_map/synthesis/pallas_call | solution.py:456
  (3 shorter events, 0.1 us)
Async XLA Ops:
  5.3 15.9 %collective-permute-start.3 = (bf16[40,768]{1,0:T(8,128)(2,1)}, bf16[40,768]{1,0:T(8,128)(2,1)S(1)}, u32[]{:S(2)}, u32[]{:S(2)}) collective-permute-start(bf16[40,768]{1,0:T(8,128)(2,1)} %get-tuple-element.30), channel_id=1, source_target_pairs={{0,32},{8,40},{16,48},{24,56},{32,64},{40,72},{48,80},{56,88},{64,... | collective-permute-start | bytes 184328 | tf_op jit(solution)/shard_map/ppermute | solution.py:400
  6.9 16.3 %collective-permute-start.4 = (bf16[40,768]{1,0:T(8,128)(2,1)}, bf16[40,768]{1,0:T(8,128)(2,1)S(1)}, u32[]{:S(2)}, u32[]{:S(2)}) collective-permute-start(bf16[40,768]{1,0:T(8,128)(2,1)} %get-tuple-element.30), channel_id=1, source_target_pairs={{0,96},{8,104},{16,112},{24,120},{32,0},{40,8},{48,16},{56,24},{64... | collective-permute-start | bytes 184328 | tf_op jit(solution)/shard_map/ppermute | solution.py:400
  7.4 15.7 %collective-permute-start.5 = (bf16[40,768]{1,0:T(8,128)(2,1)}, bf16[40,768]{1,0:T(8,128)(2,1)S(1)}, u32[]{:S(2)}, u32[]{:S(2)}) collective-permute-start(bf16[40,768]{1,0:T(8,128)(2,1)} %get-tuple-element.30), channel_id=1, source_target_pairs={{0,64},{8,72},{16,80},{24,88},{32,96},{40,104},{48,112},{56,120},{... | collective-permute-start | bytes 184328 | tf_op jit(solution)/shard_map/ppermute | solution.py:400
  9.5 13.7 %collective-permute-start = (bf16[40,768]{1,0:T(8,128)(2,1)}, bf16[40,768]{1,0:T(8,128)(2,1)S(1)}, u32[]{:S(2)}, u32[]{:S(2)}) collective-permute-start(bf16[40,768]{1,0:T(8,128)(2,1)} %get-tuple-element.29), channel_id=1, source_target_pairs={{0,8},{8,16},{16,24},{24,0},{32,40},{40,48},{48,56},{56,32},{64,72... | collective-permute-start | bytes 184328 | tf_op jit(solution)/shard_map/ppermute | solution.py:400
  11.4 11.8 %collective-permute-start.1 = (bf16[40,768]{1,0:T(8,128)(2,1)}, bf16[40,768]{1,0:T(8,128)(2,1)S(1)}, u32[]{:S(2)}, u32[]{:S(2)}) collective-permute-start(bf16[40,768]{1,0:T(8,128)(2,1)} %get-tuple-element.29), channel_id=1, source_target_pairs={{0,24},{8,0},{16,8},{24,16},{32,56},{40,32},{48,40},{56,48},{64,88... | collective-permute-start | bytes 184328 | tf_op jit(solution)/shard_map/ppermute | solution.py:400
  13.6 0.7 copy-start.4
  14.2 6.9 %copy-start.7 = (bf16[40,768]{1,0:T(8,128)(2,1)S(1)}, bf16[40,768]{1,0:T(8,128)(2,1)}, u32[]{:S(2)}) copy-start(bf16[40,768]{1,0:T(8,128)(2,1)} %get-tuple-element.29) | copy-start | bytes 184324
  14.2 8.9 %copy-start.8 = (bf16[40,768]{1,0:T(8,128)(2,1)S(1)}, bf16[40,768]{1,0:T(8,128)(2,1)}, u32[]{:S(2)}) copy-start(bf16[40,768]{1,0:T(8,128)(2,1)} %get-tuple-element.30) | copy-start | bytes 184324
  14.2 25.0 %copy-start.1 = (bf16[160,256]{1,0:T(8,128)(2,1)S(1)}, bf16[160,256]{1,0:T(8,128)(2,1)}, u32[]{:S(2)}) copy-start(bf16[160,256]{1,0:T(8,128)(2,1)} %get-tuple-element.35.refs_7_) | copy-start | bytes 245764
  14.2 25.0 %copy-start.6 = (s32[16]{0:T(128)S(1)}, s32[16]{0:T(128)}, u32[]{:S(2)}) copy-start(s32[16]{0:T(128)} %get-tuple-element.28.refs_1_) | copy-start | bytes 196
  21.2 27.1 %copy-start.5 = (s32[640]{0:T(1024)S(1)}, s32[640]{0:T(1024)}, u32[]{:S(2)}) copy-start(s32[640]{0:T(1024)} %get-tuple-element.27.order_ref.refs_0_) | copy-start | bytes 7684
  21.2 5.8 %collective-permute-start.2 = (bf16[40,768]{1,0:T(8,128)(2,1)S(1)}, bf16[40,768]{1,0:T(8,128)(2,1)S(1)}, u32[]{:S(2)}, u32[]{:S(2)}) collective-permute-start(bf16[40,768]{1,0:T(8,128)(2,1)S(1)} %copy-done.7), channel_id=1, source_target_pairs={{0,16},{8,24},{16,0},{24,8},{32,48},{40,56},{48,32},{56,40},{64,80... | collective-permute-start | bytes 184328 | tf_op jit(solution)/shard_map/ppermute | solution.py:400
  27.0 8.1 %collective-permute-start.6 = (bf16[4,40,768]{2,1,0:T(8,128)(2,1)S(1)}, bf16[4,40,768]{2,1,0:T(8,128)(2,1)S(1)}, u32[]{:S(2)}, u32[]{:S(2)}) collective-permute-start(bf16[4,40,768]{2,1,0:T(8,128)(2,1)S(1)} %pad_maximum_fusion.refs_2_), channel_id=1, source_target_pairs={{0,32},{8,40},{16,48},{24,56},{32,64},{40,72},{48,80},{56,88},{64,... | collective-permute-start | bytes 737288 | tf_op jit(solution)/shard_map/ppermute | solution.py:400
  28.2 8.5 %collective-permute-start.7 = (bf16[4,40,768]{2,1,0:T(8,128)(2,1)S(1)}, bf16[4,40,768]{2,1,0:T(8,128)(2,1)S(1)}, u32[]{:S(2)}, u32[]{:S(2)}) collective-permute-start(bf16[4,40,768]{2,1,0:T(8,128)(2,1)S(1)} %pad_maximum_fusion.refs_2_), channel_id=1, source_target_pairs={{0,96},{8,104},{16,112},{24,120},{32,0},{40,8},{48,16},{56,24},{64... | collective-permute-start | bytes 737288 | tf_op jit(solution)/shard_map/ppermute | solution.py:400
  29.1 10.1 %collective-permute-start.8 = (bf16[4,40,768]{2,1,0:T(8,128)(2,1)S(1)}, bf16[4,40,768]{2,1,0:T(8,128)(2,1)S(1)}, u32[]{:S(2)}, u32[]{:S(2)}) collective-permute-start(bf16[4,40,768]{2,1,0:T(8,128)(2,1)S(1)} %pad_maximum_fusion.refs_2_), channel_id=1, source_target_pairs={{0,64},{8,72},{16,80},{24,88},{32,96},{40,104},{48,112},{56,120},{... | collective-permute-start | bytes 737288 | tf_op jit(solution)/shard_map/ppermute | solution.py:400
  30.6 12.8 %collective-permute-start.10 = (bf16[4,40,768]{2,1,0:T(8,128)(2,1)S(1)}, bf16[4,40,768]{2,1,0:T(8,128)(2,1)S(1)}, u32[]{:S(2)}, u32[]{:S(2)}) collective-permute-start(bf16[4,40,768]{2,1,0:T(8,128)(2,1)S(1)} %pad_maximum_fusion.1.refs_2_), channel_id=1, source_target_pairs={{0,24},{8,0},{16,8},{24,16},{32,56},{40,32},{48,40},{56,48},{64,88... | collective-permute-start | bytes 737288 | tf_op jit(solution)/shard_map/ppermute | solution.py:400
  32.6 10.8 %collective-permute-start.11 = (bf16[4,40,768]{2,1,0:T(8,128)(2,1)S(1)}, bf16[4,40,768]{2,1,0:T(8,128)(2,1)S(1)}, u32[]{:S(2)}, u32[]{:S(2)}) collective-permute-start(bf16[4,40,768]{2,1,0:T(8,128)(2,1)S(1)} %pad_maximum_fusion.1.refs_2_), channel_id=1, source_target_pairs={{0,16},{8,24},{16,0},{24,8},{32,48},{40,56},{48,32},{56,40},{64,80... | collective-permute-start | bytes 737288 | tf_op jit(solution)/shard_map/ppermute | solution.py:400
  35.2 8.6 %collective-permute-start.9 = (bf16[4,40,768]{2,1,0:T(8,128)(2,1)S(1)}, bf16[4,40,768]{2,1,0:T(8,128)(2,1)S(1)}, u32[]{:S(2)}, u32[]{:S(2)}) collective-permute-start(bf16[4,40,768]{2,1,0:T(8,128)(2,1)S(1)} %pad_maximum_fusion.1.refs_2_), channel_id=1, source_target_pairs={{0,8},{8,16},{16,24},{24,0},{32,40},{40,48},{48,56},{56,32},{64,72... | collective-permute-start | bytes 737288 | tf_op jit(solution)/shard_map/ppermute | solution.py:400
  43.4 18.3 %copy-start.9 = (s32[640]{0:T(1024)S(1)}, s32[640]{0:T(1024)}, u32[]{:S(2)}) copy-start(s32[640]{0:T(1024)} %order_any.1) | copy-start | bytes 7684
  43.7 14.5 %all-to-all-start = ((bf16[8,40,768]{2,1,0:T(8,128)(2,1)}), bf16[8,40,768]{2,1,0:T(8,128)(2,1)S(1)}, u32[]{:S(2)}, u32[]{:S(2)}) async-start(bf16[8,40,768]{2,1,0:T(8,128)(2,1)} %legendre0.1), calls=%async_computation | async-start | bytes 983040 | tf_op jit(solution)/shard_map/all_to_all | solution.py:428
  48.2 2.4 %copy-start = (bf16[20,160,768]{2,1,0:T(8,128)(2,1)S(1)}, bf16[20,160,768]{2,1,0:T(8,128)(2,1)}, u32[]{:S(2)}) copy-start(bf16[20,160,768]{2,1,0:T(8,128)(2,1)} %get-tuple-element.41.refs_6_) | copy-start | bytes 14745604
  50.6 36.7 %copy-start.2 = (bf16[640,128]{1,0:T(8,128)(2,1)S(1)}, bf16[640,128]{1,0:T(8,128)(2,1)}, u32[]{:S(2)}) copy-start(bf16[640,128]{1,0:T(8,128)(2,1)} %constant.10.clone.middle_ref) | copy-start | bytes 491524
  50.6 36.7 %copy-start.3 = (bf16[160,32]{1,0:T(8,128)(2,1)S(1)}, bf16[160,32]{1,0:T(8,128)(2,1)}, u32[]{:S(2)}) copy-start(bf16[160,32]{1,0:T(8,128)(2,1)} %constant.9.clone.expand_ref) | copy-start | bytes 30724
  58.2 13.4 %all-to-all-start.1 = ((bf16[8,40,768]{2,1,0:T(8,128)(2,1)}), bf16[8,40,768]{2,1,0:T(8,128)(2,1)S(1)}, u32[]{:S(2)}, u32[]{:S(2)}) async-start(bf16[8,40,768]{2,1,0:T(8,128)(2,1)} %legendre1.1), calls=%async_computation.1 | async-start | bytes 983040 | tf_op jit(solution)/shard_map/all_to_all | solution.py:428
  72.3 9.5 %collective-permute-start.12 = (bf16[64,640]{1,0:T(8,128)(2,1)S(1)}, bf16[64,640]{1,0:T(8,128)(2,1)S(1)}, u32[]{:S(2)}, u32[]{:S(2)}) collective-permute-start(bf16[64,640]{1,0:T(8,128)(2,1)S(1)} %get-tuple-element.47), channel_id=1, source_target_pairs={{8,0},{16,8},{24,16},{32,24},{40,32},{48,40},{56,48},{64,56},{72,6... | collective-permute-start | bytes 245768 | tf_op jit(solution)/shard_map/ppermute | solution.py:443
  78.9 8.4 %collective-permute-start.13 = (bf16[64,640]{1,0:T(8,128)(2,1)S(1)}, bf16[64,640]{1,0:T(8,128)(2,1)S(1)}, u32[]{:S(2)}, u32[]{:S(2)}) collective-permute-start(bf16[64,640]{1,0:T(8,128)(2,1)S(1)} %get-tuple-element.48), channel_id=1, source_target_pairs={{0,8},{8,16},{16,24},{24,32},{32,40},{40,48},{48,56},{56,64},{64,7... | collective-permute-start | bytes 245768 | tf_op jit(solution)/shard_map/ppermute | solution.py:444

commit v4 on v3

--- a/solution.py
+++ b/solution.py
@@ -30,8 +30,8 @@
 STEPS = NLON // 2 // TILE
 GROUP = 4
 SMALL_BYTES = 16 * 2**20
-FETCH_BYTES = int(45.5 * 2**20)
-LARGE_BYTES = int(50 * 2**20)
+FETCH_BYTES = 44 * 2**20
+LARGE_BYTES = 50 * 2**20
 
 LIFT_ALPHA = -1.586134342059924
 LIFT_BETA = -0.052980118572961
@@ -100,82 +100,61 @@
     )
 
 
-def pack_kernel(order_ref, spectra_ref, order_any, writer_any, matrix_any, *refs):
-    outs, (order_out, writer_out, matrix_out) = refs[:HALVES], refs[HALVES : HALVES + 3]
-    wide, low, high, packed, sems = refs[HALVES + 3 :]
-    band = lax.axis_index("lat")
-    variant = jnp.where(band == 0, 0, jnp.where(band == BANDS - 1, 2, 1))
-    copies = [
-        pltpu.make_async_copy(order_any, order_out, sems.at[0]),
-        pltpu.make_async_copy(writer_any, writer_out, sems.at[1]),
-        pltpu.make_async_copy(matrix_any.at[variant], matrix_out, sems.at[2]),
-    ]
-    for copy in copies:
-        copy.start()
+def pack_kernel(order_ref, spectra_ref, *refs):
+    outs, (wide, low, high, packed) = refs[:HALVES], refs[HALVES:]
     first = lax.axis_index("wave") * SLOTS
     for pair in range(PAIRS):
         low[pl.ds(pair, 1), :] = jnp.full((1, LANE), order_ref[first + 2 * pair], jnp.int32)
         high[pl.ds(pair, 1), :] = jnp.full((1, LANE), order_ref[first + 2 * pair + 1], jnp.int32)
     waves_a, waves_b = low[...], high[...]
     lane = lax.broadcasted_iota(jnp.int32, (PAIRS, LANE), 1)
-    zero = jnp.zeros((PAIRS, LANE), jnp.float32)
     for part in range(2):
-        firsts, seconds = [], []
         for block in range(5):
             wide[block] = spectra_ref[0, part, :, block * LANE : (block + 1) * LANE].astype(jnp.float32)
-            values = wide[block, pl.ds(0, PAIRS, stride=2), :]
-            firsts.append(jnp.where(lane + block * LANE >= waves_a, values, zero))
-            values = wide[block, pl.ds(1, PAIRS, stride=2), :]
-            seconds.append(jnp.where(lane + block * LANE >= waves_b, values, zero))
         for block in range(BLOCKS):
-            taken = firsts[block - 1] if block else zero
-            for cut in range(block, 5):
-                inside = (waves_a >= cut * LANE) & (waves_a < (cut + 1) * LANE)
-                taken = jnp.where(inside, seconds[4 - cut + block], taken)
+            taken = jnp.zeros((PAIRS, LANE), jnp.float32)
+            if block <= 4:
+                values = wide[4 - block, pl.ds(1, PAIRS, stride=2), :]
+                taken = jnp.where(lane + (4 - block) * LANE >= waves_b, values, taken)
+            if block >= 1:
+                values = wide[block - 1, pl.ds(0, PAIRS, stride=2), :]
+                values = jnp.where(lane + (block - 1) * LANE >= waves_a, values, jnp.zeros_like(values))
+                taken = jnp.where(waves_a < block * LANE, values, taken)
             for half in range(HALVES):
                 packed[half, pl.ds(part * PART_PAIRS, PART_PAIRS), block * LANE : (block + 1) * LANE] = taken[
                     half * PART_PAIRS : (half + 1) * PART_PAIRS
                 ]
     for half in range(HALVES):
         outs[half][...] = packed[half].astype(jnp.bfloat16)
+
+
+def fetch_kernel(order_ref, writer_ref, matrix_ref, legendre_ref, order_out, writer_out, matrix_out, held_out, sems):
+    band = lax.axis_index("lat")
+    variant = jnp.where(band == 0, 0, jnp.where(band == BANDS - 1, 2, 1))
+    copies = [
+        pltpu.make_async_copy(legendre_ref.at[pl.ds(0, PART_SLOTS)], held_out, sems.at[0]),
+        pltpu.make_async_copy(order_ref, order_out, sems.at[1]),
+        pltpu.make_async_copy(writer_ref, writer_out, sems.at[2]),
+        pltpu.make_async_copy(matrix_ref.at[variant], matrix_out, sems.at[3]),
+    ]
+    for copy in copies:
+        copy.start()
     for copy in copies:
         copy.wait()
 
 
-def fetch_kernel(order_ref, legendre_ref, *refs):
-    outs, sems = refs[:HALVES], refs[HALVES]
-    first = lax.axis_index("wave") * SLOTS
-    for half in range(HALVES):
-
-        def fetch(member, carry, half=half):
-            pair = half * PART_PAIRS + member
-            block = order_ref[first + 2 * pair] // LANE
-            for cut in range(5):
-
-                @pl.when(block == cut)
-                def _():
-                    pltpu.make_async_copy(
-                        legendre_ref.at[2 * pair + 1, :, pl.ds((4 - cut) * LANE, (cut + 1) * LANE)],
-                        outs[half].at[member, :, pl.ds(0, (cut + 1) * LANE)],
-                        sems.at[half],
-                    ).start()
-                    pltpu.make_async_copy(
-                        legendre_ref.at[2 * pair, :, pl.ds(cut * LANE, (5 - cut) * LANE)],
-                        outs[half].at[member, :, pl.ds((cut + 1) * LANE, (5 - cut) * LANE)],
-                        sems.at[half],
-                    ).start()
-
-            return carry
-
-        lax.fori_loop(0, PART_PAIRS, fetch, 0)
-    for half in range(HALVES):
-        pltpu.make_async_copy(outs[half], outs[half], sems.at[half]).wait()
-
-
 def legendre_kernel(half, order_ref, writer_ref, *refs):
     parts = refs[:4]
-    held, matrix, out_ref = refs[4:7]
-    spread, rows, results = refs[7:]
+    legendre_ref, matrix, out_ref = refs[4:7]
+    spread, rows, results = refs[7:10]
+    held, copies = legendre_ref, []
+    if half:
+        held, sems = refs[10:]
+        for index in range(2):
+            some = PART_SLOTS // 2
+            source = legendre_ref.at[pl.ds(half * PART_SLOTS + index * some, some)]
+            copies.append(pltpu.make_async_copy(source, held.at[pl.ds(index * some, some)], sems.at[index]))
+            copies[-1].start()
     base = half * PART_PAIRS
     first = lax.axis_index("wave") * SLOTS + 2 * base
     band = lax.axis_index("lat")
@@ -194,17 +173,20 @@
         for member in range(GROUP):
             pair = group * GROUP + member
             wave = order_ref[first + 2 * pair]
-            lower, upper = [], []
+            lower, upper, values_of_n = [], [], []
             for block in range(BLOCKS):
                 values = spread[block, pl.ds(pair, 2 * FIELDS, stride=PART_PAIRS), :].astype(jnp.bfloat16)
                 from_a = wave < block * LANE
+                slot = 2 * pair + jnp.where(from_a, 0, 1)
+                source = pl.multiple_of(jnp.where(from_a, block - 1, 4 - block) * LANE, LANE)
+                values_of_n.append(held[slot, :, pl.ds(source, LANE)])
                 lower.append(jnp.where(from_a, values, jnp.zeros_like(values)))
                 upper.append(jnp.where(from_a, jnp.zeros_like(values), values))
             left = jnp.concatenate(
                 [jnp.concatenate(lower, axis=1), jnp.concatenate(upper, axis=1)], axis=0
             )
             sums = lax.dot_general(
-                left, held[pair], (((1,), (1,)), ((), ())), preferred_element_type=jnp.float32
+                left, jnp.concatenate(values_of_n, axis=1), (((1,), (1,)), ((), ())), preferred_element_type=jnp.float32
             )
             for which in range(2):
                 piece = sums[which * 2 * FIELDS : (which + 1) * 2 * FIELDS]
@@ -213,6 +195,8 @@
                 rows[1, where, : BAND - LANE] = piece[:, LANE:]
         return carry
 
+    for copy in copies:
+        copy.wait()
     lax.fori_loop(0, PART_PAIRS // GROUP, contract, 0)
 
     chunk = 2 * FIELDS * PART_SLOTS // 4
@@ -362,36 +346,20 @@
 
 def make_on_device(table, middle, matrices, expand):
     def on_device(spectra, legendre, wave_order, writer_order):
-        *halves, orders, writers, matrix = pl.pallas_call(
+        halves = pl.pallas_call(
             pack_kernel,
-            out_shape=[bf16(2 * PART_PAIRS, BLOCKS * LANE)] * HALVES
-            + [
-                jax.ShapeDtypeStruct((NWAVE,), jnp.int32),
-                jax.ShapeDtypeStruct((FIELDS,), jnp.int32),
-                bf16(BAND, 2 * LANE),
-            ],
-            in_specs=[SMEM, VMEM, ANY, ANY, ANY],
-            out_specs=[VMEM] * HALVES + [ANY] * 3,
+            out_shape=[bf16(2 * PART_PAIRS, BLOCKS * LANE)] * HALVES,
+            in_specs=[SMEM, VMEM],
+            out_specs=[VMEM] * HALVES,
             scratch_shapes=[
                 pltpu.VMEM((5, SLOTS, LANE), jnp.float32),
                 pltpu.VMEM((PAIRS, LANE), jnp.int32),
                 pltpu.VMEM((PAIRS, LANE), jnp.int32),
                 pltpu.VMEM((HALVES, 2 * PART_PAIRS, BLOCKS * LANE), jnp.float32),
-                pltpu.SemaphoreType.DMA((3,)),
             ],
             name="pack",
-        )(wave_order, spectra, wave_order, writer_order, matrices)
+        )(wave_order, spectra)
         order = wave_order.reshape(OWNERS, HALVES, PART_SLOTS).swapaxes(0, 1).reshape(1, NWAVE)
-        held = pl.pallas_call(
-            fetch_kernel,
-            out_shape=[bf16(PART_PAIRS, BAND, BLOCKS * LANE)] * HALVES,
-            in_specs=[SMEM, ANY],
-            out_specs=[VMEM] * HALVES,
-            scratch_shapes=[pltpu.SemaphoreType.DMA((HALVES,))],
-            compiler_params=FETCH,
-            cost_estimate=pl.CostEstimate(flops=0, bytes_accessed=14_000_000, transcendentals=0),
-            name="fetch",
-        )(orders, legendre)
 
         axes = ((along_z, along_x), (along_x, along_z))
         gathered = halves
@@ -400,27 +368,43 @@
                 [values] + [lax.ppermute(values, "lat", axes[half][stage](step)) for step in (1, 3, 2)]
                 for half, values in enumerate(gathered)
             ]
+            gathered = arrived
             if stage == 0:
-                gathered, held = lax.optimization_barrier(([jnp.stack(blocks) for blocks in arrived], held))
-            else:
-                gathered = arrived
+                gathered, legendre = lax.optimization_barrier(([jnp.stack(blocks) for blocks in arrived], legendre))
+
+        orders, writers, matrix, held = pl.pallas_call(
+            fetch_kernel,
+            out_shape=[
+                jax.ShapeDtypeStruct((NWAVE,), jnp.int32),
+                jax.ShapeDtypeStruct((FIELDS,), jnp.int32),
+                bf16(BAND, 2 * LANE),
+                bf16(PART_SLOTS, BAND, NWAVE),
+            ],
+            in_specs=[ANY] * 4,
+            out_specs=[ANY] * 3 + [VMEM],
+            scratch_shapes=[pltpu.SemaphoreType.DMA((4,))],
+            compiler_params=FETCH,
+            cost_estimate=pl.CostEstimate(flops=0, bytes_accessed=14_000_000, transcendentals=0),
+            name="fetch",
+        )(wave_order, writer_order, matrices, legendre)
 
         waves = []
         for half in range(HALVES):
             lifted = pl.pallas_call(
                 lambda *refs, half=half: legendre_kernel(half, *refs),
                 out_shape=bf16(OWNERS, PART_SLOTS, WIDTH),
-                in_specs=[SMEM, SMEM] + [VMEM] * 6,
+                in_specs=[SMEM, SMEM] + [VMEM] * 4 + [ANY if half else VMEM, VMEM],
                 out_specs=VMEM,
                 scratch_shapes=[
                     pltpu.VMEM((BLOCKS, 2 * FIELDS * PART_PAIRS, LANE), jnp.float32),
                     pltpu.VMEM((2, 2 * FIELDS * PART_SLOTS, LANE), jnp.float32),
                     pltpu.VMEM((2, 2 * FIELDS * PART_SLOTS, LANE), jnp.float32),
-                ],
-                compiler_params=SMALL,
+                ]
+                + [pltpu.VMEM((PART_SLOTS, BAND, NWAVE), jnp.bfloat16), pltpu.SemaphoreType.DMA((2,))] * half,
+                compiler_params=FETCH if half else SMALL,
                 cost_estimate=pl.CostEstimate(flops=400_000_000, bytes_accessed=8_000_000, transcendentals=0),
                 name=f"legendre{half}",
-            )(orders, writers, *gathered[half], held[half], matrix)
+            )(orders, writers, *gathered[half], legendre if half else held, matrix)
             if half + 1 < HALVES:
                 lifted, gathered[half + 1] = lax.optimization_barrier((lifted, gathered[half + 1]))
             if waves:

time: 96 us -> 91 us (0.948)
  waiting for transfers between devices: 29.5 us -> 24 us
  Pallas kernels: 30.3 us -> 26.4 us
  starting transfers between devices: 32.3 us -> 35.7 us
  other arithmetic: 0.07 us -> 1.72 us
    ppermute x12, waiting for transfers between devices: 10.8 us -> 6.16 us  [on_device(): lax.ppermute(values, 'lat', axes[half][stage](step))]
    pallas_call x1, Pallas kernels: 5.29 us -> 1.7 us  [on_device(): pl.pallas_call(pack_kernel, out_shape=[bf16(2 * PART_PAIRS, BLOCKS * LANE...]
    pallas_call x1, Pallas kernels: 6.9 us -> 3.37 us  [on_device(): pl.pallas_call(fetch_kernel, out_shape=[jax.ShapeDtypeStruct((NWAVE,), jn...]
    ppermute x1, starting transfers between devices: 6.63 us -> 10.2 us  [on_device(): above = lax.ppermute(above, 'lat', neighbour(-1))]
    pallas_call x2, Pallas kernels: 8.29 us -> 11.5 us  [on_device(): pl.pallas_call(lambda *refs, half=half: legendre_kernel(half, *refs), out...]
    another operation x2, other arithmetic: 0.07 us -> 1.72 us  [on_device(): jnp.stack(blocks)]
    unnamed x20 -> x12, local copies, waits for them, and re-layouts: 3.1 us -> 2.3 us
  transfers between devices with their start and end apart: 16 -> 16, of which waited for: 8 -> 5; matrix products, arithmetic and copies ran while one was open for 0% -> 1% of each run, Pallas kernels for 17% -> 17%
where the time goes in v4:
time: 91 us; the launch traced here: 90.5 us
  starting transfers between devices  35.7 us (39%)
  Pallas kernels  26.4 us (29%)
  waiting for transfers between devices  24 us (26%)
  local copies, waits for them, and re-layouts  2.48 us (3%)
  other arithmetic  1.72 us (2%)
    ppermute x12, starting transfers between devices, on_device(): lax.ppermute(values, 'lat', axes[half][stage](step))  15.7 us
    all_to_all x2, waiting for transfers between devices, on_device(): lax.all_to_all(lifted, 'wave', split_axis=0, concat_axis=0, tiled=True)  12.3 us
    pallas_call x2, Pallas kernels, on_device(): pl.pallas_call(lambda *refs, half=half: legendre_kernel(half, *refs), out...  11.5 us
    ppermute x1, starting transfers between devices, on_device(): above = lax.ppermute(above, 'lat', neighbour(-1))  10.2 us
    pallas_call x1, Pallas kernels, on_device(): pl.pallas_call(synthesis_kernel, out_shape=bf16(2, BAND, NLON), in_specs=...  8.23 us
    all_to_all x2, starting transfers between devices, on_device(): lax.all_to_all(lifted, 'wave', split_axis=0, concat_axis=0, tiled=True)  7.97 us
    ppermute x12, waiting for transfers between devices, on_device(): lax.ppermute(values, 'lat', axes[half][stage](step))  6.16 us
    ppermute x1, waiting for transfers between devices, on_device(): below = lax.ppermute(below, 'lat', neighbour(1))  5.55 us
  transfers between devices with their start and end apart: 16, of which 5 were waited for; matrix products, arithmetic and copies ran while one was open for 1% of the time, Pallas kernels for 17%

profile of v4, /device:TPU:2, one launch (start us, length us, event | category | flops | bytes accessed | tf_op | source)
XLA Modules:
  0.0 90.5 jit_solution(12544307313845384371)
XLA Ops:
  0.0 1.7 %pack.1 = (bf16[40,768]{1,0:T(8,128)(2,1)}, bf16[40,768]{1,0:T(8,128)(2,1)}) custom-call(s32[640]{0:T(1024)} %order_ref.3, bf16[1,2,80,640]{3,2,1,0:T(8,128)(2,1)} %spectra_ref.1), custom_call_target="tpu_custom_call" | custom-call | tf_op jit(solution)/shard_map/pack/pallas_call | solution.py:349
  1.7 1.5 %collective-permute-start.3 = (bf16[40,768]{1,0:T(8,128)(2,1)}, bf16[40,768]{1,0:T(8,128)(2,1)S(1)}, u32[]{:S(2)}, u32[]{:S(2)}) collective-permute-start(bf16[40,768]{1,0:T(8,128)(2,1)} %get-tuple-element.26), channel_id=1, source_target_pairs={{0,32},{8,40},{16,48},{24,56},{32,64},{40,72},{48,80},{56,88},{64,... | collective-permute-start | bytes 184328 | tf_op jit(solution)/shard_map/ppermute | solution.py:368
  3.2 0.5 collective-permute-start.4
  3.7 2.1 %collective-permute-start.5 = (bf16[40,768]{1,0:T(8,128)(2,1)}, bf16[40,768]{1,0:T(8,128)(2,1)S(1)}, u32[]{:S(2)}, u32[]{:S(2)}) collective-permute-start(bf16[40,768]{1,0:T(8,128)(2,1)} %get-tuple-element.26), channel_id=1, source_target_pairs={{0,64},{8,72},{16,80},{24,88},{32,96},{40,104},{48,112},{56,120},{... | collective-permute-start | bytes 184328 | tf_op jit(solution)/shard_map/ppermute | solution.py:368
  5.9 1.9 %collective-permute-start = (bf16[40,768]{1,0:T(8,128)(2,1)}, bf16[40,768]{1,0:T(8,128)(2,1)S(1)}, u32[]{:S(2)}, u32[]{:S(2)}) collective-permute-start(bf16[40,768]{1,0:T(8,128)(2,1)} %get-tuple-element.25), channel_id=1, source_target_pairs={{0,8},{8,16},{16,24},{24,0},{32,40},{40,48},{48,56},{56,32},{64,72... | collective-permute-start | bytes 184328 | tf_op jit(solution)/shard_map/ppermute | solution.py:368
  7.8 2.1 %collective-permute-start.1 = (bf16[40,768]{1,0:T(8,128)(2,1)}, bf16[40,768]{1,0:T(8,128)(2,1)S(1)}, u32[]{:S(2)}, u32[]{:S(2)}) collective-permute-start(bf16[40,768]{1,0:T(8,128)(2,1)} %get-tuple-element.25), channel_id=1, source_target_pairs={{0,24},{8,0},{16,8},{24,16},{32,56},{40,32},{48,40},{56,48},{64,88... | collective-permute-start | bytes 184328 | tf_op jit(solution)/shard_map/ppermute | solution.py:368
  9.9 0.0 collective-permute-done.3
  9.9 1.9 %collective-permute-start.2 = (bf16[40,768]{1,0:T(8,128)(2,1)}, bf16[40,768]{1,0:T(8,128)(2,1)S(1)}, u32[]{:S(2)}, u32[]{:S(2)}) collective-permute-start(bf16[40,768]{1,0:T(8,128)(2,1)} %get-tuple-element.25), channel_id=1, source_target_pairs={{0,16},{8,24},{16,0},{24,8},{32,48},{40,56},{48,32},{56,40},{64,80... | collective-permute-start | bytes 184328 | tf_op jit(solution)/shard_map/ppermute | solution.py:368
  11.8 0.0 collective-permute-done.4
  11.8 0.0 collective-permute-done.5
  11.8 0.9 pad_maximum_fusion.1.refs_2_
  12.6 0.0 collective-permute-done
  12.6 0.0 collective-permute-done.1
  12.7 3.2 %collective-permute-done.2 = bf16[40,768]{1,0:T(8,128)(2,1)S(1)} collective-permute-done((bf16[40,768]{1,0:T(8,128)(2,1)}, bf16[40,768]{1,0:T(8,128)(2,1)S(1)}, u32[]{:S(2)}, u32[]{:S(2)}) %collective-permute-start.2) | collective-permute-done | bytes 61472 | tf_op jit(solution)/shard_map/ppermute | solution.py:368
  15.8 0.9 pad_maximum_fusion.refs_2_
  16.7 1.2 %collective-permute-start.6 = (bf16[4,40,768]{2,1,0:T(8,128)(2,1)S(1)}, bf16[4,40,768]{2,1,0:T(8,128)(2,1)S(1)}, u32[]{:S(2)}, u32[]{:S(2)}) collective-permute-start(bf16[4,40,768]{2,1,0:T(8,128)(2,1)S(1)} %pad_maximum_fusion.refs_2_), channel_id=1, source_target_pairs={{0,32},{8,40},{16,48},{24,56},{32,64},{40,72},{48,80},{56,88},{64,... | collective-permute-start | bytes 737288 | tf_op jit(solution)/shard_map/ppermute | solution.py:368
  17.9 0.9 %collective-permute-start.7 = (bf16[4,40,768]{2,1,0:T(8,128)(2,1)S(1)}, bf16[4,40,768]{2,1,0:T(8,128)(2,1)S(1)}, u32[]{:S(2)}, u32[]{:S(2)}) collective-permute-start(bf16[4,40,768]{2,1,0:T(8,128)(2,1)S(1)} %pad_maximum_fusion.refs_2_), channel_id=1, source_target_pairs={{0,96},{8,104},{16,112},{24,120},{32,0},{40,8},{48,16},{56,24},{64... | collective-permute-start | bytes 737288 | tf_op jit(solution)/shard_map/ppermute | solution.py:368
  18.8 1.5 %collective-permute-start.8 = (bf16[4,40,768]{2,1,0:T(8,128)(2,1)S(1)}, bf16[4,40,768]{2,1,0:T(8,128)(2,1)S(1)}, u32[]{:S(2)}, u32[]{:S(2)}) collective-permute-start(bf16[4,40,768]{2,1,0:T(8,128)(2,1)S(1)} %pad_maximum_fusion.refs_2_), channel_id=1, source_target_pairs={{0,64},{8,72},{16,80},{24,88},{32,96},{40,104},{48,112},{56,120},{... | collective-permute-start | bytes 737288 | tf_op jit(solution)/shard_map/ppermute | solution.py:368
  20.3 2.0 %collective-permute-start.10 = (bf16[4,40,768]{2,1,0:T(8,128)(2,1)S(1)}, bf16[4,40,768]{2,1,0:T(8,128)(2,1)S(1)}, u32[]{:S(2)}, u32[]{:S(2)}) collective-permute-start(bf16[4,40,768]{2,1,0:T(8,128)(2,1)S(1)} %pad_maximum_fusion.1.refs_2_), channel_id=1, source_target_pairs={{0,24},{8,0},{16,8},{24,16},{32,56},{40,32},{48,40},{56,48},{64,88... | collective-permute-start | bytes 737288 | tf_op jit(solution)/shard_map/ppermute | solution.py:368
  22.3 0.0 collective-permute-start.11
  22.3 3.0 %collective-permute-done.6.refs_3_ = bf16[4,40,768]{2,1,0:T(8,128)(2,1)S(1)} collective-permute-done((bf16[4,40,768]{2,1,0:T(8,128)(2,1)S(1)}, bf16[4,40,768]{2,1,0:T(8,128)(2,1)S(1)}, u32[]{:S(2)}, u32[]{:S(2)}) %collective-permute-start.6) | collective-permute-done | bytes 245792 | tf_op jit(solution)/shard_map/ppermute | solution.py:368
  25.3 0.0 collective-permute-start.9
  25.3 0.0 copy-start
  25.3 0.9 %copy-done = bf16[3,160,256]{2,1,0:T(8,128)(2,1)S(1)} copy-done((bf16[3,160,256]{2,1,0:T(8,128)(2,1)S(1)}, bf16[3,160,256]{2,1,0:T(8,128)(2,1)}, u32[]{:S(2)}) %copy-start) | copy-done | bytes 245784
  26.3 0.0 copy-start.3
  26.3 0.7 copy-done.3
  26.9 0.0 copy-start.5
  26.9 0.7 copy-done.5
  27.6 3.4 %fetch.1 = (s32[640]{0:T(1024)S(1)}, s32[16]{0:T(128)S(1)}, bf16[160,256]{1,0:T(8,128)(2,1)S(1)}, bf16[40,160,640]{2,1,0:T(8,128)(2,1)S(1)}) custom-call(s32[640]{0:T(1024)S(1)} %copy-done.3, s32[16]{0:T(128)S(1)} %copy-done.5, bf16[3,160,256]{2,1,0:T(8,128)(2,1)S(1)} %copy-done, bf16[80,160,640]{2,1,0:T(8,128)(2,1)} %refs_6_), custom_call_target="tpu_custom_call" | custom-call | bytes 14000000 | tf_op jit(solution)/shard_map/fetch/pallas_call | solution.py:375
  31.0 0.0 collective-permute-done.7.refs_4_
  31.0 0.0 collective-permute-done.8.refs_5_
  31.0 4.1 %legendre0.1 = bf16[8,40,768]{2,1,0:T(8,128)(2,1)} custom-call(s32[640]{0:T(1024)S(1)} %get-tuple-element.28.refs_0_, s32[16]{0:T(128)S(1)} %get-tuple-element.29.refs_1_, bf16[4,40,768]{2,1,0:T(8,128)(2,1)S(1)} %pad_maximum_fusion.refs_2_, bf16[4,40,768]{2,1,0:T(8,128)(2,1)S(1)} %collective-permute-done.6.refs_3_, ...), custom_call_target="tpu_custom_call" | custom-call | flops 400000000 | bytes 8000000 | tf_op jit(solution)/shard_map/legendre0/pallas_call | solution.py:393
  35.1 0.0 collective-permute-done.10.refs_4_
  35.1 0.0 collective-permute-done.11.refs_5_
  35.1 0.0 collective-permute-done.9.refs_3_
  35.1 4.5 %all-to-all-start = ((bf16[8,40,768]{2,1,0:T(8,128)(2,1)}), bf16[8,40,768]{2,1,0:T(8,128)(2,1)S(1)}, u32[]{:S(2)}, u32[]{:S(2)}) async-start(bf16[8,40,768]{2,1,0:T(8,128)(2,1)} %legendre0.1), calls=%async_computation | async-start | bytes 983040 | tf_op jit(solution)/shard_map/all_to_all | solution.py:412
  39.6 0.0 copy-start.4
  39.6 0.0 copy-start.1
  39.6 0.0 copy-start.2
  39.6 7.4 %legendre1.1 = bf16[8,40,768]{2,1,0:T(8,128)(2,1)} custom-call(s32[640]{0:T(1024)S(1)} %get-tuple-element.28.refs_0_, s32[16]{0:T(128)S(1)} %get-tuple-element.29.refs_1_, bf16[4,40,768]{2,1,0:T(8,128)(2,1)S(1)} %pad_maximum_fusion.1.refs_2_, bf16[4,40,768]{2,1,0:T(8,128)(2,1)S(1)} %collective-permute-done.9.refs_3_, ...), custom_call_target="tpu_custom_call" | custom-call | flops 400000000 | bytes 8000000 | tf_op jit(solution)/shard_map/legendre1/pallas_call | solution.py:393
  47.0 2.6 %all-to-all-done = bf16[8,40,768]{2,1,0:T(8,128)(2,1)S(1)} async-done(((bf16[8,40,768]{2,1,0:T(8,128)(2,1)}), bf16[8,40,768]{2,1,0:T(8,128)(2,1)S(1)}, u32[]{:S(2)}, u32[]{:S(2)}) %all-to-all-start) | async-done | bytes 491552 | tf_op jit(solution)/shard_map/all_to_all | solution.py:412
  49.6 3.5 %all-to-all-start.1 = ((bf16[8,40,768]{2,1,0:T(8,128)(2,1)}), bf16[8,40,768]{2,1,0:T(8,128)(2,1)S(1)}, u32[]{:S(2)}, u32[]{:S(2)}) async-start(bf16[8,40,768]{2,1,0:T(8,128)(2,1)} %legendre1.1), calls=%async_computation.1 | async-start | bytes 983040 | tf_op jit(solution)/shard_map/all_to_all | solution.py:412
  53.1 0.0 copy-done.4
  53.1 0.1 reshape.12
  53.2 0.1 reshape.13.order_ref
  53.3 9.7 %all-to-all-done.1 = bf16[8,40,768]{2,1,0:T(8,128)(2,1)S(1)} async-done(((bf16[8,40,768]{2,1,0:T(8,128)(2,1)}), bf16[8,40,768]{2,1,0:T(8,128)(2,1)S(1)}, u32[]{:S(2)}, u32[]{:S(2)}) %all-to-all-start.1) | async-done | bytes 491552 | tf_op jit(solution)/shard_map/all_to_all | solution.py:412
  63.0 0.7 edges.1
  63.7 10.2 %collective-permute-start.12 = (bf16[64,640]{1,0:T(8,128)(2,1)S(1)}, bf16[64,640]{1,0:T(8,128)(2,1)S(1)}, u32[]{:S(2)}, u32[]{:S(2)}) collective-permute-start(bf16[64,640]{1,0:T(8,128)(2,1)S(1)} %get-tuple-element.43), channel_id=1, source_target_pairs={{8,0},{16,8},{24,16},{32,24},{40,32},{48,40},{56,48},{64,56},{72,6... | collective-permute-start | bytes 245768 | tf_op jit(solution)/shard_map/ppermute | solution.py:427
  73.8 1.9 %collective-permute-start.13 = (bf16[64,640]{1,0:T(8,128)(2,1)S(1)}, bf16[64,640]{1,0:T(8,128)(2,1)S(1)}, u32[]{:S(2)}, u32[]{:S(2)}) collective-permute-start(bf16[64,640]{1,0:T(8,128)(2,1)S(1)} %get-tuple-element.44), channel_id=1, source_target_pairs={{0,8},{8,16},{16,24},{24,32},{32,40},{40,48},{48,56},{56,64},{64,7... | collective-permute-start | bytes 245768 | tf_op jit(solution)/shard_map/ppermute | solution.py:428
  75.7 1.0 %order.1.main_ref = bf16[512,640]{1,0:T(8,128)(2,1)S(1)} custom-call(bf16[640,640]{1,0:T(8,128)(2,1)S(1)} %get-tuple-element.41.chosen_ref, bf16[320,768]{1,0:T(8,128)(2,1)S(1)} %bitcast.12, bf16[320,768]{1,0:T(8,128)(2,1)S(1)} %bitcast.14), custom_call_target="tpu_custom_call" | custom-call | flops 800000000 | bytes 4000000 | tf_op jit(solution)/shard_map/order/pallas_call | solution.py:429
  76.7 0.0 collective-permute-done.12.above_ref
  76.7 5.5 %collective-permute-done.13.below_ref = bf16[64,640]{1,0:T(8,128)(2,1)S(1)} collective-permute-done((bf16[64,640]{1,0:T(8,128)(2,1)S(1)}, bf16[64,640]{1,0:T(8,128)(2,1)S(1)}, u32[]{:S(2)}, u32[]{:S(2)}) %collective-permute-start.13) | collective-permute-done | bytes 81952 | tf_op jit(solution)/shard_map/ppermute | solution.py:428
  82.3 0.0 copy-done.1
  82.3 0.0 copy-done.2
  82.3 8.2 %synthesis.1 = bf16[2,160,5120]{2,1,0:T(8,128)(2,1)} custom-call(bf16[512,640]{1,0:T(8,128)(2,1)S(1)} %order.1.main_ref, bf16[128,640]{1,0:T(8,128)(2,1)S(1)} %get-tuple-element.42.rest_ref, bf16[64,640]{1,0:T(8,128)(2,1)S(1)} %collective-permute-done.12.above_ref, bf16[64,640]{1,0:T(8,128)(2,1)S(1)} %collective-permute-done.13.below_ref, ...), custom_call_target="tpu_custom_call" | custom-call | flops 2400000000 | bytes 11000000 | tf_op jit(solution)/shard_map/synthesis/pallas_call | solution.py:440
  (1 shorter events, 0.0 us)
Async XLA Ops:
  1.7 8.2 %collective-permute-start.3 = (bf16[40,768]{1,0:T(8,128)(2,1)}, bf16[40,768]{1,0:T(8,128)(2,1)S(1)}, u32[]{:S(2)}, u32[]{:S(2)}) collective-permute-start(bf16[40,768]{1,0:T(8,128)(2,1)} %get-tuple-element.26), channel_id=1, source_target_pairs={{0,32},{8,40},{16,48},{24,56},{32,64},{40,72},{48,80},{56,88},{64,... | collective-permute-start | bytes 184328 | tf_op jit(solution)/shard_map/ppermute | solution.py:368
  3.2 8.6 %collective-permute-start.4 = (bf16[40,768]{1,0:T(8,128)(2,1)}, bf16[40,768]{1,0:T(8,128)(2,1)S(1)}, u32[]{:S(2)}, u32[]{:S(2)}) collective-permute-start(bf16[40,768]{1,0:T(8,128)(2,1)} %get-tuple-element.26), channel_id=1, source_target_pairs={{0,96},{8,104},{16,112},{24,120},{32,0},{40,8},{48,16},{56,24},{64... | collective-permute-start | bytes 184328 | tf_op jit(solution)/shard_map/ppermute | solution.py:368
  3.7 8.0 %collective-permute-start.5 = (bf16[40,768]{1,0:T(8,128)(2,1)}, bf16[40,768]{1,0:T(8,128)(2,1)S(1)}, u32[]{:S(2)}, u32[]{:S(2)}) collective-permute-start(bf16[40,768]{1,0:T(8,128)(2,1)} %get-tuple-element.26), channel_id=1, source_target_pairs={{0,64},{8,72},{16,80},{24,88},{32,96},{40,104},{48,112},{56,120},{... | collective-permute-start | bytes 184328 | tf_op jit(solution)/shard_map/ppermute | solution.py:368
  5.9 6.8 %collective-permute-start = (bf16[40,768]{1,0:T(8,128)(2,1)}, bf16[40,768]{1,0:T(8,128)(2,1)S(1)}, u32[]{:S(2)}, u32[]{:S(2)}) collective-permute-start(bf16[40,768]{1,0:T(8,128)(2,1)} %get-tuple-element.25), channel_id=1, source_target_pairs={{0,8},{8,16},{16,24},{24,0},{32,40},{40,48},{48,56},{56,32},{64,72... | collective-permute-start | bytes 184328 | tf_op jit(solution)/shard_map/ppermute | solution.py:368
  7.8 4.9 %collective-permute-start.1 = (bf16[40,768]{1,0:T(8,128)(2,1)}, bf16[40,768]{1,0:T(8,128)(2,1)S(1)}, u32[]{:S(2)}, u32[]{:S(2)}) collective-permute-start(bf16[40,768]{1,0:T(8,128)(2,1)} %get-tuple-element.25), channel_id=1, source_target_pairs={{0,24},{8,0},{16,8},{24,16},{32,56},{40,32},{48,40},{56,48},{64,88... | collective-permute-start | bytes 184328 | tf_op jit(solution)/shard_map/ppermute | solution.py:368
  9.9 5.9 %collective-permute-start.2 = (bf16[40,768]{1,0:T(8,128)(2,1)}, bf16[40,768]{1,0:T(8,128)(2,1)S(1)}, u32[]{:S(2)}, u32[]{:S(2)}) collective-permute-start(bf16[40,768]{1,0:T(8,128)(2,1)} %get-tuple-element.25), channel_id=1, source_target_pairs={{0,16},{8,24},{16,0},{24,8},{32,48},{40,56},{48,32},{56,40},{64,80... | collective-permute-start | bytes 184328 | tf_op jit(solution)/shard_map/ppermute | solution.py:368
  16.7 8.6 %collective-permute-start.6 = (bf16[4,40,768]{2,1,0:T(8,128)(2,1)S(1)}, bf16[4,40,768]{2,1,0:T(8,128)(2,1)S(1)}, u32[]{:S(2)}, u32[]{:S(2)}) collective-permute-start(bf16[4,40,768]{2,1,0:T(8,128)(2,1)S(1)} %pad_maximum_fusion.refs_2_), channel_id=1, source_target_pairs={{0,32},{8,40},{16,48},{24,56},{32,64},{40,72},{48,80},{56,88},{64,... | collective-permute-start | bytes 737288 | tf_op jit(solution)/shard_map/ppermute | solution.py:368
  17.9 13.1 %collective-permute-start.7 = (bf16[4,40,768]{2,1,0:T(8,128)(2,1)S(1)}, bf16[4,40,768]{2,1,0:T(8,128)(2,1)S(1)}, u32[]{:S(2)}, u32[]{:S(2)}) collective-permute-start(bf16[4,40,768]{2,1,0:T(8,128)(2,1)S(1)} %pad_maximum_fusion.refs_2_), channel_id=1, source_target_pairs={{0,96},{8,104},{16,112},{24,120},{32,0},{40,8},{48,16},{56,24},{64... | collective-permute-start | bytes 737288 | tf_op jit(solution)/shard_map/ppermute | solution.py:368
  18.8 12.2 %collective-permute-start.8 = (bf16[4,40,768]{2,1,0:T(8,128)(2,1)S(1)}, bf16[4,40,768]{2,1,0:T(8,128)(2,1)S(1)}, u32[]{:S(2)}, u32[]{:S(2)}) collective-permute-start(bf16[4,40,768]{2,1,0:T(8,128)(2,1)S(1)} %pad_maximum_fusion.refs_2_), channel_id=1, source_target_pairs={{0,64},{8,72},{16,80},{24,88},{32,96},{40,104},{48,112},{56,120},{... | collective-permute-start | bytes 737288 | tf_op jit(solution)/shard_map/ppermute | solution.py:368
  20.3 14.8 %collective-permute-start.10 = (bf16[4,40,768]{2,1,0:T(8,128)(2,1)S(1)}, bf16[4,40,768]{2,1,0:T(8,128)(2,1)S(1)}, u32[]{:S(2)}, u32[]{:S(2)}) collective-permute-start(bf16[4,40,768]{2,1,0:T(8,128)(2,1)S(1)} %pad_maximum_fusion.1.refs_2_), channel_id=1, source_target_pairs={{0,24},{8,0},{16,8},{24,16},{32,56},{40,32},{48,40},{56,48},{64,88... | collective-permute-start | bytes 737288 | tf_op jit(solution)/shard_map/ppermute | solution.py:368
  22.3 12.8 %collective-permute-start.11 = (bf16[4,40,768]{2,1,0:T(8,128)(2,1)S(1)}, bf16[4,40,768]{2,1,0:T(8,128)(2,1)S(1)}, u32[]{:S(2)}, u32[]{:S(2)}) collective-permute-start(bf16[4,40,768]{2,1,0:T(8,128)(2,1)S(1)} %pad_maximum_fusion.1.refs_2_), channel_id=1, source_target_pairs={{0,16},{8,24},{16,0},{24,8},{32,48},{40,56},{48,32},{56,40},{64,80... | collective-permute-start | bytes 737288 | tf_op jit(solution)/shard_map/ppermute | solution.py:368
  25.3 9.8 %collective-permute-start.9 = (bf16[4,40,768]{2,1,0:T(8,128)(2,1)S(1)}, bf16[4,40,768]{2,1,0:T(8,128)(2,1)S(1)}, u32[]{:S(2)}, u32[]{:S(2)}) collective-permute-start(bf16[4,40,768]{2,1,0:T(8,128)(2,1)S(1)} %pad_maximum_fusion.1.refs_2_), channel_id=1, source_target_pairs={{0,8},{8,16},{16,24},{24,0},{32,40},{40,48},{48,56},{56,32},{64,72... | collective-permute-start | bytes 737288 | tf_op jit(solution)/shard_map/ppermute | solution.py:368
  25.3 0.9 %copy-start = (bf16[3,160,256]{2,1,0:T(8,128)(2,1)S(1)}, bf16[3,160,256]{2,1,0:T(8,128)(2,1)}, u32[]{:S(2)}) copy-start(bf16[3,160,256]{2,1,0:T(8,128)(2,1)} %constant.8.clone.matrix_ref) | copy-start | bytes 737284
  26.3 0.7 copy-start.3
  26.9 0.7 copy-start.5
  35.1 14.5 %all-to-all-start = ((bf16[8,40,768]{2,1,0:T(8,128)(2,1)}), bf16[8,40,768]{2,1,0:T(8,128)(2,1)S(1)}, u32[]{:S(2)}, u32[]{:S(2)}) async-start(bf16[8,40,768]{2,1,0:T(8,128)(2,1)} %legendre0.1), calls=%async_computation | async-start | bytes 983040 | tf_op jit(solution)/shard_map/all_to_all | solution.py:412
  39.6 13.5 %copy-start.4 = (s32[640]{0:T(1024)S(1)}, s32[640]{0:T(1024)}, u32[]{:S(2)}) copy-start(s32[640]{0:T(1024)} %order_ref.3) | copy-start | bytes 7684
  39.6 42.7 %copy-start.1 = (bf16[640,128]{1,0:T(8,128)(2,1)S(1)}, bf16[640,128]{1,0:T(8,128)(2,1)}, u32[]{:S(2)}) copy-start(bf16[640,128]{1,0:T(8,128)(2,1)} %constant.10.clone.middle_ref) | copy-start | bytes 491524
  39.6 42.7 %copy-start.2 = (bf16[160,32]{1,0:T(8,128)(2,1)S(1)}, bf16[160,32]{1,0:T(8,128)(2,1)}, u32[]{:S(2)}) copy-start(bf16[160,32]{1,0:T(8,128)(2,1)} %constant.9.clone.expand_ref) | copy-start | bytes 30724
  49.6 13.4 %all-to-all-start.1 = ((bf16[8,40,768]{2,1,0:T(8,128)(2,1)}), bf16[8,40,768]{2,1,0:T(8,128)(2,1)S(1)}, u32[]{:S(2)}, u32[]{:S(2)}) async-start(bf16[8,40,768]{2,1,0:T(8,128)(2,1)} %legendre1.1), calls=%async_computation.1 | async-start | bytes 983040 | tf_op jit(solution)/shard_map/all_to_all | solution.py:412
  63.7 13.0 %collective-permute-start.12 = (bf16[64,640]{1,0:T(8,128)(2,1)S(1)}, bf16[64,640]{1,0:T(8,128)(2,1)S(1)}, u32[]{:S(2)}, u32[]{:S(2)}) collective-permute-start(bf16[64,640]{1,0:T(8,128)(2,1)S(1)} %get-tuple-element.43), channel_id=1, source_target_pairs={{8,0},{16,8},{24,16},{32,24},{40,32},{48,40},{56,48},{64,56},{72,6... | collective-permute-start | bytes 245768 | tf_op jit(solution)/shard_map/ppermute | solution.py:427
  73.8 8.4 %collective-permute-start.13 = (bf16[64,640]{1,0:T(8,128)(2,1)S(1)}, bf16[64,640]{1,0:T(8,128)(2,1)S(1)}, u32[]{:S(2)}, u32[]{:S(2)}) collective-permute-start(bf16[64,640]{1,0:T(8,128)(2,1)S(1)} %get-tuple-element.44), channel_id=1, source_target_pairs={{0,8},{8,16},{16,24},{24,32},{32,40},{40,48},{48,56},{56,64},{64,7... | collective-permute-start | bytes 245768 | tf_op jit(solution)/shard_map/ppermute | solution.py:428

commit v5 on v4

--- a/solution.py
+++ b/solution.py
@@ -30,6 +30,7 @@
 STEPS = NLON // 2 // TILE
 GROUP = 4
 SMALL_BYTES = 16 * 2**20
+MIDDLE_BYTES = 40 * 2**20
 FETCH_BYTES = 44 * 2**20
 LARGE_BYTES = 50 * 2**20
 
@@ -143,98 +144,94 @@
         copy.wait()
 
 
-def legendre_kernel(half, order_ref, writer_ref, *refs):
-    parts = refs[:4]
-    legendre_ref, matrix, out_ref = refs[4:7]
-    spread, rows, results = refs[7:10]
-    held, copies = legendre_ref, []
-    if half:
-        held, sems = refs[10:]
-        for index in range(2):
-            some = PART_SLOTS // 2
-            source = legendre_ref.at[pl.ds(half * PART_SLOTS + index * some, some)]
-            copies.append(pltpu.make_async_copy(source, held.at[pl.ds(index * some, some)], sems.at[index]))
-            copies[-1].start()
-    base = half * PART_PAIRS
-    first = lax.axis_index("wave") * SLOTS + 2 * base
+def legendre_kernel(order_ref, writer_ref, *refs):
+    parts = refs[: 4 * HALVES]
+    near_ref, legendre_ref, matrix, out_ref = refs[4 * HALVES : 4 * HALVES + 4]
+    spread, rows, results, rest, sems = refs[4 * HALVES + 4 :]
+    held = (near_ref, rest)
+    some = PART_SLOTS // 2
+    copies = [
+        pltpu.make_async_copy(
+            legendre_ref.at[pl.ds(PART_SLOTS + index * some, some)], rest.at[pl.ds(index * some, some)], sems.at[index]
+        )
+        for index in range(2)
+    ]
+    for copy in copies:
+        copy.start()
+    first = lax.axis_index("wave") * SLOTS
     band = lax.axis_index("lat")
     band_x, band_z = band // 4, lax.rem(band, 4)
     steps = (0, 3, 1, 2)
-    for outer in range(4):
-        for inner in range(4):
-            along_x, along_z = (outer, inner) if half == 0 else (inner, outer)
-            field = 4 * lax.rem(band_x + steps[along_x], 4) + lax.rem(band_z + steps[along_z], 4)
-            start = pl.multiple_of(field * 2 * PART_PAIRS, 8)
-            for block in range(BLOCKS):
-                values = parts[outer][inner, :, block * LANE : (block + 1) * LANE]
-                spread[block, pl.ds(start, 2 * PART_PAIRS), :] = values.astype(jnp.float32)
-
-    def contract(group, carry):
-        for member in range(GROUP):
-            pair = group * GROUP + member
-            wave = order_ref[first + 2 * pair]
-            lower, upper, values_of_n = [], [], []
-            for block in range(BLOCKS):
-                values = spread[block, pl.ds(pair, 2 * FIELDS, stride=PART_PAIRS), :].astype(jnp.bfloat16)
-                from_a = wave < block * LANE
-                slot = 2 * pair + jnp.where(from_a, 0, 1)
-                source = pl.multiple_of(jnp.where(from_a, block - 1, 4 - block) * LANE, LANE)
-                values_of_n.append(held[slot, :, pl.ds(source, LANE)])
-                lower.append(jnp.where(from_a, values, jnp.zeros_like(values)))
-                upper.append(jnp.where(from_a, jnp.zeros_like(values), values))
-            left = jnp.concatenate(
-                [jnp.concatenate(lower, axis=1), jnp.concatenate(upper, axis=1)], axis=0
-            )
-            sums = lax.dot_general(
-                left, jnp.concatenate(values_of_n, axis=1), (((1,), (1,)), ((), ())), preferred_element_type=jnp.float32
-            )
-            for which in range(2):
-                piece = sums[which * 2 * FIELDS : (which + 1) * 2 * FIELDS]
-                where = pl.ds(2 * pair + which, 2 * FIELDS, stride=PART_SLOTS)
-                rows[0, where, :] = piece[:, :LANE]
-                rows[1, where, : BAND - LANE] = piece[:, LANE:]
-        return carry
-
-    for copy in copies:
-        copy.wait()
-    lax.fori_loop(0, PART_PAIRS // GROUP, contract, 0)
-
-    chunk = 2 * FIELDS * PART_SLOTS // 4
-    for index in range(4):
+    for half in range(HALVES):
+        for outer in range(4):
+            for inner in range(4):
+                along_x, along_z = (outer, inner) if half == 0 else (inner, outer)
+                field = 4 * lax.rem(band_x + steps[along_x], 4) + lax.rem(band_z + steps[along_z], 4)
+                start = pl.multiple_of(field * 2 * PART_PAIRS, 8)
+                for block in range(BLOCKS):
+                    values = parts[4 * half + outer][inner, :, block * LANE : (block + 1) * LANE]
+                    spread[block, pl.ds(start, 2 * PART_PAIRS), :] = values.astype(jnp.float32)
+
+        def contract(group, carry, half=half):
+            for member in range(GROUP):
+                pair = group * GROUP + member
+                wave = order_ref[first + half * PART_SLOTS + 2 * pair]
+                lower, upper, values_of_n = [], [], []
+                for block in range(BLOCKS):
+                    values = spread[block, pl.ds(pair, 2 * FIELDS, stride=PART_PAIRS), :].astype(jnp.bfloat16)
+                    from_a = wave < block * LANE
+                    slot = 2 * pair + jnp.where(from_a, 0, 1)
+                    source = pl.multiple_of(jnp.where(from_a, block - 1, 4 - block) * LANE, LANE)
+                    values_of_n.append(held[half][slot, :, pl.ds(source, LANE)])
+                    lower.append(jnp.where(from_a, values, jnp.zeros_like(values)))
+                    upper.append(jnp.where(from_a, jnp.zeros_like(values), values))
+                left = jnp.concatenate(
+                    [jnp.concatenate(lower, axis=1), jnp.concatenate(upper, axis=1)], axis=0
+                )
+                sums = lax.dot_general(
+                    left,
+                    jnp.concatenate(values_of_n, axis=1),
+                    (((1,), (1,)), ((), ())),
+                    preferred_element_type=jnp.float32,
+                )
+                for which in range(2):
+                    piece = sums[which * 2 * FIELDS : (which + 1) * 2 * FIELDS]
+                    where = pl.ds(half * PART_SLOTS + 2 * pair + which, 2 * FIELDS, stride=SLOTS)
+                    rows[0, where, :] = piece[:, :LANE]
+                    rows[1, where, : BAND - LANE] = piece[:, LANE:]
+            return carry
+
+        if half:
+            for copy in copies:
+                copy.wait()
+        lax.fori_loop(0, PART_PAIRS // GROUP, contract, 0)
+
+    chunk = 2 * FIELDS * SLOTS // 8
+    for index in range(8):
         picked = slice(index * chunk, (index + 1) * chunk)
         left = jnp.concatenate([rows[0, picked, :], rows[1, picked, : BAND - LANE]], axis=1).astype(jnp.bfloat16)
         sums = jnp.dot(left, matrix[...], preferred_element_type=jnp.float32)
         results[0, picked, :] = sums[:, :LANE]
         results[1, picked, :] = sums[:, LANE:]
 
-    lane = lax.broadcasted_iota(jnp.int32, (PART_SLOTS, LANE), 1)
+    lane = lax.broadcasted_iota(jnp.int32, (SLOTS, LANE), 1)
     for owner in range(OWNERS):
         for member in range(2):
             field = writer_ref[2 * owner + member]
             tails = []
             for part in range(2):
-                start = pl.multiple_of((2 * field + part) * PART_SLOTS, 8)
+                start = pl.multiple_of((2 * field + part) * SLOTS, 8)
                 place = (2 * member + part) * LANE
-                out_ref[owner, :, place : place + LANE] = results[0, pl.ds(start, PART_SLOTS), :].astype(jnp.bfloat16)
-                tails.append(results[1, pl.ds(start, PART_SLOTS), :])
+                out_ref[owner, :, place : place + LANE] = results[0, pl.ds(start, SLOTS), :].astype(jnp.bfloat16)
+                tails.append(results[1, pl.ds(start, SLOTS), :])
             place = (4 + member) * LANE
             out_ref[owner, :, place : place + LANE] = jnp.where(lane < LANE // 2, *tails).astype(jnp.bfloat16)
 
 
-def edge_kernel(order_ref, *refs):
-    waves = refs[:HALVES]
-    chosen_ref, rest_ref, above_ref, below_ref = refs[HALVES:]
+def edge_kernel(order_ref, waves_ref, chosen_ref, rest_ref, above_ref, below_ref):
     row = lax.broadcasted_iota(jnp.int32, (NWAVE, NWAVE), 0)
     chosen_ref[...] = jnp.where(row == order_ref[...], 1.0, 0.0).astype(jnp.bfloat16)
-    count = NWAVE // HALVES
-    ordered = sum(
-        jnp.dot(
-            chosen_ref[:, half * count : (half + 1) * count],
-            waves[half][...],
-            preferred_element_type=jnp.float32,
-        )
-        for half in range(HALVES)
-    )
+    ordered = jnp.dot(chosen_ref[...], waves_ref[...], preferred_element_type=jnp.float32)
     turned = ordered.T.astype(jnp.bfloat16)
     rest = BAND - LANE
     for part in range(4):
@@ -244,17 +241,8 @@
         below_ref[part * RANK : (part + 1) * RANK] = turned[start + rest + RANK : start + rest + 2 * RANK]
 
 
-def order_kernel(chosen_ref, *refs):
-    waves, out_ref = refs[:HALVES], refs[HALVES]
-    count = NWAVE // HALVES
-    ordered = sum(
-        jnp.dot(
-            chosen_ref[:, half * count : (half + 1) * count],
-            waves[half][...],
-            preferred_element_type=jnp.float32,
-        )
-        for half in range(HALVES)
-    )
+def order_kernel(chosen_ref, waves_ref, out_ref):
+    ordered = jnp.dot(chosen_ref[...], waves_ref[...], preferred_element_type=jnp.float32)
     out_ref[...] = ordered.T.astype(jnp.bfloat16)
 
 
@@ -336,6 +324,7 @@
 VMEM = pl.BlockSpec(memory_space=pltpu.VMEM)
 ANY = pl.BlockSpec(memory_space=pl.ANY)
 FETCH = pltpu.CompilerParams(vmem_limit_bytes=FETCH_BYTES)
+MIDDLE = pltpu.CompilerParams(vmem_limit_bytes=MIDDLE_BYTES)
 SMALL = pltpu.CompilerParams(vmem_limit_bytes=SMALL_BYTES)
 LARGE = pltpu.CompilerParams(vmem_limit_bytes=LARGE_BYTES)
 
@@ -359,20 +348,14 @@
             ],
             name="pack",
         )(wave_order, spectra)
-        order = wave_order.reshape(OWNERS, HALVES, PART_SLOTS).swapaxes(0, 1).reshape(1, NWAVE)
 
         axes = ((along_z, along_x), (along_x, along_z))
-        gathered = halves
-        for stage in range(2):
-            arrived = [
-                [values] + [lax.ppermute(values, "lat", axes[half][stage](step)) for step in (1, 3, 2)]
-                for half, values in enumerate(gathered)
-            ]
-            gathered = arrived
-            if stage == 0:
-                gathered, legendre = lax.optimization_barrier(([jnp.stack(blocks) for blocks in arrived], legendre))
-
-        orders, writers, matrix, held = pl.pallas_call(
+        firsts = []
+        for half, values in enumerate(halves):
+            sent = [lax.ppermute(values, "lat", axes[half][0](step)) for step in (1, 3, 2)]
+            firsts.append(jnp.stack([values] + sent))
+        firsts, legendre = lax.optimization_barrier((firsts, legendre))
+        orders, writers, matrix, near = pl.pallas_call(
             fetch_kernel,
             out_shape=[
                 jax.ShapeDtypeStruct((NWAVE,), jnp.int32),
@@ -387,43 +370,45 @@
             cost_estimate=pl.CostEstimate(flops=0, bytes_accessed=14_000_000, transcendentals=0),
             name="fetch",
         )(wave_order, writer_order, matrices, legendre)
-
-        waves = []
+        parts, opposites = [], []
+        for half, values in enumerate(firsts):
+            along = axes[half][1]
+            before, after = [lax.ppermute(values, "lat", along(step)) for step in (1, 3)]
+            parts.append([values, before, after])
+            opposites.append(before)
+        opposites, near = lax.optimization_barrier((opposites, near))
         for half in range(HALVES):
-            lifted = pl.pallas_call(
-                lambda *refs, half=half: legendre_kernel(half, *refs),
-                out_shape=bf16(OWNERS, PART_SLOTS, WIDTH),
-                in_specs=[SMEM, SMEM] + [VMEM] * 4 + [ANY if half else VMEM, VMEM],
-                out_specs=VMEM,
-                scratch_shapes=[
-                    pltpu.VMEM((BLOCKS, 2 * FIELDS * PART_PAIRS, LANE), jnp.float32),
-                    pltpu.VMEM((2, 2 * FIELDS * PART_SLOTS, LANE), jnp.float32),
-                    pltpu.VMEM((2, 2 * FIELDS * PART_SLOTS, LANE), jnp.float32),
-                ]
-                + [pltpu.VMEM((PART_SLOTS, BAND, NWAVE), jnp.bfloat16), pltpu.SemaphoreType.DMA((2,))] * half,
-                compiler_params=FETCH if half else SMALL,
-                cost_estimate=pl.CostEstimate(flops=400_000_000, bytes_accessed=8_000_000, transcendentals=0),
-                name=f"legendre{half}",
-            )(orders, writers, *gathered[half], legendre if half else held, matrix)
-            if half + 1 < HALVES:
-                lifted, gathered[half + 1] = lax.optimization_barrier((lifted, gathered[half + 1]))
-            if waves:
-                lifted, waves[-1] = lax.optimization_barrier((lifted, waves[-1]))
-            received = lax.all_to_all(lifted, "wave", split_axis=0, concat_axis=0, tiled=True)
-            waves.append(received.reshape(OWNERS * PART_SLOTS, WIDTH))
+            parts[half].append(lax.ppermute(opposites[half], "lat", axes[half][1](1)))
+
+        lifted = pl.pallas_call(
+            legendre_kernel,
+            out_shape=bf16(OWNERS, SLOTS, WIDTH),
+            in_specs=[SMEM, SMEM] + [VMEM] * (4 * HALVES) + [VMEM, ANY, VMEM],
+            out_specs=VMEM,
+            scratch_shapes=[
+                pltpu.VMEM((BLOCKS, 2 * FIELDS * PART_PAIRS, LANE), jnp.float32),
+                pltpu.VMEM((2, 2 * FIELDS * SLOTS, LANE), jnp.float32),
+                pltpu.VMEM((2, 2 * FIELDS * SLOTS, LANE), jnp.float32),
+                pltpu.VMEM((PART_SLOTS, BAND, NWAVE), jnp.bfloat16),
+                pltpu.SemaphoreType.DMA((2,)),
+            ],
+            compiler_params=MIDDLE,
+            cost_estimate=pl.CostEstimate(flops=800_000_000, bytes_accessed=16_000_000, transcendentals=0),
+            name="legendre",
+        )(orders, writers, *parts[0], *parts[1], near, legendre, matrix)
+        waves = lax.all_to_all(lifted, "wave", split_axis=0, concat_axis=0, tiled=True).reshape(NWAVE, WIDTH)
 
         main, rest = 4 * LANE, 4 * (BAND - LANE)
-        count = NWAVE // HALVES
         chosen, tail, above, below = pl.pallas_call(
             edge_kernel,
             grid=(1,),
             out_shape=[bf16(NWAVE, NWAVE), bf16(rest, NWAVE), bf16(4 * RANK, NWAVE), bf16(4 * RANK, NWAVE)],
             in_specs=[pl.BlockSpec((1, NWAVE), lambda i: (0, 0))]
-            + [pl.BlockSpec((count, WIDTH - main), lambda i: (0, main // (WIDTH - main)))] * HALVES,
+            + [pl.BlockSpec((NWAVE, WIDTH - main), lambda i: (0, main // (WIDTH - main)))],
             out_specs=[VMEM] * 4,
             compiler_params=SMALL,
             name="edges",
-        )(order, *waves)
+        )(wave_order.reshape(1, NWAVE), waves)
         above = lax.ppermute(above, "lat", neighbour(-1))
         below = lax.ppermute(below, "lat", neighbour(1))
         ordered = pl.pallas_call(
@@ -431,12 +416,12 @@
             grid=(1,),
             out_shape=bf16(main, NWAVE),
             in_specs=[pl.BlockSpec((NWAVE, NWAVE), lambda i: (0, 0))]
-            + [pl.BlockSpec((count, main), lambda i: (0, 0))] * HALVES,
+            + [pl.BlockSpec((NWAVE, main), lambda i: (0, 0))],
             out_specs=VMEM,
             compiler_params=SMALL,
             cost_estimate=pl.CostEstimate(flops=800_000_000, bytes_accessed=4_000_000, transcendentals=0),
             name="order",
-        )(chosen, *waves)
+        )(chosen, waves)
         return pl.pallas_call(
             synthesis_kernel,
             out_shape=bf16(2, BAND, NLON),

time: 91 us -> 87.8 us (0.965)
  waiting for transfers between devices: 24 us -> 30.4 us
  starting transfers between devices: 35.7 us -> 30.2 us
  Pallas kernels: 26.4 us -> 22.5 us
    pallas_call x2 -> x1, Pallas kernels: 11.5 us -> 7.94 us  [on_device(): pl.pallas_call(legendre_kernel, out_shape=bf16(OWNERS, SLOTS, WIDTH), in_...]
    all_to_all x2 -> x1, starting transfers between devices: 7.97 us -> 4.48 us  [on_device(): lax.all_to_all(lifted, 'wave', split_axis=0, concat_axis=0, tiled=True)]
    ppermute x12, waiting for transfers between devices: 6.16 us -> 9.44 us  [the longest x2 6.24 us: on_device(): parts[half].append(lax.ppermute(opposites[half], 'lat', axes[half][1](1)))]
    all_to_all x2 -> x1, waiting for transfers between devices: 12.3 us -> 15.2 us  [on_device(): lax.all_to_all(lifted, 'wave', split_axis=0, concat_axis=0, tiled=True)]
    ppermute x1, starting transfers between devices: 10.2 us -> 7.21 us  [on_device(): above = lax.ppermute(above, 'lat', neighbour(-1))]
    ppermute x12, starting transfers between devices: 15.7 us -> 16.6 us  [the longest x6 10.1 us: on_device(): lax.ppermute(values, 'lat', axes[half][0](step))]
  transfers between devices with their start and end apart: 16 -> 15, of which waited for: 5 -> 4; matrix products, arithmetic and copies ran while one was open for 1% -> 1% of each run, Pallas kernels for 17% -> 5%
where the time goes in v5:
time: 87.8 us; the launch traced here: 87.4 us
  waiting for transfers between devices  30.4 us (35%)
  starting transfers between devices  30.2 us (34%)
  Pallas kernels  22.5 us (26%)
  local copies, waits for them, and re-layouts  2.3 us (3%)
  other arithmetic  1.72 us (2%)
    all_to_all x1, waiting for transfers between devices, on_device(): lax.all_to_all(lifted, 'wave', split_axis=0, concat_axis=0, tiled=True)  15.2 us
    ppermute x6, starting transfers between devices, on_device(): lax.ppermute(values, 'lat', axes[half][0](step))  10.1 us
    pallas_call x1, Pallas kernels, on_device(): pl.pallas_call(synthesis_kernel, out_shape=bf16(2, BAND, NLON), in_specs=...  8.22 us
    pallas_call x1, Pallas kernels, on_device(): pl.pallas_call(legendre_kernel, out_shape=bf16(OWNERS, SLOTS, WIDTH), in_...  7.94 us
    ppermute x1, starting transfers between devices, on_device(): above = lax.ppermute(above, 'lat', neighbour(-1))  7.21 us
    ppermute x2, waiting for transfers between devices, on_device(): parts[half].append(lax.ppermute(opposites[half], 'lat', axes[half][1](1)))  6.24 us
    ppermute x1, waiting for transfers between devices, on_device(): below = lax.ppermute(below, 'lat', neighbour(1))  5.75 us
    ppermute x4, starting transfers between devices, on_device(): lax.ppermute(values, 'lat', along(step))  5.33 us
  transfers between devices with their start and end apart: 15, of which 4 were waited for; matrix products, arithmetic and copies ran while one was open for 1% of the time, Pallas kernels for 5%

profile of v5, /device:TPU:2, one launch (start us, length us, event | category | flops | bytes accessed | tf_op | source)
XLA Modules:
  0.0 87.4 jit_solution(2969398152734695700)
XLA Ops:
  0.0 1.7 %pack.1 = (bf16[40,768]{1,0:T(8,128)(2,1)}, bf16[40,768]{1,0:T(8,128)(2,1)}) custom-call(s32[640]{0:T(1024)} %order_ref.3, bf16[1,2,80,640]{3,2,1,0:T(8,128)(2,1)} %spectra_ref.1), custom_call_target="tpu_custom_call" | custom-call | tf_op jit(solution)/shard_map/pack/pallas_call | solution.py:338
  1.7 1.5 %collective-permute-start.3 = (bf16[40,768]{1,0:T(8,128)(2,1)}, bf16[40,768]{1,0:T(8,128)(2,1)S(1)}, u32[]{:S(2)}, u32[]{:S(2)}) collective-permute-start(bf16[40,768]{1,0:T(8,128)(2,1)} %get-tuple-element.22), channel_id=1, source_target_pairs={{0,32},{8,40},{16,48},{24,56},{32,64},{40,72},{48,80},{56,88},{64,... | collective-permute-start | bytes 184328 | tf_op jit(solution)/shard_map/ppermute | solution.py:355
  3.2 0.5 collective-permute-start.4
  3.7 2.1 %collective-permute-start.5 = (bf16[40,768]{1,0:T(8,128)(2,1)}, bf16[40,768]{1,0:T(8,128)(2,1)S(1)}, u32[]{:S(2)}, u32[]{:S(2)}) collective-permute-start(bf16[40,768]{1,0:T(8,128)(2,1)} %get-tuple-element.22), channel_id=1, source_target_pairs={{0,64},{8,72},{16,80},{24,88},{32,96},{40,104},{48,112},{56,120},{... | collective-permute-start | bytes 184328 | tf_op jit(solution)/shard_map/ppermute | solution.py:355
  5.9 1.9 %collective-permute-start = (bf16[40,768]{1,0:T(8,128)(2,1)}, bf16[40,768]{1,0:T(8,128)(2,1)S(1)}, u32[]{:S(2)}, u32[]{:S(2)}) collective-permute-start(bf16[40,768]{1,0:T(8,128)(2,1)} %get-tuple-element.21), channel_id=1, source_target_pairs={{0,8},{8,16},{16,24},{24,0},{32,40},{40,48},{48,56},{56,32},{64,72... | collective-permute-start | bytes 184328 | tf_op jit(solution)/shard_map/ppermute | solution.py:355
  7.8 2.1 %collective-permute-start.1 = (bf16[40,768]{1,0:T(8,128)(2,1)}, bf16[40,768]{1,0:T(8,128)(2,1)S(1)}, u32[]{:S(2)}, u32[]{:S(2)}) collective-permute-start(bf16[40,768]{1,0:T(8,128)(2,1)} %get-tuple-element.21), channel_id=1, source_target_pairs={{0,24},{8,0},{16,8},{24,16},{32,56},{40,32},{48,40},{56,48},{64,88... | collective-permute-start | bytes 184328 | tf_op jit(solution)/shard_map/ppermute | solution.py:355
  9.9 0.0 collective-permute-done.3
  9.9 1.9 %collective-permute-start.2 = (bf16[40,768]{1,0:T(8,128)(2,1)}, bf16[40,768]{1,0:T(8,128)(2,1)S(1)}, u32[]{:S(2)}, u32[]{:S(2)}) collective-permute-start(bf16[40,768]{1,0:T(8,128)(2,1)} %get-tuple-element.21), channel_id=1, source_target_pairs={{0,16},{8,24},{16,0},{24,8},{32,48},{40,56},{48,32},{56,40},{64,80... | collective-permute-start | bytes 184328 | tf_op jit(solution)/shard_map/ppermute | solution.py:355
  11.8 0.0 collective-permute-done.4
  11.8 0.0 collective-permute-done.5
  11.8 0.9 pad_maximum_fusion.1.refs_4_
  12.6 0.0 collective-permute-done
  12.6 0.0 collective-permute-done.1
  12.7 3.2 %collective-permute-done.2 = bf16[40,768]{1,0:T(8,128)(2,1)S(1)} collective-permute-done((bf16[40,768]{1,0:T(8,128)(2,1)}, bf16[40,768]{1,0:T(8,128)(2,1)S(1)}, u32[]{:S(2)}, u32[]{:S(2)}) %collective-permute-start.2) | collective-permute-done | bytes 61472 | tf_op jit(solution)/shard_map/ppermute | solution.py:355
  15.8 0.9 pad_maximum_fusion.refs_0_
  16.7 1.2 %collective-permute-start.6 = (bf16[4,40,768]{2,1,0:T(8,128)(2,1)S(1)}, bf16[4,40,768]{2,1,0:T(8,128)(2,1)S(1)}, u32[]{:S(2)}, u32[]{:S(2)}) collective-permute-start(bf16[4,40,768]{2,1,0:T(8,128)(2,1)S(1)} %pad_maximum_fusion.refs_0_), channel_id=1, source_target_pairs={{0,32},{8,40},{16,48},{24,56},{32,64},{40,72},{48,80},{56,88},{64,... | collective-permute-start | bytes 737288 | tf_op jit(solution)/shard_map/ppermute | solution.py:376
  17.9 0.0 collective-permute-start.8
  17.9 3.2 %collective-permute-start.10 = (bf16[4,40,768]{2,1,0:T(8,128)(2,1)S(1)}, bf16[4,40,768]{2,1,0:T(8,128)(2,1)S(1)}, u32[]{:S(2)}, u32[]{:S(2)}) collective-permute-start(bf16[4,40,768]{2,1,0:T(8,128)(2,1)S(1)} %pad_maximum_fusion.1.refs_4_), channel_id=1, source_target_pairs={{0,24},{8,0},{16,8},{24,16},{32,56},{40,32},{48,40},{56,48},{64,88... | collective-permute-start | bytes 737288 | tf_op jit(solution)/shard_map/ppermute | solution.py:376
  21.1 0.9 %collective-permute-start.7 = (bf16[4,40,768]{2,1,0:T(8,128)(2,1)S(1)}, bf16[4,40,768]{2,1,0:T(8,128)(2,1)S(1)}, u32[]{:S(2)}, u32[]{:S(2)}) collective-permute-start(bf16[4,40,768]{2,1,0:T(8,128)(2,1)S(1)} %pad_maximum_fusion.refs_0_), channel_id=1, source_target_pairs={{0,96},{8,104},{16,112},{24,120},{32,0},{40,8},{48,16},{56,24},{64... | collective-permute-start | bytes 737288 | tf_op jit(solution)/shard_map/ppermute | solution.py:376
  22.0 0.0 copy-start
  22.0 0.9 %copy-done = bf16[3,160,256]{2,1,0:T(8,128)(2,1)S(1)} copy-done((bf16[3,160,256]{2,1,0:T(8,128)(2,1)S(1)}, bf16[3,160,256]{2,1,0:T(8,128)(2,1)}, u32[]{:S(2)}) %copy-start) | copy-done | bytes 245784
  23.0 0.0 copy-start.3
  23.0 0.7 copy-done.3
  23.7 0.0 copy-start.5
  23.7 0.7 copy-done.5
  24.3 3.4 %fetch.1 = (s32[640]{0:T(1024)S(1)}, s32[16]{0:T(128)S(1)}, bf16[160,256]{1,0:T(8,128)(2,1)S(1)}, bf16[40,160,640]{2,1,0:T(8,128)(2,1)S(1)}) custom-call(s32[640]{0:T(1024)S(1)} %copy-done.3, s32[16]{0:T(128)S(1)} %copy-done.5, bf16[3,160,256]{2,1,0:T(8,128)(2,1)S(1)} %copy-done, bf16[80,160,640]{2,1,0:T(8,128)(2,1)} %refs_9_), custom_call_target="tpu_custom_call" | custom-call | bytes 14000000 | tf_op jit(solution)/shard_map/fetch/pallas_call | solution.py:358
  27.7 0.0 collective-permute-done.6.refs_1_
  27.7 0.0 collective-permute-done.8.refs_5_
  27.7 0.1 collective-permute-start.11
  27.8 1.2 %collective-permute-start.9 = (bf16[4,40,768]{2,1,0:T(8,128)(2,1)S(1)}, bf16[4,40,768]{2,1,0:T(8,128)(2,1)S(1)}, u32[]{:S(2)}, u32[]{:S(2)}) collective-permute-start(bf16[4,40,768]{2,1,0:T(8,128)(2,1)S(1)} %collective-permute-done.6.refs_1_), channel_id=1, source_target_pairs={{0,32},{8,40},{16,48},{24,56},{32,64},{40,72},{48,80},{56,88},{64,... | collective-permute-start | bytes 737288 | tf_op jit(solution)/shard_map/ppermute | solution.py:381
  28.9 0.0 collective-permute-done.10.refs_6_
  29.0 0.0 collective-permute-done.7.refs_2_
  29.0 6.2 %collective-permute-done.11.refs_7_ = bf16[4,40,768]{2,1,0:T(8,128)(2,1)S(1)} collective-permute-done((bf16[4,40,768]{2,1,0:T(8,128)(2,1)S(1)}, bf16[4,40,768]{2,1,0:T(8,128)(2,1)S(1)}, u32[]{:S(2)}, u32[]{:S(2)}) %collective-permute-start.11) | collective-permute-done | bytes 245792 | tf_op jit(solution)/shard_map/ppermute | solution.py:381
  35.2 0.0 collective-permute-done.9.refs_3_
  35.2 0.0 copy-start.4
  35.2 0.0 copy-start.1
  35.2 0.0 copy-start.2
  35.2 7.9 %legendre.1 = bf16[8,80,768]{2,1,0:T(8,128)(2,1)} custom-call(s32[640]{0:T(1024)S(1)} %get-tuple-element.24.order_ref, s32[16]{0:T(128)S(1)} %get-tuple-element.25.writer_ref, bf16[4,40,768]{2,1,0:T(8,128)(2,1)S(1)} %pad_maximum_fusion.refs_0_, bf16[4,40,768]{2,1,0:T(8,128)(2,1)S(1)} %collective-permute-done.6.refs_1_, ...), custom_call_target="tpu_custom_call" | custom-call | flops 800000000 | bytes 16000000 | tf_op jit(solution)/shard_map/legendre/pallas_call | solution.py:383
  43.2 4.5 %all-to-all-start = ((bf16[8,80,768]{2,1,0:T(8,128)(2,1)}), bf16[8,80,768]{2,1,0:T(8,128)(2,1)S(1)}, u32[]{:S(2)}, u32[]{:S(2)}) async-start(bf16[8,80,768]{2,1,0:T(8,128)(2,1)} %legendre.1), calls=%async_computation | async-start | bytes 1966080 | tf_op jit(solution)/shard_map/all_to_all | solution.py:399
  47.6 0.0 copy-done.4
  47.6 15.2 %all-to-all-done = bf16[8,80,768]{2,1,0:T(8,128)(2,1)S(1)} async-done(((bf16[8,80,768]{2,1,0:T(8,128)(2,1)}), bf16[8,80,768]{2,1,0:T(8,128)(2,1)S(1)}, u32[]{:S(2)}, u32[]{:S(2)}) %all-to-all-start) | async-done | bytes 983072 | tf_op jit(solution)/shard_map/all_to_all | solution.py:399
  62.9 0.6 edges.1
  63.5 7.2 %collective-permute-start.12 = (bf16[64,640]{1,0:T(8,128)(2,1)S(1)}, bf16[64,640]{1,0:T(8,128)(2,1)S(1)}, u32[]{:S(2)}, u32[]{:S(2)}) collective-permute-start(bf16[64,640]{1,0:T(8,128)(2,1)S(1)} %get-tuple-element.35), channel_id=1, source_target_pairs={{8,0},{16,8},{24,16},{32,24},{40,32},{48,40},{56,48},{64,56},{72,6... | collective-permute-start | bytes 245768 | tf_op jit(solution)/shard_map/ppermute | solution.py:412
  70.7 1.9 %collective-permute-start.13 = (bf16[64,640]{1,0:T(8,128)(2,1)S(1)}, bf16[64,640]{1,0:T(8,128)(2,1)S(1)}, u32[]{:S(2)}, u32[]{:S(2)}) collective-permute-start(bf16[64,640]{1,0:T(8,128)(2,1)S(1)} %get-tuple-element.36), channel_id=1, source_target_pairs={{0,8},{8,16},{16,24},{24,32},{32,40},{40,48},{48,56},{56,64},{64,7... | collective-permute-start | bytes 245768 | tf_op jit(solution)/shard_map/ppermute | solution.py:413
  72.6 0.7 order.1.main_ref
  73.4 0.0 collective-permute-done.12.above_ref
  73.4 5.8 %collective-permute-done.13.below_ref = bf16[64,640]{1,0:T(8,128)(2,1)S(1)} collective-permute-done((bf16[64,640]{1,0:T(8,128)(2,1)S(1)}, bf16[64,640]{1,0:T(8,128)(2,1)S(1)}, u32[]{:S(2)}, u32[]{:S(2)}) %collective-permute-start.13) | collective-permute-done | bytes 81952 | tf_op jit(solution)/shard_map/ppermute | solution.py:413
  79.1 0.0 copy-done.1
  79.1 0.0 copy-done.2
  79.1 8.2 %synthesis.1 = bf16[2,160,5120]{2,1,0:T(8,128)(2,1)} custom-call(bf16[512,640]{1,0:T(8,128)(2,1)S(1)} %order.1.main_ref, bf16[128,640]{1,0:T(8,128)(2,1)S(1)} %get-tuple-element.34.rest_ref, bf16[64,640]{1,0:T(8,128)(2,1)S(1)} %collective-permute-done.12.above_ref, bf16[64,640]{1,0:T(8,128)(2,1)S(1)} %collective-permute-done.13.below_ref, ...), custom_call_target="tpu_custom_call" | custom-call | flops 2400000000 | bytes 11000000 | tf_op jit(solution)/shard_map/synthesis/pallas_call | solution.py:425
  (1 shorter events, 0.0 us)
Async XLA Ops:
  1.7 8.2 %collective-permute-start.3 = (bf16[40,768]{1,0:T(8,128)(2,1)}, bf16[40,768]{1,0:T(8,128)(2,1)S(1)}, u32[]{:S(2)}, u32[]{:S(2)}) collective-permute-start(bf16[40,768]{1,0:T(8,128)(2,1)} %get-tuple-element.22), channel_id=1, source_target_pairs={{0,32},{8,40},{16,48},{24,56},{32,64},{40,72},{48,80},{56,88},{64,... | collective-permute-start | bytes 184328 | tf_op jit(solution)/shard_map/ppermute | solution.py:355
  3.2 8.6 %collective-permute-start.4 = (bf16[40,768]{1,0:T(8,128)(2,1)}, bf16[40,768]{1,0:T(8,128)(2,1)S(1)}, u32[]{:S(2)}, u32[]{:S(2)}) collective-permute-start(bf16[40,768]{1,0:T(8,128)(2,1)} %get-tuple-element.22), channel_id=1, source_target_pairs={{0,96},{8,104},{16,112},{24,120},{32,0},{40,8},{48,16},{56,24},{64... | collective-permute-start | bytes 184328 | tf_op jit(solution)/shard_map/ppermute | solution.py:355
  3.7 8.0 %collective-permute-start.5 = (bf16[40,768]{1,0:T(8,128)(2,1)}, bf16[40,768]{1,0:T(8,128)(2,1)S(1)}, u32[]{:S(2)}, u32[]{:S(2)}) collective-permute-start(bf16[40,768]{1,0:T(8,128)(2,1)} %get-tuple-element.22), channel_id=1, source_target_pairs={{0,64},{8,72},{16,80},{24,88},{32,96},{40,104},{48,112},{56,120},{... | collective-permute-start | bytes 184328 | tf_op jit(solution)/shard_map/ppermute | solution.py:355
  5.9 6.8 %collective-permute-start = (bf16[40,768]{1,0:T(8,128)(2,1)}, bf16[40,768]{1,0:T(8,128)(2,1)S(1)}, u32[]{:S(2)}, u32[]{:S(2)}) collective-permute-start(bf16[40,768]{1,0:T(8,128)(2,1)} %get-tuple-element.21), channel_id=1, source_target_pairs={{0,8},{8,16},{16,24},{24,0},{32,40},{40,48},{48,56},{56,32},{64,72... | collective-permute-start | bytes 184328 | tf_op jit(solution)/shard_map/ppermute | solution.py:355
  7.8 4.9 %collective-permute-start.1 = (bf16[40,768]{1,0:T(8,128)(2,1)}, bf16[40,768]{1,0:T(8,128)(2,1)S(1)}, u32[]{:S(2)}, u32[]{:S(2)}) collective-permute-start(bf16[40,768]{1,0:T(8,128)(2,1)} %get-tuple-element.21), channel_id=1, source_target_pairs={{0,24},{8,0},{16,8},{24,16},{32,56},{40,32},{48,40},{56,48},{64,88... | collective-permute-start | bytes 184328 | tf_op jit(solution)/shard_map/ppermute | solution.py:355
  9.9 5.9 %collective-permute-start.2 = (bf16[40,768]{1,0:T(8,128)(2,1)}, bf16[40,768]{1,0:T(8,128)(2,1)S(1)}, u32[]{:S(2)}, u32[]{:S(2)}) collective-permute-start(bf16[40,768]{1,0:T(8,128)(2,1)} %get-tuple-element.21), channel_id=1, source_target_pairs={{0,16},{8,24},{16,0},{24,8},{32,48},{40,56},{48,32},{56,40},{64,80... | collective-permute-start | bytes 184328 | tf_op jit(solution)/shard_map/ppermute | solution.py:355
  16.7 11.0 %collective-permute-start.6 = (bf16[4,40,768]{2,1,0:T(8,128)(2,1)S(1)}, bf16[4,40,768]{2,1,0:T(8,128)(2,1)S(1)}, u32[]{:S(2)}, u32[]{:S(2)}) collective-permute-start(bf16[4,40,768]{2,1,0:T(8,128)(2,1)S(1)} %pad_maximum_fusion.refs_0_), channel_id=1, source_target_pairs={{0,32},{8,40},{16,48},{24,56},{32,64},{40,72},{48,80},{56,88},{64,... | collective-permute-start | bytes 737288 | tf_op jit(solution)/shard_map/ppermute | solution.py:376
  17.9 9.9 %collective-permute-start.8 = (bf16[4,40,768]{2,1,0:T(8,128)(2,1)S(1)}, bf16[4,40,768]{2,1,0:T(8,128)(2,1)S(1)}, u32[]{:S(2)}, u32[]{:S(2)}) collective-permute-start(bf16[4,40,768]{2,1,0:T(8,128)(2,1)S(1)} %pad_maximum_fusion.1.refs_4_), channel_id=1, source_target_pairs={{0,8},{8,16},{16,24},{24,0},{32,40},{40,48},{48,56},{56,32},{64,72... | collective-permute-start | bytes 737288 | tf_op jit(solution)/shard_map/ppermute | solution.py:376
  17.9 11.1 %collective-permute-start.10 = (bf16[4,40,768]{2,1,0:T(8,128)(2,1)S(1)}, bf16[4,40,768]{2,1,0:T(8,128)(2,1)S(1)}, u32[]{:S(2)}, u32[]{:S(2)}) collective-permute-start(bf16[4,40,768]{2,1,0:T(8,128)(2,1)S(1)} %pad_maximum_fusion.1.refs_4_), channel_id=1, source_target_pairs={{0,24},{8,0},{16,8},{24,16},{32,56},{40,32},{48,40},{56,48},{64,88... | collective-permute-start | bytes 737288 | tf_op jit(solution)/shard_map/ppermute | solution.py:376
  21.1 7.9 %collective-permute-start.7 = (bf16[4,40,768]{2,1,0:T(8,128)(2,1)S(1)}, bf16[4,40,768]{2,1,0:T(8,128)(2,1)S(1)}, u32[]{:S(2)}, u32[]{:S(2)}) collective-permute-start(bf16[4,40,768]{2,1,0:T(8,128)(2,1)S(1)} %pad_maximum_fusion.refs_0_), channel_id=1, source_target_pairs={{0,96},{8,104},{16,112},{24,120},{32,0},{40,8},{48,16},{56,24},{64... | collective-permute-start | bytes 737288 | tf_op jit(solution)/shard_map/ppermute | solution.py:376
  22.0 0.9 %copy-start = (bf16[3,160,256]{2,1,0:T(8,128)(2,1)S(1)}, bf16[3,160,256]{2,1,0:T(8,128)(2,1)}, u32[]{:S(2)}) copy-start(bf16[3,160,256]{2,1,0:T(8,128)(2,1)} %constant.8.clone.matrix_ref) | copy-start | bytes 737284
  23.0 0.7 copy-start.3
  23.7 0.7 copy-start.5
  27.7 7.5 %collective-permute-start.11 = (bf16[4,40,768]{2,1,0:T(8,128)(2,1)S(1)}, bf16[4,40,768]{2,1,0:T(8,128)(2,1)S(1)}, u32[]{:S(2)}, u32[]{:S(2)}) collective-permute-start(bf16[4,40,768]{2,1,0:T(8,128)(2,1)S(1)} %collective-permute-done.8.refs_5_), channel_id=1, source_target_pairs={{0,8},{8,16},{16,24},{24,0},{32,40},{40,48},{48,56},{56,32},{64,72... | collective-permute-start | bytes 737288 | tf_op jit(solution)/shard_map/ppermute | solution.py:381
  27.8 7.4 %collective-permute-start.9 = (bf16[4,40,768]{2,1,0:T(8,128)(2,1)S(1)}, bf16[4,40,768]{2,1,0:T(8,128)(2,1)S(1)}, u32[]{:S(2)}, u32[]{:S(2)}) collective-permute-start(bf16[4,40,768]{2,1,0:T(8,128)(2,1)S(1)} %collective-permute-done.6.refs_1_), channel_id=1, source_target_pairs={{0,32},{8,40},{16,48},{24,56},{32,64},{40,72},{48,80},{56,88},{64,... | collective-permute-start | bytes 737288 | tf_op jit(solution)/shard_map/ppermute | solution.py:381
  35.2 12.4 %copy-start.4 = (s32[640]{0:T(1024)S(1)}, s32[640]{0:T(1024)}, u32[]{:S(2)}) copy-start(s32[640]{0:T(1024)} %order_ref.3) | copy-start | bytes 7684
  35.2 43.9 %copy-start.1 = (bf16[640,128]{1,0:T(8,128)(2,1)S(1)}, bf16[640,128]{1,0:T(8,128)(2,1)}, u32[]{:S(2)}) copy-start(bf16[640,128]{1,0:T(8,128)(2,1)} %constant.10.clone.middle_ref) | copy-start | bytes 491524
  35.2 43.9 %copy-start.2 = (bf16[160,32]{1,0:T(8,128)(2,1)S(1)}, bf16[160,32]{1,0:T(8,128)(2,1)}, u32[]{:S(2)}) copy-start(bf16[160,32]{1,0:T(8,128)(2,1)} %constant.9.clone.expand_ref) | copy-start | bytes 30724
  43.2 19.7 %all-to-all-start = ((bf16[8,80,768]{2,1,0:T(8,128)(2,1)}), bf16[8,80,768]{2,1,0:T(8,128)(2,1)S(1)}, u32[]{:S(2)}, u32[]{:S(2)}) async-start(bf16[8,80,768]{2,1,0:T(8,128)(2,1)} %legendre.1), calls=%async_computation | async-start | bytes 1966080 | tf_op jit(solution)/shard_map/all_to_all | solution.py:399
  63.5 9.9 %collective-permute-start.12 = (bf16[64,640]{1,0:T(8,128)(2,1)S(1)}, bf16[64,640]{1,0:T(8,128)(2,1)S(1)}, u32[]{:S(2)}, u32[]{:S(2)}) collective-permute-start(bf16[64,640]{1,0:T(8,128)(2,1)S(1)} %get-tuple-element.35), channel_id=1, source_target_pairs={{8,0},{16,8},{24,16},{32,24},{40,32},{48,40},{56,48},{64,56},{72,6... | collective-permute-start | bytes 245768 | tf_op jit(solution)/shard_map/ppermute | solution.py:412
  70.7 8.4 %collective-permute-start.13 = (bf16[64,640]{1,0:T(8,128)(2,1)S(1)}, bf16[64,640]{1,0:T(8,128)(2,1)S(1)}, u32[]{:S(2)}, u32[]{:S(2)}) collective-permute-start(bf16[64,640]{1,0:T(8,128)(2,1)S(1)} %get-tuple-element.36), channel_id=1, source_target_pairs={{0,8},{8,16},{16,24},{24,32},{32,40},{40,48},{48,56},{56,64},{64,7... | collective-permute-start | bytes 245768 | tf_op jit(solution)/shard_map/ppermute | solution.py:413

commit v6 on v5

--- a/solution.py
+++ b/solution.py
@@ -146,8 +146,8 @@
 
 def legendre_kernel(order_ref, writer_ref, *refs):
     parts = refs[: 4 * HALVES]
-    near_ref, legendre_ref, matrix, out_ref = refs[4 * HALVES : 4 * HALVES + 4]
-    spread, rows, results, rest, sems = refs[4 * HALVES + 4 :]
+    near_ref, legendre_ref, matrix, out_ref, tail_ref = refs[4 * HALVES : 4 * HALVES + 5]
+    spread, rows, results, rest, sems = refs[4 * HALVES + 5 :]
     held = (near_ref, rest)
     some = PART_SLOTS // 2
     copies = [
@@ -224,8 +224,8 @@
                 place = (2 * member + part) * LANE
                 out_ref[owner, :, place : place + LANE] = results[0, pl.ds(start, SLOTS), :].astype(jnp.bfloat16)
                 tails.append(results[1, pl.ds(start, SLOTS), :])
-            place = (4 + member) * LANE
-            out_ref[owner, :, place : place + LANE] = jnp.where(lane < LANE // 2, *tails).astype(jnp.bfloat16)
+            place = member * LANE
+            tail_ref[owner, :, place : place + LANE] = jnp.where(lane < LANE // 2, *tails).astype(jnp.bfloat16)
 
 
 def edge_kernel(order_ref, waves_ref, chosen_ref, rest_ref, above_ref, below_ref):
@@ -380,11 +380,11 @@
         for half in range(HALVES):
             parts[half].append(lax.ppermute(opposites[half], "lat", axes[half][1](1)))
 
-        lifted = pl.pallas_call(
+        lifted, tails = pl.pallas_call(
             legendre_kernel,
-            out_shape=bf16(OWNERS, SLOTS, WIDTH),
+            out_shape=[bf16(OWNERS, SLOTS, 4 * LANE), bf16(OWNERS, SLOTS, WIDTH - 4 * LANE)],
             in_specs=[SMEM, SMEM] + [VMEM] * (4 * HALVES) + [VMEM, ANY, VMEM],
-            out_specs=VMEM,
+            out_specs=[VMEM] * 2,
             scratch_shapes=[
                 pltpu.VMEM((BLOCKS, 2 * FIELDS * PART_PAIRS, LANE), jnp.float32),
                 pltpu.VMEM((2, 2 * FIELDS * SLOTS, LANE), jnp.float32),
@@ -396,7 +396,8 @@
             cost_estimate=pl.CostEstimate(flops=800_000_000, bytes_accessed=16_000_000, transcendentals=0),
             name="legendre",
         )(orders, writers, *parts[0], *parts[1], near, legendre, matrix)
-        waves = lax.all_to_all(lifted, "wave", split_axis=0, concat_axis=0, tiled=True).reshape(NWAVE, WIDTH)
+        edges = lax.all_to_all(tails, "wave", split_axis=0, concat_axis=0, tiled=True)
+        waves = lax.all_to_all(lifted, "wave", split_axis=0, concat_axis=0, tiled=True)
 
         main, rest = 4 * LANE, 4 * (BAND - LANE)
         chosen, tail, above, below = pl.pallas_call(
@@ -404,11 +405,11 @@
             grid=(1,),
             out_shape=[bf16(NWAVE, NWAVE), bf16(rest, NWAVE), bf16(4 * RANK, NWAVE), bf16(4 * RANK, NWAVE)],
             in_specs=[pl.BlockSpec((1, NWAVE), lambda i: (0, 0))]
-            + [pl.BlockSpec((NWAVE, WIDTH - main), lambda i: (0, main // (WIDTH - main)))],
+            + [pl.BlockSpec((NWAVE, WIDTH - main), lambda i: (0, 0))],
             out_specs=[VMEM] * 4,
             compiler_params=SMALL,
             name="edges",
-        )(wave_order.reshape(1, NWAVE), waves)
+        )(wave_order.reshape(1, NWAVE), edges.reshape(NWAVE, WIDTH - main))
         above = lax.ppermute(above, "lat", neighbour(-1))
         below = lax.ppermute(below, "lat", neighbour(1))
         ordered = pl.pallas_call(
@@ -421,7 +422,7 @@
             compiler_params=SMALL,
             cost_estimate=pl.CostEstimate(flops=800_000_000, bytes_accessed=4_000_000, transcendentals=0),
             name="order",
-        )(chosen, waves)
+        )(chosen, waves.reshape(NWAVE, main))
         return pl.pallas_call(
             synthesis_kernel,
             out_shape=bf16(2, BAND, NLON),

time: 87.8 us -> 84.4 us (0.961)
  waiting for transfers between devices: 30.4 us -> 15.2 us
  blocking collectives: 0 us -> 12.5 us
  starting transfers between devices: 30.2 us -> 29.3 us
    all_to_all x1, waiting for transfers between devices: 15.2 us -> 1.91 us  [on_device(): lax.all_to_all(lifted, 'wave', split_axis=0, concat_axis=0, tiled=True)]
    all_to_all x0 -> x1, blocking collectives: none -> 12.5 us  [on_device(): lax.all_to_all(tails, 'wave', split_axis=0, concat_axis=0, tiled=True)]
    ppermute x1, waiting for transfers between devices: 5.75 us -> 3.85 us  [on_device(): below = lax.ppermute(below, 'lat', neighbour(1))]
    all_to_all x1, starting transfers between devices: 4.48 us -> 3.54 us  [on_device(): lax.all_to_all(lifted, 'wave', split_axis=0, concat_axis=0, tiled=True)]
  transfers between devices with their start and end apart: 15 -> 15, of which waited for: 4 -> 4; matrix products, arithmetic and copies ran while one was open for 1% -> 1% of each run, Pallas kernels for 5% -> 6%
where the time goes in v6:
time: 84.4 us; the launch traced here: 83.6 us
  starting transfers between devices  29.3 us (35%)
  Pallas kernels  22.4 us (27%)
  waiting for transfers between devices  15.2 us (18%)
  blocking collectives  12.5 us (15%)
  local copies, waits for them, and re-layouts  2.3 us (3%)
  other arithmetic  1.72 us (2%)
    all_to_all x1, blocking collectives, on_device(): lax.all_to_all(tails, 'wave', split_axis=0, concat_axis=0, tiled=True)  12.5 us
    ppermute x6, starting transfers between devices, on_device(): lax.ppermute(values, 'lat', axes[half][0](step))  10.1 us
    pallas_call x1, Pallas kernels, on_device(): pl.pallas_call(synthesis_kernel, out_shape=bf16(2, BAND, NLON), in_specs=...  8.22 us
    pallas_call x1, Pallas kernels, on_device(): pl.pallas_call(legendre_kernel, out_shape=[bf16(OWNERS, SLOTS, 4 * LANE),...  7.82 us
    ppermute x1, starting transfers between devices, on_device(): above = lax.ppermute(above, 'lat', neighbour(-1))  7.24 us
    ppermute x2, waiting for transfers between devices, on_device(): parts[half].append(lax.ppermute(opposites[half], 'lat', axes[half][1](1)))  6.24 us
    ppermute x4, starting transfers between devices, on_device(): lax.ppermute(values, 'lat', along(step))  5.33 us
    ppermute x1, waiting for transfers between devices, on_device(): below = lax.ppermute(below, 'lat', neighbour(1))  3.85 us
  transfers between devices with their start and end apart: 15, of which 4 were waited for; matrix products, arithmetic and copies ran while one was open for 1% of the time, Pallas kernels for 6%

profile of v6, /device:TPU:2, one launch (start us, length us, event | category | flops | bytes accessed | tf_op | source)
XLA Modules:
  0.0 83.6 jit_solution(8771061359190228324)
XLA Ops:
  0.0 1.7 %pack.1 = (bf16[40,768]{1,0:T(8,128)(2,1)}, bf16[40,768]{1,0:T(8,128)(2,1)}) custom-call(s32[640]{0:T(1024)} %order_ref.3, bf16[1,2,80,640]{3,2,1,0:T(8,128)(2,1)} %spectra_ref.1), custom_call_target="tpu_custom_call" | custom-call | tf_op jit(solution)/shard_map/pack/pallas_call | solution.py:338
  1.7 1.5 %collective-permute-start.3 = (bf16[40,768]{1,0:T(8,128)(2,1)}, bf16[40,768]{1,0:T(8,128)(2,1)S(1)}, u32[]{:S(2)}, u32[]{:S(2)}) collective-permute-start(bf16[40,768]{1,0:T(8,128)(2,1)} %get-tuple-element.24), channel_id=1, source_target_pairs={{0,32},{8,40},{16,48},{24,56},{32,64},{40,72},{48,80},{56,88},{64,... | collective-permute-start | bytes 184328 | tf_op jit(solution)/shard_map/ppermute | solution.py:355
  3.2 0.5 collective-permute-start.4
  3.7 2.1 %collective-permute-start.5 = (bf16[40,768]{1,0:T(8,128)(2,1)}, bf16[40,768]{1,0:T(8,128)(2,1)S(1)}, u32[]{:S(2)}, u32[]{:S(2)}) collective-permute-start(bf16[40,768]{1,0:T(8,128)(2,1)} %get-tuple-element.24), channel_id=1, source_target_pairs={{0,64},{8,72},{16,80},{24,88},{32,96},{40,104},{48,112},{56,120},{... | collective-permute-start | bytes 184328 | tf_op jit(solution)/shard_map/ppermute | solution.py:355
  5.9 1.9 %collective-permute-start = (bf16[40,768]{1,0:T(8,128)(2,1)}, bf16[40,768]{1,0:T(8,128)(2,1)S(1)}, u32[]{:S(2)}, u32[]{:S(2)}) collective-permute-start(bf16[40,768]{1,0:T(8,128)(2,1)} %get-tuple-element.23), channel_id=1, source_target_pairs={{0,8},{8,16},{16,24},{24,0},{32,40},{40,48},{48,56},{56,32},{64,72... | collective-permute-start | bytes 184328 | tf_op jit(solution)/shard_map/ppermute | solution.py:355
  7.8 2.1 %collective-permute-start.1 = (bf16[40,768]{1,0:T(8,128)(2,1)}, bf16[40,768]{1,0:T(8,128)(2,1)S(1)}, u32[]{:S(2)}, u32[]{:S(2)}) collective-permute-start(bf16[40,768]{1,0:T(8,128)(2,1)} %get-tuple-element.23), channel_id=1, source_target_pairs={{0,24},{8,0},{16,8},{24,16},{32,56},{40,32},{48,40},{56,48},{64,88... | collective-permute-start | bytes 184328 | tf_op jit(solution)/shard_map/ppermute | solution.py:355
  9.9 0.0 collective-permute-done.3
  9.9 1.9 %collective-permute-start.2 = (bf16[40,768]{1,0:T(8,128)(2,1)}, bf16[40,768]{1,0:T(8,128)(2,1)S(1)}, u32[]{:S(2)}, u32[]{:S(2)}) collective-permute-start(bf16[40,768]{1,0:T(8,128)(2,1)} %get-tuple-element.23), channel_id=1, source_target_pairs={{0,16},{8,24},{16,0},{24,8},{32,48},{40,56},{48,32},{56,40},{64,80... | collective-permute-start | bytes 184328 | tf_op jit(solution)/shard_map/ppermute | solution.py:355
  11.8 0.0 collective-permute-done.4
  11.8 0.0 collective-permute-done.5
  11.8 0.9 %pad_maximum_fusion.1.refs_4_ = bf16[4,40,768]{2,1,0:T(8,128)(2,1)S(1)} fusion(bf16[1,40,768]{2,1,0:T(8,128)(2,1)S(1)} %bitcast.18, bf16[1,40,768]{2,1,0:T(8,128)(2,1)S(1)} %bitcast.17, bf16[1,40,768]{2,1,0:T(8,128)(2,1)S(1)} %bitcast.15, bf16[1,40,768]{2,1,0:T(8,128)(2,1)} %bitcast.13), kind=kLoop, calls=%fused_computation.1 | loop fusion | flops 368640 | bytes 491520 | tf_op jit(solution)/shard_map/stack | solution.py:356
  12.6 0.0 collective-permute-done
  12.6 0.0 collective-permute-done.1
  12.7 3.2 %collective-permute-done.2 = bf16[40,768]{1,0:T(8,128)(2,1)S(1)} collective-permute-done((bf16[40,768]{1,0:T(8,128)(2,1)}, bf16[40,768]{1,0:T(8,128)(2,1)S(1)}, u32[]{:S(2)}, u32[]{:S(2)}) %collective-permute-start.2) | collective-permute-done | bytes 61472 | tf_op jit(solution)/shard_map/ppermute | solution.py:355
  15.8 0.9 %pad_maximum_fusion.refs_0_ = bf16[4,40,768]{2,1,0:T(8,128)(2,1)S(1)} fusion(bf16[1,40,768]{2,1,0:T(8,128)(2,1)S(1)} %bitcast.19, bf16[1,40,768]{2,1,0:T(8,128)(2,1)S(1)} %bitcast.16, bf16[1,40,768]{2,1,0:T(8,128)(2,1)S(1)} %bitcast.14, bf16[1,40,768]{2,1,0:T(8,128)(2,1)} %bitcast.12), kind=kLoop, calls=%fused_computation | loop fusion | flops 368640 | bytes 491520 | tf_op jit(solution)/shard_map/stack | solution.py:356
  16.7 1.2 %collective-permute-start.6 = (bf16[4,40,768]{2,1,0:T(8,128)(2,1)S(1)}, bf16[4,40,768]{2,1,0:T(8,128)(2,1)S(1)}, u32[]{:S(2)}, u32[]{:S(2)}) collective-permute-start(bf16[4,40,768]{2,1,0:T(8,128)(2,1)S(1)} %pad_maximum_fusion.refs_0_), channel_id=1, source_target_pairs={{0,32},{8,40},{16,48},{24,56},{32,64},{40,72},{48,80},{56,88},{64,... | collective-permute-start | bytes 737288 | tf_op jit(solution)/shard_map/ppermute | solution.py:376
  17.9 0.0 collective-permute-start.8
  17.9 3.2 %collective-permute-start.10 = (bf16[4,40,768]{2,1,0:T(8,128)(2,1)S(1)}, bf16[4,40,768]{2,1,0:T(8,128)(2,1)S(1)}, u32[]{:S(2)}, u32[]{:S(2)}) collective-permute-start(bf16[4,40,768]{2,1,0:T(8,128)(2,1)S(1)} %pad_maximum_fusion.1.refs_4_), channel_id=1, source_target_pairs={{0,24},{8,0},{16,8},{24,16},{32,56},{40,32},{48,40},{56,48},{64,88... | collective-permute-start | bytes 737288 | tf_op jit(solution)/shard_map/ppermute | solution.py:376
  21.1 0.9 %collective-permute-start.7 = (bf16[4,40,768]{2,1,0:T(8,128)(2,1)S(1)}, bf16[4,40,768]{2,1,0:T(8,128)(2,1)S(1)}, u32[]{:S(2)}, u32[]{:S(2)}) collective-permute-start(bf16[4,40,768]{2,1,0:T(8,128)(2,1)S(1)} %pad_maximum_fusion.refs_0_), channel_id=1, source_target_pairs={{0,96},{8,104},{16,112},{24,120},{32,0},{40,8},{48,16},{56,24},{64... | collective-permute-start | bytes 737288 | tf_op jit(solution)/shard_map/ppermute | solution.py:376
  22.0 0.0 copy-start
  22.0 0.9 %copy-done = bf16[3,160,256]{2,1,0:T(8,128)(2,1)S(1)} copy-done((bf16[3,160,256]{2,1,0:T(8,128)(2,1)S(1)}, bf16[3,160,256]{2,1,0:T(8,128)(2,1)}, u32[]{:S(2)}) %copy-start) | copy-done | bytes 245784
  23.0 0.0 copy-start.3
  23.0 0.7 copy-done.3
  23.7 0.0 copy-start.5
  23.7 0.7 copy-done.5
  24.3 3.4 %fetch.1 = (s32[640]{0:T(1024)S(1)}, s32[16]{0:T(128)S(1)}, bf16[160,256]{1,0:T(8,128)(2,1)S(1)}, bf16[40,160,640]{2,1,0:T(8,128)(2,1)S(1)}) custom-call(s32[640]{0:T(1024)S(1)} %copy-done.3, s32[16]{0:T(128)S(1)} %copy-done.5, bf16[3,160,256]{2,1,0:T(8,128)(2,1)S(1)} %copy-done, bf16[80,160,640]{2,1,0:T(8,128)(2,1)} %refs_9_), custom_call_target="tpu_custom_call" | custom-call | bytes 14000000 | tf_op jit(solution)/shard_map/fetch/pallas_call | solution.py:358
  27.7 0.0 collective-permute-done.6.refs_1_
  27.7 0.0 collective-permute-done.8.refs_5_
  27.7 0.1 collective-permute-start.11
  27.8 1.2 %collective-permute-start.9 = (bf16[4,40,768]{2,1,0:T(8,128)(2,1)S(1)}, bf16[4,40,768]{2,1,0:T(8,128)(2,1)S(1)}, u32[]{:S(2)}, u32[]{:S(2)}) collective-permute-start(bf16[4,40,768]{2,1,0:T(8,128)(2,1)S(1)} %collective-permute-done.6.refs_1_), channel_id=1, source_target_pairs={{0,32},{8,40},{16,48},{24,56},{32,64},{40,72},{48,80},{56,88},{64,... | collective-permute-start | bytes 737288 | tf_op jit(solution)/shard_map/ppermute | solution.py:381
  28.9 0.0 collective-permute-done.10.refs_6_
  29.0 0.0 collective-permute-done.7.refs_2_
  29.0 6.2 %collective-permute-done.11.refs_7_ = bf16[4,40,768]{2,1,0:T(8,128)(2,1)S(1)} collective-permute-done((bf16[4,40,768]{2,1,0:T(8,128)(2,1)S(1)}, bf16[4,40,768]{2,1,0:T(8,128)(2,1)S(1)}, u32[]{:S(2)}, u32[]{:S(2)}) %collective-permute-start.11) | collective-permute-done | bytes 245792 | tf_op jit(solution)/shard_map/ppermute | solution.py:381
  35.2 0.0 collective-permute-done.9.refs_3_
  35.2 0.0 copy-start.4
  35.2 0.0 copy-start.1
  35.2 0.0 copy-start.2
  35.2 7.8 %legendre.1 = (bf16[8,80,512]{2,1,0:T(8,128)(2,1)}, bf16[8,80,256]{2,1,0:T(8,128)(2,1)S(1)}) custom-call(s32[640]{0:T(1024)S(1)} %get-tuple-element.26.order_ref, s32[16]{0:T(128)S(1)} %get-tuple-element.27.writer_ref, bf16[4,40,768]{2,1,0:T(8,128)(2,1)S(1)} %pad_maximum_fusion.refs_0_, bf16[4,40,768]{2,1,0:T(8,128)(2,1)S(1)} %collective-permute-done.6.refs_1_, ...), custom_call_target="tpu_custom_call" | custom-call | flops 800000000 | bytes 16000000 | tf_op jit(solution)/shard_map/legendre/pallas_call | solution.py:383
  43.0 12.5 %all_to_all.10 = bf16[8,80,256]{2,1,0:T(8,128)(2,1)S(1)} all-to-all(bf16[8,80,256]{2,1,0:T(8,128)(2,1)S(1)} %get-tuple-element.35), channel_id=1, replica_groups=mesh['lat'=16,'wave'=8] {'wave'}, dimensions={0} | all-to-all | bytes 655360 | tf_op jit(solution)/shard_map/all_to_all | solution.py:399
  55.5 3.5 %all-to-all-start.1 = ((bf16[8,80,512]{2,1,0:T(8,128)(2,1)}), bf16[8,80,512]{2,1,0:T(8,128)(2,1)S(1)}, u32[]{:S(2)}, u32[]{:S(2)}) async-start(bf16[8,80,512]{2,1,0:T(8,128)(2,1)} %get-tuple-element.37), calls=%async_computation.1 | async-start | bytes 1310720 | tf_op jit(solution)/shard_map/all_to_all | solution.py:400
  59.1 0.0 copy-done.4
  59.1 0.6 edges.1
  59.7 7.2 %collective-permute-start.12 = (bf16[64,640]{1,0:T(8,128)(2,1)S(1)}, bf16[64,640]{1,0:T(8,128)(2,1)S(1)}, u32[]{:S(2)}, u32[]{:S(2)}) collective-permute-start(bf16[64,640]{1,0:T(8,128)(2,1)S(1)} %get-tuple-element.39), channel_id=1, source_target_pairs={{8,0},{16,8},{24,16},{32,24},{40,32},{48,40},{56,48},{64,56},{72,6... | collective-permute-start | bytes 245768 | tf_op jit(solution)/shard_map/ppermute | solution.py:413
  66.9 1.9 %collective-permute-start.13 = (bf16[64,640]{1,0:T(8,128)(2,1)S(1)}, bf16[64,640]{1,0:T(8,128)(2,1)S(1)}, u32[]{:S(2)}, u32[]{:S(2)}) collective-permute-start(bf16[64,640]{1,0:T(8,128)(2,1)S(1)} %get-tuple-element.40), channel_id=1, source_target_pairs={{0,8},{8,16},{16,24},{24,32},{32,40},{40,48},{48,56},{56,64},{64,7... | collective-permute-start | bytes 245768 | tf_op jit(solution)/shard_map/ppermute | solution.py:414
  68.9 1.9 %all-to-all-done.1 = bf16[8,80,512]{2,1,0:T(8,128)(2,1)S(1)} async-done(((bf16[8,80,512]{2,1,0:T(8,128)(2,1)}), bf16[8,80,512]{2,1,0:T(8,128)(2,1)S(1)}, u32[]{:S(2)}, u32[]{:S(2)}) %all-to-all-start.1) | async-done | bytes 655392 | tf_op jit(solution)/shard_map/all_to_all | solution.py:400
  70.8 0.7 order.1.main_ref
  71.5 0.0 collective-permute-done.12.above_ref
  71.5 3.8 %collective-permute-done.13.below_ref = bf16[64,640]{1,0:T(8,128)(2,1)S(1)} collective-permute-done((bf16[64,640]{1,0:T(8,128)(2,1)S(1)}, bf16[64,640]{1,0:T(8,128)(2,1)S(1)}, u32[]{:S(2)}, u32[]{:S(2)}) %collective-permute-start.13) | collective-permute-done | bytes 81952 | tf_op jit(solution)/shard_map/ppermute | solution.py:414
  75.4 0.0 copy-done.1
  75.4 0.0 copy-done.2
  75.4 8.2 %synthesis.1 = bf16[2,160,5120]{2,1,0:T(8,128)(2,1)} custom-call(bf16[512,640]{1,0:T(8,128)(2,1)S(1)} %order.1.main_ref, bf16[128,640]{1,0:T(8,128)(2,1)S(1)} %get-tuple-element.38.rest_ref, bf16[64,640]{1,0:T(8,128)(2,1)S(1)} %collective-permute-done.12.above_ref, bf16[64,640]{1,0:T(8,128)(2,1)S(1)} %collective-permute-done.13.below_ref, ...), custom_call_target="tpu_custom_call" | custom-call | flops 2400000000 | bytes 11000000 | tf_op jit(solution)/shard_map/synthesis/pallas_call | solution.py:426
  (1 shorter events, 0.0 us)
Async XLA Ops:
  1.7 8.2 %collective-permute-start.3 = (bf16[40,768]{1,0:T(8,128)(2,1)}, bf16[40,768]{1,0:T(8,128)(2,1)S(1)}, u32[]{:S(2)}, u32[]{:S(2)}) collective-permute-start(bf16[40,768]{1,0:T(8,128)(2,1)} %get-tuple-element.24), channel_id=1, source_target_pairs={{0,32},{8,40},{16,48},{24,56},{32,64},{40,72},{48,80},{56,88},{64,... | collective-permute-start | bytes 184328 | tf_op jit(solution)/shard_map/ppermute | solution.py:355
  3.2 8.6 %collective-permute-start.4 = (bf16[40,768]{1,0:T(8,128)(2,1)}, bf16[40,768]{1,0:T(8,128)(2,1)S(1)}, u32[]{:S(2)}, u32[]{:S(2)}) collective-permute-start(bf16[40,768]{1,0:T(8,128)(2,1)} %get-tuple-element.24), channel_id=1, source_target_pairs={{0,96},{8,104},{16,112},{24,120},{32,0},{40,8},{48,16},{56,24},{64... | collective-permute-start | bytes 184328 | tf_op jit(solution)/shard_map/ppermute | solution.py:355
  3.7 8.0 %collective-permute-start.5 = (bf16[40,768]{1,0:T(8,128)(2,1)}, bf16[40,768]{1,0:T(8,128)(2,1)S(1)}, u32[]{:S(2)}, u32[]{:S(2)}) collective-permute-start(bf16[40,768]{1,0:T(8,128)(2,1)} %get-tuple-element.24), channel_id=1, source_target_pairs={{0,64},{8,72},{16,80},{24,88},{32,96},{40,104},{48,112},{56,120},{... | collective-permute-start | bytes 184328 | tf_op jit(solution)/shard_map/ppermute | solution.py:355
  5.9 6.8 %collective-permute-start = (bf16[40,768]{1,0:T(8,128)(2,1)}, bf16[40,768]{1,0:T(8,128)(2,1)S(1)}, u32[]{:S(2)}, u32[]{:S(2)}) collective-permute-start(bf16[40,768]{1,0:T(8,128)(2,1)} %get-tuple-element.23), channel_id=1, source_target_pairs={{0,8},{8,16},{16,24},{24,0},{32,40},{40,48},{48,56},{56,32},{64,72... | collective-permute-start | bytes 184328 | tf_op jit(solution)/shard_map/ppermute | solution.py:355
  7.8 4.9 %collective-permute-start.1 = (bf16[40,768]{1,0:T(8,128)(2,1)}, bf16[40,768]{1,0:T(8,128)(2,1)S(1)}, u32[]{:S(2)}, u32[]{:S(2)}) collective-permute-start(bf16[40,768]{1,0:T(8,128)(2,1)} %get-tuple-element.23), channel_id=1, source_target_pairs={{0,24},{8,0},{16,8},{24,16},{32,56},{40,32},{48,40},{56,48},{64,88... | collective-permute-start | bytes 184328 | tf_op jit(solution)/shard_map/ppermute | solution.py:355
  9.9 5.9 %collective-permute-start.2 = (bf16[40,768]{1,0:T(8,128)(2,1)}, bf16[40,768]{1,0:T(8,128)(2,1)S(1)}, u32[]{:S(2)}, u32[]{:S(2)}) collective-permute-start(bf16[40,768]{1,0:T(8,128)(2,1)} %get-tuple-element.23), channel_id=1, source_target_pairs={{0,16},{8,24},{16,0},{24,8},{32,48},{40,56},{48,32},{56,40},{64,80... | collective-permute-start | bytes 184328 | tf_op jit(solution)/shard_map/ppermute | solution.py:355
  16.7 11.0 %collective-permute-start.6 = (bf16[4,40,768]{2,1,0:T(8,128)(2,1)S(1)}, bf16[4,40,768]{2,1,0:T(8,128)(2,1)S(1)}, u32[]{:S(2)}, u32[]{:S(2)}) collective-permute-start(bf16[4,40,768]{2,1,0:T(8,128)(2,1)S(1)} %pad_maximum_fusion.refs_0_), channel_id=1, source_target_pairs={{0,32},{8,40},{16,48},{24,56},{32,64},{40,72},{48,80},{56,88},{64,... | collective-permute-start | bytes 737288 | tf_op jit(solution)/shard_map/ppermute | solution.py:376
  17.9 9.9 %collective-permute-start.8 = (bf16[4,40,768]{2,1,0:T(8,128)(2,1)S(1)}, bf16[4,40,768]{2,1,0:T(8,128)(2,1)S(1)}, u32[]{:S(2)}, u32[]{:S(2)}) collective-permute-start(bf16[4,40,768]{2,1,0:T(8,128)(2,1)S(1)} %pad_maximum_fusion.1.refs_4_), channel_id=1, source_target_pairs={{0,8},{8,16},{16,24},{24,0},{32,40},{40,48},{48,56},{56,32},{64,72... | collective-permute-start | bytes 737288 | tf_op jit(solution)/shard_map/ppermute | solution.py:376
  17.9 11.1 %collective-permute-start.10 = (bf16[4,40,768]{2,1,0:T(8,128)(2,1)S(1)}, bf16[4,40,768]{2,1,0:T(8,128)(2,1)S(1)}, u32[]{:S(2)}, u32[]{:S(2)}) collective-permute-start(bf16[4,40,768]{2,1,0:T(8,128)(2,1)S(1)} %pad_maximum_fusion.1.refs_4_), channel_id=1, source_target_pairs={{0,24},{8,0},{16,8},{24,16},{32,56},{40,32},{48,40},{56,48},{64,88... | collective-permute-start | bytes 737288 | tf_op jit(solution)/shard_map/ppermute | solution.py:376
  21.1 7.9 %collective-permute-start.7 = (bf16[4,40,768]{2,1,0:T(8,128)(2,1)S(1)}, bf16[4,40,768]{2,1,0:T(8,128)(2,1)S(1)}, u32[]{:S(2)}, u32[]{:S(2)}) collective-permute-start(bf16[4,40,768]{2,1,0:T(8,128)(2,1)S(1)} %pad_maximum_fusion.refs_0_), channel_id=1, source_target_pairs={{0,96},{8,104},{16,112},{24,120},{32,0},{40,8},{48,16},{56,24},{64... | collective-permute-start | bytes 737288 | tf_op jit(solution)/shard_map/ppermute | solution.py:376
  22.0 0.9 %copy-start = (bf16[3,160,256]{2,1,0:T(8,128)(2,1)S(1)}, bf16[3,160,256]{2,1,0:T(8,128)(2,1)}, u32[]{:S(2)}) copy-start(bf16[3,160,256]{2,1,0:T(8,128)(2,1)} %constant.8.clone.matrix_ref) | copy-start | bytes 737284
  23.0 0.7 copy-start.3
  23.7 0.7 copy-start.5
  27.7 7.5 %collective-permute-start.11 = (bf16[4,40,768]{2,1,0:T(8,128)(2,1)S(1)}, bf16[4,40,768]{2,1,0:T(8,128)(2,1)S(1)}, u32[]{:S(2)}, u32[]{:S(2)}) collective-permute-start(bf16[4,40,768]{2,1,0:T(8,128)(2,1)S(1)} %collective-permute-done.8.refs_5_), channel_id=1, source_target_pairs={{0,8},{8,16},{16,24},{24,0},{32,40},{40,48},{48,56},{56,32},{64,72... | collective-permute-start | bytes 737288 | tf_op jit(solution)/shard_map/ppermute | solution.py:381
  27.8 7.4 %collective-permute-start.9 = (bf16[4,40,768]{2,1,0:T(8,128)(2,1)S(1)}, bf16[4,40,768]{2,1,0:T(8,128)(2,1)S(1)}, u32[]{:S(2)}, u32[]{:S(2)}) collective-permute-start(bf16[4,40,768]{2,1,0:T(8,128)(2,1)S(1)} %collective-permute-done.6.refs_1_), channel_id=1, source_target_pairs={{0,32},{8,40},{16,48},{24,56},{32,64},{40,72},{48,80},{56,88},{64,... | collective-permute-start | bytes 737288 | tf_op jit(solution)/shard_map/ppermute | solution.py:381
  35.2 23.9 %copy-start.4 = (s32[640]{0:T(1024)S(1)}, s32[640]{0:T(1024)}, u32[]{:S(2)}) copy-start(s32[640]{0:T(1024)} %order_ref.3) | copy-start | bytes 7684
  35.2 40.2 %copy-start.1 = (bf16[640,128]{1,0:T(8,128)(2,1)S(1)}, bf16[640,128]{1,0:T(8,128)(2,1)}, u32[]{:S(2)}) copy-start(bf16[640,128]{1,0:T(8,128)(2,1)} %constant.10.clone.middle_ref) | copy-start | bytes 491524
  35.2 40.2 %copy-start.2 = (bf16[160,32]{1,0:T(8,128)(2,1)S(1)}, bf16[160,32]{1,0:T(8,128)(2,1)}, u32[]{:S(2)}) copy-start(bf16[160,32]{1,0:T(8,128)(2,1)} %constant.9.clone.expand_ref) | copy-start | bytes 30724
  55.5 15.2 %all-to-all-start.1 = ((bf16[8,80,512]{2,1,0:T(8,128)(2,1)}), bf16[8,80,512]{2,1,0:T(8,128)(2,1)S(1)}, u32[]{:S(2)}, u32[]{:S(2)}) async-start(bf16[8,80,512]{2,1,0:T(8,128)(2,1)} %get-tuple-element.37), calls=%async_computation.1 | async-start | bytes 1310720 | tf_op jit(solution)/shard_map/all_to_all | solution.py:400
  59.7 11.8 %collective-permute-start.12 = (bf16[64,640]{1,0:T(8,128)(2,1)S(1)}, bf16[64,640]{1,0:T(8,128)(2,1)S(1)}, u32[]{:S(2)}, u32[]{:S(2)}) collective-permute-start(bf16[64,640]{1,0:T(8,128)(2,1)S(1)} %get-tuple-element.39), channel_id=1, source_target_pairs={{8,0},{16,8},{24,16},{32,24},{40,32},{48,40},{56,48},{64,56},{72,6... | collective-permute-start | bytes 245768 | tf_op jit(solution)/shard_map/ppermute | solution.py:413
  66.9 8.4 %collective-permute-start.13 = (bf16[64,640]{1,0:T(8,128)(2,1)S(1)}, bf16[64,640]{1,0:T(8,128)(2,1)S(1)}, u32[]{:S(2)}, u32[]{:S(2)}) collective-permute-start(bf16[64,640]{1,0:T(8,128)(2,1)S(1)} %get-tuple-element.40), channel_id=1, source_target_pairs={{0,8},{8,16},{16,24},{24,32},{32,40},{40,48},{48,56},{56,64},{64,7... | collective-permute-start | bytes 245768 | tf_op jit(solution)/shard_map/ppermute | solution.py:414

commit v7 on v6

--- a/solution.py
+++ b/solution.py
@@ -27,7 +27,7 @@
 RANK = 16
 WIDTH = 4 * LANE + 4 * (BAND - LANE + 2 * RANK)
 TILE = 256
-STEPS = NLON // 2 // TILE
+STEPS = NLON // 4 // TILE
 GROUP = 4
 SMALL_BYTES = 16 * 2**20
 MIDDLE_BYTES = 40 * 2**20
@@ -58,17 +58,19 @@
 
 
 def longitude_matrices():
-    waves = np.arange(NWAVE)
+    waves = np.concatenate([np.arange(0, NWAVE, 2), np.arange(1, NWAVE, 2)])
     phase = waves[:, None] * np.arange(NLON)[None, :] % NLON
     angle = phase * (2.0 * math.pi / NLON)
     weight = np.where(waves == 0, 1.0, 2.0)[:, None] / math.sqrt(2.0 * NWAVE)
     table = np.concatenate([weight * np.cos(angle), -weight * np.sin(angle)], axis=0)
     table = table.astype(np.float32).astype(ml_dtypes.bfloat16).astype(np.float64)
-    lifted = analyze(table.T, WL, "wrap").T
-    half = lifted[:, : NLON // 2].reshape(2 * NWAVE, STEPS, TILE).swapaxes(0, 1)
-    middle = np.zeros((NWAVE, LANE))
-    middle[:, 0] = lifted[:NWAVE, NLON // 2]
-    return [values.astype(np.float32).astype(ml_dtypes.bfloat16) for values in (half, middle)]
+    cosine, sine = analyze(table.T, WL, "wrap").T.reshape(2, NWAVE, NLON)
+    half = NWAVE // 2
+    both = np.stack([np.concatenate([cosine[:half], sine[half:]]), np.concatenate([sine[:half], cosine[half:]])])
+    quarter = both[:, :, : NLON // 4].reshape(2, NWAVE, STEPS, TILE).transpose(2, 0, 1, 3)
+    middle = np.zeros((2, NWAVE, LANE))
+    middle[:, :, 0] = both[:, :, NLON // 4]
+    return [values.astype(np.float32).astype(ml_dtypes.bfloat16) for values in (quarter, middle)]
 
 
 def latitude_matrices():
@@ -102,14 +104,16 @@
 
 
 def pack_kernel(order_ref, spectra_ref, *refs):
-    outs, (wide, low, high, packed) = refs[:HALVES], refs[HALVES:]
+    out_ref, wide, low, high = refs
     first = lax.axis_index("wave") * SLOTS
     for pair in range(PAIRS):
         low[pl.ds(pair, 1), :] = jnp.full((1, LANE), order_ref[first + 2 * pair], jnp.int32)
         high[pl.ds(pair, 1), :] = jnp.full((1, LANE), order_ref[first + 2 * pair + 1], jnp.int32)
     waves_a, waves_b = low[...], high[...]
     lane = lax.broadcasted_iota(jnp.int32, (PAIRS, LANE), 1)
+    rows = []
     for part in range(2):
+        packed = []
         for block in range(5):
             wide[block] = spectra_ref[0, part, :, block * LANE : (block + 1) * LANE].astype(jnp.float32)
         for block in range(BLOCKS):
@@ -121,12 +125,9 @@
                 values = wide[block - 1, pl.ds(0, PAIRS, stride=2), :]
                 values = jnp.where(lane + (block - 1) * LANE >= waves_a, values, jnp.zeros_like(values))
                 taken = jnp.where(waves_a < block * LANE, values, taken)
-            for half in range(HALVES):
-                packed[half, pl.ds(part * PART_PAIRS, PART_PAIRS), block * LANE : (block + 1) * LANE] = taken[
-                    half * PART_PAIRS : (half + 1) * PART_PAIRS
-                ]
-    for half in range(HALVES):
-        outs[half][...] = packed[half].astype(jnp.bfloat16)
+            packed.append(taken)
+        rows.append(jnp.concatenate(packed, axis=1))
+    out_ref[...] = jnp.concatenate(rows, axis=0).astype(jnp.bfloat16)
 
 
 def fetch_kernel(order_ref, writer_ref, matrix_ref, legendre_ref, order_out, writer_out, matrix_out, held_out, sems):
@@ -145,9 +146,9 @@
 
 
 def legendre_kernel(order_ref, writer_ref, *refs):
-    parts = refs[: 4 * HALVES]
-    near_ref, legendre_ref, matrix, out_ref, tail_ref = refs[4 * HALVES : 4 * HALVES + 5]
-    spread, rows, results, rest, sems = refs[4 * HALVES + 5 :]
+    parts = refs[:8]
+    near_ref, legendre_ref, matrix, out_ref, tail_ref = refs[8:13]
+    spread, rows, results, rest, sems = refs[13:]
     held = (near_ref, rest)
     some = PART_SLOTS // 2
     copies = [
@@ -162,15 +163,15 @@
     band = lax.axis_index("lat")
     band_x, band_z = band // 4, lax.rem(band, 4)
     steps = (0, 3, 1, 2)
+    for outer in range(4):
+        for inner in range(4):
+            field = 4 * lax.rem(band_x + steps[outer], 4) + lax.rem(band_z + steps[inner], 4)
+            start = pl.multiple_of(field * 2 * PAIRS, 16)
+            for block in range(BLOCKS):
+                values = parts[2 * outer + inner // 2][inner % 2, :, block * LANE : (block + 1) * LANE]
+                spread[block, pl.ds(start, 2 * PAIRS), :] = values.astype(jnp.float32)
+
     for half in range(HALVES):
-        for outer in range(4):
-            for inner in range(4):
-                along_x, along_z = (outer, inner) if half == 0 else (inner, outer)
-                field = 4 * lax.rem(band_x + steps[along_x], 4) + lax.rem(band_z + steps[along_z], 4)
-                start = pl.multiple_of(field * 2 * PART_PAIRS, 8)
-                for block in range(BLOCKS):
-                    values = parts[4 * half + outer][inner, :, block * LANE : (block + 1) * LANE]
-                    spread[block, pl.ds(start, 2 * PART_PAIRS), :] = values.astype(jnp.float32)
 
         def contract(group, carry, half=half):
             for member in range(GROUP):
@@ -178,7 +179,7 @@
                 wave = order_ref[first + half * PART_SLOTS + 2 * pair]
                 lower, upper, values_of_n = [], [], []
                 for block in range(BLOCKS):
-                    values = spread[block, pl.ds(pair, 2 * FIELDS, stride=PART_PAIRS), :].astype(jnp.bfloat16)
+                    values = spread[block, pl.ds(half * PART_PAIRS + pair, 2 * FIELDS, stride=PAIRS), :].astype(jnp.bfloat16)
                     from_a = wave < block * LANE
                     slot = 2 * pair + jnp.where(from_a, 0, 1)
                     source = pl.multiple_of(jnp.where(from_a, block - 1, 4 - block) * LANE, LANE)
@@ -230,7 +231,8 @@
 
 def edge_kernel(order_ref, waves_ref, chosen_ref, rest_ref, above_ref, below_ref):
     row = lax.broadcasted_iota(jnp.int32, (NWAVE, NWAVE), 0)
-    chosen_ref[...] = jnp.where(row == order_ref[...], 1.0, 0.0).astype(jnp.bfloat16)
+    wave = jnp.where(row < NWAVE // 2, 2 * row, 2 * row + 1 - NWAVE)
+    chosen_ref[...] = jnp.where(wave == order_ref[...], 1.0, 0.0).astype(jnp.bfloat16)
     ordered = jnp.dot(chosen_ref[...], waves_ref[...], preferred_element_type=jnp.float32)
     turned = ordered.T.astype(jnp.bfloat16)
     rest = BAND - LANE
@@ -247,12 +249,15 @@
 
 
 def synthesis_kernel(main_ref, rest_ref, above_ref, below_ref, expand_ref, middle_ref, table_ref, out_ref, *refs):
-    left, table, tiles, even, flip, table_sems, out_sems = refs
+    left, table, tiles, ends, flip, table_sems, out_sems = refs
     tables = [pltpu.make_async_copy(table_ref.at[step], table.at[step], table_sems.at[step]) for step in range(STEPS)]
     for copy in reversed(tables):
         copy.start()
     rest = BAND - LANE
+    rows = 2 * BAND
+    low = lax.broadcasted_iota(jnp.int32, (BAND, NWAVE), 1) < NWAVE // 2
     for field in range(2):
+        summed = []
         for part in range(2):
             which = 2 * field + part
             edges = slice(which * RANK, (which + 1) * RANK)
@@ -261,13 +266,22 @@
                 jnp.concatenate([above_ref[edges], below_ref[edges]], axis=0),
                 preferred_element_type=jnp.float32,
             )
-            own = main_ref[which * LANE : (which + 1) * LANE].astype(jnp.float32)
-            left[part, field * BAND : field * BAND + LANE] = (own + added[:LANE]).astype(jnp.bfloat16)
-            own = rest_ref[which * rest : (which + 1) * rest].astype(jnp.float32)
-            left[part, field * BAND + LANE : (field + 1) * BAND] = (own + added[LANE:]).astype(jnp.bfloat16)
+            own = [main_ref[which * LANE : (which + 1) * LANE], rest_ref[which * rest : (which + 1) * rest]]
+            summed.append(jnp.concatenate(own, axis=0).astype(jnp.float32) + added)
+        cosine, sine = summed
+        for turned, value in enumerate((sine, -sine)):
+            picked = slice(turned * rows + field * BAND, turned * rows + (field + 1) * BAND)
+            left[0, picked] = jnp.where(low, cosine, value).astype(jnp.bfloat16)
+            left[1, picked] = jnp.where(low, value, cosine).astype(jnp.bfloat16)
     total = lax.broadcasted_iota(jnp.int32, (TILE, TILE), 0) + lax.broadcasted_iota(jnp.int32, (TILE, TILE), 1)
     flip[...] = jnp.where(total == TILE, 1.0, 0.0).astype(jnp.bfloat16)
-    even[...] = jnp.dot(left[0], middle_ref[...], preferred_element_type=jnp.float32)
+
+    def products(first, second):
+        a = jnp.dot(left[0], first, preferred_element_type=jnp.float32)
+        b = jnp.dot(left[1], second, preferred_element_type=jnp.float32)
+        return a[:rows] + b[:rows], a[:rows] - b[:rows], a[rows:] - b[rows:], a[rows:] + b[rows:]
+
+    _, ends[0], _, ends[1] = products(middle_ref[0], middle_ref[1])
 
     def place(tile, where):
         return [
@@ -279,31 +293,22 @@
             for field in range(2)
         ]
 
-    def step(count, carry):
-        tile = STEPS - 1 - count
-        pltpu.make_async_copy(table_ref.at[tile], table.at[tile], table_sems.at[tile]).wait()
-        cosine = jnp.dot(left[0], table[tile, :NWAVE], preferred_element_type=jnp.float32)
-        sine = jnp.dot(left[1], table[tile, NWAVE:], preferred_element_type=jnp.float32)
-        front = (cosine + sine).astype(jnp.bfloat16)
-        back = cosine - sine
-        turned = jnp.dot(back.astype(jnp.bfloat16), flip[...], preferred_element_type=jnp.float32)
-        lane = lax.broadcasted_iota(jnp.int32, (2 * BAND, LANE), 1)
-        mirror = 2 * STEPS - 1 - tile
-        head = jnp.where(lane == 0, even[...], turned[:, :LANE]).astype(jnp.bfloat16)
-        tail = turned[:, LANE:].astype(jnp.bfloat16)
-        even[...] = back[:, :LANE]
-        for field in range(2):
-            rows = slice(field * BAND, (field + 1) * BAND)
-            tiles[tile, field] = front[rows]
-            tiles[mirror, field, :, :LANE] = head[rows]
-            tiles[mirror, field, :, LANE:] = tail[rows]
-        for which in (tile, mirror):
-            for copy in place(which, pl.multiple_of(which * TILE, TILE)):
+    lane = lax.broadcasted_iota(jnp.int32, (rows, LANE), 1)
+    for tile in reversed(range(STEPS)):
+        tables[tile].wait()
+        east, back, south, west = products(table[tile, 0], table[tile, 1])
+        written = [(tile, east), (2 * STEPS + tile, south)]
+        for which, (values, target) in enumerate(((back, 2 * STEPS - 1 - tile), (west, 4 * STEPS - 1 - tile))):
+            turned = jnp.dot(values.astype(jnp.bfloat16), flip[...], preferred_element_type=jnp.float32)
+            head = jnp.where(lane == 0, ends[which], turned[:, :LANE])
+            ends[which] = values[:, :LANE]
+            written.append((target, jnp.concatenate([head, turned[:, LANE:]], axis=1)))
+        for target, values in written:
+            for field in range(2):
+                tiles[target, field] = values[field * BAND : (field + 1) * BAND].astype(jnp.bfloat16)
+            for copy in place(target, target * TILE):
                 copy.start()
-        return carry
-
-    lax.fori_loop(0, STEPS, step, 0)
-    for tile in range(2 * STEPS):
+    for tile in range(4 * STEPS):
         for copy in place(tile, tile * TILE):
             copy.wait()
 
@@ -335,25 +340,21 @@
 
 def make_on_device(table, middle, matrices, expand):
     def on_device(spectra, legendre, wave_order, writer_order):
-        halves = pl.pallas_call(
+        packed = pl.pallas_call(
             pack_kernel,
-            out_shape=[bf16(2 * PART_PAIRS, BLOCKS * LANE)] * HALVES,
+            out_shape=bf16(2 * PAIRS, BLOCKS * LANE),
             in_specs=[SMEM, VMEM],
-            out_specs=[VMEM] * HALVES,
+            out_specs=VMEM,
             scratch_shapes=[
                 pltpu.VMEM((5, SLOTS, LANE), jnp.float32),
                 pltpu.VMEM((PAIRS, LANE), jnp.int32),
                 pltpu.VMEM((PAIRS, LANE), jnp.int32),
-                pltpu.VMEM((HALVES, 2 * PART_PAIRS, BLOCKS * LANE), jnp.float32),
             ],
             name="pack",
         )(wave_order, spectra)
 
-        axes = ((along_z, along_x), (along_x, along_z))
-        firsts = []
-        for half, values in enumerate(halves):
-            sent = [lax.ppermute(values, "lat", axes[half][0](step)) for step in (1, 3, 2)]
-            firsts.append(jnp.stack([values] + sent))
+        below_z, above_z, across_z = [lax.ppermute(packed, "lat", along_z(step)) for step in (1, 3, 2)]
+        firsts = [jnp.stack([packed, below_z]), jnp.stack([above_z, across_z])]
         firsts, legendre = lax.optimization_barrier((firsts, legendre))
         orders, writers, matrix, near = pl.pallas_call(
             fetch_kernel,
@@ -370,23 +371,18 @@
             cost_estimate=pl.CostEstimate(flops=0, bytes_accessed=14_000_000, transcendentals=0),
             name="fetch",
         )(wave_order, writer_order, matrices, legendre)
-        parts, opposites = [], []
-        for half, values in enumerate(firsts):
-            along = axes[half][1]
-            before, after = [lax.ppermute(values, "lat", along(step)) for step in (1, 3)]
-            parts.append([values, before, after])
-            opposites.append(before)
-        opposites, near = lax.optimization_barrier((opposites, near))
-        for half in range(HALVES):
-            parts[half].append(lax.ppermute(opposites[half], "lat", axes[half][1](1)))
+        before = [lax.ppermute(values, "lat", along_x(1)) for values in firsts]
+        after = [lax.ppermute(values, "lat", along_x(3)) for values in firsts]
+        relayed, near = lax.optimization_barrier(((before[0], after[1]), near))
+        opposite = [lax.ppermute(relayed[0], "lat", along_x(1)), lax.ppermute(relayed[1], "lat", along_x(3))]
 
         lifted, tails = pl.pallas_call(
             legendre_kernel,
             out_shape=[bf16(OWNERS, SLOTS, 4 * LANE), bf16(OWNERS, SLOTS, WIDTH - 4 * LANE)],
-            in_specs=[SMEM, SMEM] + [VMEM] * (4 * HALVES) + [VMEM, ANY, VMEM],
+            in_specs=[SMEM, SMEM] + [VMEM] * 8 + [VMEM, ANY, VMEM],
             out_specs=[VMEM] * 2,
             scratch_shapes=[
-                pltpu.VMEM((BLOCKS, 2 * FIELDS * PART_PAIRS, LANE), jnp.float32),
+                pltpu.VMEM((BLOCKS, 2 * FIELDS * PAIRS, LANE), jnp.float32),
                 pltpu.VMEM((2, 2 * FIELDS * SLOTS, LANE), jnp.float32),
                 pltpu.VMEM((2, 2 * FIELDS * SLOTS, LANE), jnp.float32),
                 pltpu.VMEM((PART_SLOTS, BAND, NWAVE), jnp.bfloat16),
@@ -395,7 +391,7 @@
             compiler_params=MIDDLE,
             cost_estimate=pl.CostEstimate(flops=800_000_000, bytes_accessed=16_000_000, transcendentals=0),
             name="legendre",
-        )(orders, writers, *parts[0], *parts[1], near, legendre, matrix)
+        )(orders, writers, *firsts, *before, *after, *opposite, near, legendre, matrix)
         edges = lax.all_to_all(tails, "wave", split_axis=0, concat_axis=0, tiled=True)
         waves = lax.all_to_all(lifted, "wave", split_axis=0, concat_axis=0, tiled=True)
 
@@ -429,13 +425,13 @@
             in_specs=[VMEM] * 6 + [ANY],
             out_specs=ANY,
             scratch_shapes=[
-                pltpu.VMEM((2, 2 * BAND, NWAVE), jnp.bfloat16),
-                pltpu.VMEM((STEPS, 2 * NWAVE, TILE), jnp.bfloat16),
-                pltpu.VMEM((2 * STEPS, 2, BAND, TILE), jnp.bfloat16),
-                pltpu.VMEM((2 * BAND, LANE), jnp.float32),
+                pltpu.VMEM((2, 4 * BAND, NWAVE), jnp.bfloat16),
+                pltpu.VMEM((STEPS, 2, NWAVE, TILE), jnp.bfloat16),
+                pltpu.VMEM((4 * STEPS, 2, BAND, TILE), jnp.bfloat16),
+                pltpu.VMEM((2, 2 * BAND, LANE), jnp.float32),
                 pltpu.VMEM((TILE, TILE), jnp.bfloat16),
                 pltpu.SemaphoreType.DMA((STEPS,)),
-                pltpu.SemaphoreType.DMA((2 * STEPS, 2)),
+                pltpu.SemaphoreType.DMA((4 * STEPS, 2)),
             ],
             compiler_params=LARGE,
             cost_estimate=pl.CostEstimate(flops=2_400_000_000, bytes_accessed=11_000_000, transcendentals=0),

time: 84.4 us -> 79.4 us (0.941)
  the two profiles are of different devices: /device:TPU:2 before, /device:TPU:1 now
where the time goes in v7:
time: 79.4 us; the launch traced here: 79 us
  Pallas kernels  20.8 us (26%)
  starting transfers between devices  20.2 us (25%)
  waiting for transfers between devices  20 us (25%)
  blocking collectives  14.6 us (18%)
  local copies, waits for them, and re-layouts  2.3 us (3%)
  other arithmetic  0.95 us (1%)
    all_to_all x1, blocking collectives, on_device(): lax.all_to_all(tails, 'wave', split_axis=0, concat_axis=0, tiled=True)  14.6 us
    ppermute x3, waiting for transfers between devices, on_device(): lax.ppermute(packed, 'lat', along_z(step))  8.23 us
    pallas_call x1, Pallas kernels, on_device(): pl.pallas_call(legendre_kernel, out_shape=[bf16(OWNERS, SLOTS, 4 * LANE),...  7.95 us
    all_to_all x1, waiting for transfers between devices, on_device(): lax.all_to_all(lifted, 'wave', split_axis=0, concat_axis=0, tiled=True)  7.78 us
    pallas_call x1, Pallas kernels, on_device(): pl.pallas_call(synthesis_kernel, out_shape=bf16(2, BAND, NLON), in_specs=...  6.5 us
    ppermute x3, starting transfers between devices, on_device(): lax.ppermute(packed, 'lat', along_z(step))  5.29 us
    all_to_all x1, starting transfers between devices, on_device(): lax.all_to_all(lifted, 'wave', split_axis=0, concat_axis=0, tiled=True)  4.19 us
    ppermute x2, starting transfers between devices, on_device(): after = [lax.ppermute(values, 'lat', along_x(3)) for values in firsts]  4.14 us
  transfers between devices with their start and end apart: 12, of which 4 were waited for; matrix products, arithmetic and copies ran while one was open for 0% of the time, Pallas kernels for 6%

profile of v7, /device:TPU:1, one launch (start us, length us, event | category | flops | bytes accessed | tf_op | source)
XLA Modules:
  0.0 79.0 jit_solution(16679777806070267883)
XLA Ops:
  0.0 1.7 %pack.1 = bf16[80,768]{1,0:T(8,128)(2,1)} custom-call(s32[640]{0:T(1024)} %order_ref.3, bf16[1,2,80,640]{3,2,1,0:T(8,128)(2,1)} %spectra_ref.1), custom_call_target="tpu_custom_call" | custom-call | tf_op jit(solution)/shard_map/pack/pallas_call | solution.py:343
  1.7 4.6 %collective-permute-start.1 = (bf16[80,768]{1,0:T(8,128)(2,1)}, bf16[80,768]{1,0:T(8,128)(2,1)S(1)}, u32[]{:S(2)}, u32[]{:S(2)}) collective-permute-start(bf16[80,768]{1,0:T(8,128)(2,1)} %pack.1), channel_id=1, source_target_pairs={{0,24},{8,0},{16,8},{24,16},{32,56},{40,32},{48,40},{56,48},{64,88... | collective-permute-start | bytes 368648 | tf_op jit(solution)/shard_map/ppermute | solution.py:356
  6.3 0.0 collective-permute-start.2
  6.3 0.7 collective-permute-start
  7.0 4.9 %collective-permute-done.1 = bf16[80,768]{1,0:T(8,128)(2,1)S(1)} collective-permute-done((bf16[80,768]{1,0:T(8,128)(2,1)}, bf16[80,768]{1,0:T(8,128)(2,1)S(1)}, u32[]{:S(2)}, u32[]{:S(2)}) %collective-permute-start.1) | collective-permute-done | bytes 122912 | tf_op jit(solution)/shard_map/ppermute | solution.py:356
  11.8 0.0 collective-permute-done.2
  11.9 3.4 %collective-permute-done = bf16[80,768]{1,0:T(8,128)(2,1)S(1)} collective-permute-done((bf16[80,768]{1,0:T(8,128)(2,1)}, bf16[80,768]{1,0:T(8,128)(2,1)S(1)}, u32[]{:S(2)}, u32[]{:S(2)}) %collective-permute-start) | collective-permute-done | bytes 122912 | tf_op jit(solution)/shard_map/ppermute | solution.py:356
  15.2 0.9 %pad_maximum_fusion.refs_0_ = bf16[2,80,768]{2,1,0:T(8,128)(2,1)S(1)} fusion(bf16[1,80,768]{2,1,0:T(8,128)(2,1)S(1)} %bitcast.10, bf16[1,80,768]{2,1,0:T(8,128)(2,1)} %bitcast.8), kind=kLoop, calls=%fused_computation | loop fusion | flops 122880 | bytes 491520 | tf_op jit(solution)/shard_map/stack | solution.py:357
  16.2 1.3 %collective-permute-start.3 = (bf16[2,80,768]{2,1,0:T(8,128)(2,1)S(1)}, bf16[2,80,768]{2,1,0:T(8,128)(2,1)S(1)}, u32[]{:S(2)}, u32[]{:S(2)}) collective-permute-start(bf16[2,80,768]{2,1,0:T(8,128)(2,1)S(1)} %pad_maximum_fusion.refs_0_), channel_id=1, source_target_pairs={{0,32},{8,40},{16,48},{24,56},{32,64},{40,72},{48,80},{56,88},{64,... | collective-permute-start | bytes 737288 | tf_op jit(solution)/shard_map/ppermute | solution.py:374
  17.4 1.5 %collective-permute-start.6 = (bf16[2,80,768]{2,1,0:T(8,128)(2,1)S(1)}, bf16[2,80,768]{2,1,0:T(8,128)(2,1)S(1)}, u32[]{:S(2)}, u32[]{:S(2)}) collective-permute-start(bf16[2,80,768]{2,1,0:T(8,128)(2,1)S(1)} %pad_maximum_fusion.1.refs_1_), channel_id=1, source_target_pairs={{0,96},{8,104},{16,112},{24,120},{32,0},{40,8},{48,16},{56,24},{64... | collective-permute-start | bytes 737288 | tf_op jit(solution)/shard_map/ppermute | solution.py:375
  18.9 0.0 collective-permute-start.4
  18.9 2.7 %collective-permute-start.5 = (bf16[2,80,768]{2,1,0:T(8,128)(2,1)S(1)}, bf16[2,80,768]{2,1,0:T(8,128)(2,1)S(1)}, u32[]{:S(2)}, u32[]{:S(2)}) collective-permute-start(bf16[2,80,768]{2,1,0:T(8,128)(2,1)S(1)} %pad_maximum_fusion.refs_0_), channel_id=1, source_target_pairs={{0,96},{8,104},{16,112},{24,120},{32,0},{40,8},{48,16},{56,24},{64... | collective-permute-start | bytes 737288 | tf_op jit(solution)/shard_map/ppermute | solution.py:375
  21.6 0.0 copy-start
  21.6 0.9 %copy-done = bf16[3,160,256]{2,1,0:T(8,128)(2,1)S(1)} copy-done((bf16[3,160,256]{2,1,0:T(8,128)(2,1)S(1)}, bf16[3,160,256]{2,1,0:T(8,128)(2,1)}, u32[]{:S(2)}) %copy-start) | copy-done | bytes 245784
  22.5 0.0 copy-start.1
  22.5 0.7 copy-done.1
  23.2 0.0 copy-start.3
  23.2 0.7 copy-done.3
  23.9 3.4 %fetch.1 = (s32[640]{0:T(1024)S(1)}, s32[16]{0:T(128)S(1)}, bf16[160,256]{1,0:T(8,128)(2,1)S(1)}, bf16[40,160,640]{2,1,0:T(8,128)(2,1)S(1)}) custom-call(s32[640]{0:T(1024)S(1)} %copy-done.1, s32[16]{0:T(128)S(1)} %copy-done.3, bf16[3,160,256]{2,1,0:T(8,128)(2,1)S(1)} %copy-done, bf16[80,160,640]{2,1,0:T(8,128)(2,1)} %refs_9_), custom_call_target="tpu_custom_call" | custom-call | bytes 14000000 | tf_op jit(solution)/shard_map/fetch/pallas_call | solution.py:359
  27.2 0.0 collective-permute-done.3.refs_2_
  27.3 0.0 collective-permute-done.6.refs_5_
  27.3 0.1 collective-permute-start.7
  27.3 2.7 %collective-permute-start.8 = (bf16[2,80,768]{2,1,0:T(8,128)(2,1)S(1)}, bf16[2,80,768]{2,1,0:T(8,128)(2,1)S(1)}, u32[]{:S(2)}, u32[]{:S(2)}) collective-permute-start(bf16[2,80,768]{2,1,0:T(8,128)(2,1)S(1)} %collective-permute-done.6.refs_5_), channel_id=1, source_target_pairs={{0,96},{8,104},{16,112},{24,120},{32,0},{40,8},{48,16},{56,24},{64... | collective-permute-start | bytes 737288 | tf_op jit(solution)/shard_map/ppermute | solution.py:377
  30.0 0.0 collective-permute-done.4.refs_3_
  30.0 0.0 collective-permute-done.5.refs_4_
  30.0 4.0 %collective-permute-done.7.refs_6_ = bf16[2,80,768]{2,1,0:T(8,128)(2,1)S(1)} collective-permute-done((bf16[2,80,768]{2,1,0:T(8,128)(2,1)S(1)}, bf16[2,80,768]{2,1,0:T(8,128)(2,1)S(1)}, u32[]{:S(2)}, u32[]{:S(2)}) %collective-permute-start.7) | collective-permute-done | bytes 245792 | tf_op jit(solution)/shard_map/ppermute | solution.py:377
  34.0 0.0 collective-permute-done.8.refs_7_
  34.0 0.0 copy-start.2
  34.0 0.0 copy-start.4
  34.0 0.0 copy-start.5
  34.0 8.0 %legendre.1 = (bf16[8,80,512]{2,1,0:T(8,128)(2,1)}, bf16[8,80,256]{2,1,0:T(8,128)(2,1)S(1)}) custom-call(s32[640]{0:T(1024)S(1)} %get-tuple-element.22.order_ref, s32[16]{0:T(128)S(1)} %get-tuple-element.23.writer_ref, bf16[2,80,768]{2,1,0:T(8,128)(2,1)S(1)} %pad_maximum_fusion.refs_0_, bf16[2,80,768]{2,1,0:T(8,128)(2,1)S(1)} %pad_maximum_fusion.1.refs_1_, ...), custom_call_target="tpu_custom_call" | custom-call | flops 800000000 | bytes 16000000 | tf_op jit(solution)/shard_map/legendre/pallas_call | solution.py:379
  42.0 14.6 %all_to_all.10 = bf16[8,80,256]{2,1,0:T(8,128)(2,1)S(1)} all-to-all(bf16[8,80,256]{2,1,0:T(8,128)(2,1)S(1)} %get-tuple-element.31), channel_id=1, replica_groups=mesh['lat'=16,'wave'=8] {'wave'}, dimensions={0} | all-to-all | bytes 655360 | tf_op jit(solution)/shard_map/all_to_all | solution.py:395
  56.7 4.2 %all-to-all-start.1 = ((bf16[8,80,512]{2,1,0:T(8,128)(2,1)}), bf16[8,80,512]{2,1,0:T(8,128)(2,1)S(1)}, u32[]{:S(2)}, u32[]{:S(2)}) async-start(bf16[8,80,512]{2,1,0:T(8,128)(2,1)} %get-tuple-element.33), calls=%async_computation.1 | async-start | bytes 1310720 | tf_op jit(solution)/shard_map/all_to_all | solution.py:396
  60.8 0.0 copy-done.2
  60.9 0.5 edges.1
  61.4 1.3 %collective-permute-start.10 = (bf16[64,640]{1,0:T(8,128)(2,1)S(1)}, bf16[64,640]{1,0:T(8,128)(2,1)S(1)}, u32[]{:S(2)}, u32[]{:S(2)}) collective-permute-start(bf16[64,640]{1,0:T(8,128)(2,1)S(1)} %get-tuple-element.36), channel_id=1, source_target_pairs={{0,8},{8,16},{16,24},{24,32},{32,40},{40,48},{48,56},{56,64},{64,7... | collective-permute-start | bytes 245768 | tf_op jit(solution)/shard_map/ppermute | solution.py:410
  62.7 1.3 %collective-permute-start.9 = (bf16[64,640]{1,0:T(8,128)(2,1)S(1)}, bf16[64,640]{1,0:T(8,128)(2,1)S(1)}, u32[]{:S(2)}, u32[]{:S(2)}) collective-permute-start(bf16[64,640]{1,0:T(8,128)(2,1)S(1)} %get-tuple-element.35), channel_id=1, source_target_pairs={{8,0},{16,8},{24,16},{32,24},{40,32},{48,40},{56,48},{64,56},{72,6... | collective-permute-start | bytes 245768 | tf_op jit(solution)/shard_map/ppermute | solution.py:409
  64.0 7.8 %all-to-all-done.1 = bf16[8,80,512]{2,1,0:T(8,128)(2,1)S(1)} async-done(((bf16[8,80,512]{2,1,0:T(8,128)(2,1)}), bf16[8,80,512]{2,1,0:T(8,128)(2,1)S(1)}, u32[]{:S(2)}, u32[]{:S(2)}) %all-to-all-start.1) | async-done | bytes 655392 | tf_op jit(solution)/shard_map/all_to_all | solution.py:396
  71.7 0.7 order.1.main_ref
  72.5 0.0 collective-permute-done.10.below_ref
  72.5 0.0 collective-permute-done.9.above_ref
  72.5 0.0 copy-done.4
  72.5 0.0 copy-done.5
  72.5 6.5 %synthesis.1 = bf16[2,160,5120]{2,1,0:T(8,128)(2,1)} custom-call(bf16[512,640]{1,0:T(8,128)(2,1)S(1)} %order.1.main_ref, bf16[128,640]{1,0:T(8,128)(2,1)S(1)} %get-tuple-element.34.rest_ref, bf16[64,640]{1,0:T(8,128)(2,1)S(1)} %collective-permute-done.9.above_ref, bf16[64,640]{1,0:T(8,128)(2,1)S(1)} %collective-permute-done.10.below_ref, ...), custom_call_target="tpu_custom_call" | custom-call | flops 2400000000 | bytes 11000000 | tf_op jit(solution)/shard_map/synthesis/pallas_call | solution.py:422
  (2 shorter events, 0.0 us)
Async XLA Ops:
  1.7 10.1 %collective-permute-start.1 = (bf16[80,768]{1,0:T(8,128)(2,1)}, bf16[80,768]{1,0:T(8,128)(2,1)S(1)}, u32[]{:S(2)}, u32[]{:S(2)}) collective-permute-start(bf16[80,768]{1,0:T(8,128)(2,1)} %pack.1), channel_id=1, source_target_pairs={{0,24},{8,0},{16,8},{24,16},{32,56},{40,32},{48,40},{56,48},{64,88... | collective-permute-start | bytes 368648 | tf_op jit(solution)/shard_map/ppermute | solution.py:356
  6.3 5.6 %collective-permute-start.2 = (bf16[80,768]{1,0:T(8,128)(2,1)}, bf16[80,768]{1,0:T(8,128)(2,1)S(1)}, u32[]{:S(2)}, u32[]{:S(2)}) collective-permute-start(bf16[80,768]{1,0:T(8,128)(2,1)} %pack.1), channel_id=1, source_target_pairs={{0,16},{8,24},{16,0},{24,8},{32,48},{40,56},{48,32},{56,40},{64,80... | collective-permute-start | bytes 368648 | tf_op jit(solution)/shard_map/ppermute | solution.py:356
  6.3 9.0 %collective-permute-start = (bf16[80,768]{1,0:T(8,128)(2,1)}, bf16[80,768]{1,0:T(8,128)(2,1)S(1)}, u32[]{:S(2)}, u32[]{:S(2)}) collective-permute-start(bf16[80,768]{1,0:T(8,128)(2,1)} %pack.1), channel_id=1, source_target_pairs={{0,8},{8,16},{16,24},{24,0},{32,40},{40,48},{48,56},{56,32},{64,72... | collective-permute-start | bytes 368648 | tf_op jit(solution)/shard_map/ppermute | solution.py:356
  16.2 11.1 %collective-permute-start.3 = (bf16[2,80,768]{2,1,0:T(8,128)(2,1)S(1)}, bf16[2,80,768]{2,1,0:T(8,128)(2,1)S(1)}, u32[]{:S(2)}, u32[]{:S(2)}) collective-permute-start(bf16[2,80,768]{2,1,0:T(8,128)(2,1)S(1)} %pad_maximum_fusion.refs_0_), channel_id=1, source_target_pairs={{0,32},{8,40},{16,48},{24,56},{32,64},{40,72},{48,80},{56,88},{64,... | collective-permute-start | bytes 737288 | tf_op jit(solution)/shard_map/ppermute | solution.py:374
  17.4 9.8 %collective-permute-start.6 = (bf16[2,80,768]{2,1,0:T(8,128)(2,1)S(1)}, bf16[2,80,768]{2,1,0:T(8,128)(2,1)S(1)}, u32[]{:S(2)}, u32[]{:S(2)}) collective-permute-start(bf16[2,80,768]{2,1,0:T(8,128)(2,1)S(1)} %pad_maximum_fusion.1.refs_1_), channel_id=1, source_target_pairs={{0,96},{8,104},{16,112},{24,120},{32,0},{40,8},{48,16},{56,24},{64... | collective-permute-start | bytes 737288 | tf_op jit(solution)/shard_map/ppermute | solution.py:375
  18.9 11.1 %collective-permute-start.4 = (bf16[2,80,768]{2,1,0:T(8,128)(2,1)S(1)}, bf16[2,80,768]{2,1,0:T(8,128)(2,1)S(1)}, u32[]{:S(2)}, u32[]{:S(2)}) collective-permute-start(bf16[2,80,768]{2,1,0:T(8,128)(2,1)S(1)} %pad_maximum_fusion.1.refs_1_), channel_id=1, source_target_pairs={{0,32},{8,40},{16,48},{24,56},{32,64},{40,72},{48,80},{56,88},{64,... | collective-permute-start | bytes 737288 | tf_op jit(solution)/shard_map/ppermute | solution.py:374
  18.9 11.1 %collective-permute-start.5 = (bf16[2,80,768]{2,1,0:T(8,128)(2,1)S(1)}, bf16[2,80,768]{2,1,0:T(8,128)(2,1)S(1)}, u32[]{:S(2)}, u32[]{:S(2)}) collective-permute-start(bf16[2,80,768]{2,1,0:T(8,128)(2,1)S(1)} %pad_maximum_fusion.refs_0_), channel_id=1, source_target_pairs={{0,96},{8,104},{16,112},{24,120},{32,0},{40,8},{48,16},{56,24},{64... | collective-permute-start | bytes 737288 | tf_op jit(solution)/shard_map/ppermute | solution.py:375
  21.6 0.9 %copy-start = (bf16[3,160,256]{2,1,0:T(8,128)(2,1)S(1)}, bf16[3,160,256]{2,1,0:T(8,128)(2,1)}, u32[]{:S(2)}) copy-start(bf16[3,160,256]{2,1,0:T(8,128)(2,1)} %constant.8.clone.matrix_ref) | copy-start | bytes 737284
  22.5 0.7 copy-start.1
  23.2 0.7 copy-start.3
  27.3 6.8 %collective-permute-start.7 = (bf16[2,80,768]{2,1,0:T(8,128)(2,1)S(1)}, bf16[2,80,768]{2,1,0:T(8,128)(2,1)S(1)}, u32[]{:S(2)}, u32[]{:S(2)}) collective-permute-start(bf16[2,80,768]{2,1,0:T(8,128)(2,1)S(1)} %collective-permute-done.3.refs_2_), channel_id=1, source_target_pairs={{0,32},{8,40},{16,48},{24,56},{32,64},{40,72},{48,80},{56,88},{64,... | collective-permute-start | bytes 737288 | tf_op jit(solution)/shard_map/ppermute | solution.py:377
  27.3 6.7 %collective-permute-start.8 = (bf16[2,80,768]{2,1,0:T(8,128)(2,1)S(1)}, bf16[2,80,768]{2,1,0:T(8,128)(2,1)S(1)}, u32[]{:S(2)}, u32[]{:S(2)}) collective-permute-start(bf16[2,80,768]{2,1,0:T(8,128)(2,1)S(1)} %collective-permute-done.6.refs_5_), channel_id=1, source_target_pairs={{0,96},{8,104},{16,112},{24,120},{32,0},{40,8},{48,16},{56,24},{64... | collective-permute-start | bytes 737288 | tf_op jit(solution)/shard_map/ppermute | solution.py:377
  34.0 26.8 %copy-start.2 = (s32[640]{0:T(1024)S(1)}, s32[640]{0:T(1024)}, u32[]{:S(2)}) copy-start(s32[640]{0:T(1024)} %order_ref.3) | copy-start | bytes 7684
  34.0 38.5 %copy-start.4 = (bf16[2,640,128]{2,1,0:T(8,128)(2,1)S(1)}, bf16[2,640,128]{2,1,0:T(8,128)(2,1)}, u32[]{:S(2)}) copy-start(bf16[2,640,128]{2,1,0:T(8,128)(2,1)} %constant.10.clone.middle_ref) | copy-start | bytes 983044
  34.0 38.5 %copy-start.5 = (bf16[160,32]{1,0:T(8,128)(2,1)S(1)}, bf16[160,32]{1,0:T(8,128)(2,1)}, u32[]{:S(2)}) copy-start(bf16[160,32]{1,0:T(8,128)(2,1)} %constant.9.clone.expand_ref) | copy-start | bytes 30724
  56.7 15.1 %all-to-all-start.1 = ((bf16[8,80,512]{2,1,0:T(8,128)(2,1)}), bf16[8,80,512]{2,1,0:T(8,128)(2,1)S(1)}, u32[]{:S(2)}, u32[]{:S(2)}) async-start(bf16[8,80,512]{2,1,0:T(8,128)(2,1)} %get-tuple-element.33), calls=%async_computation.1 | async-start | bytes 1310720 | tf_op jit(solution)/shard_map/all_to_all | solution.py:396
  61.4 11.1 %collective-permute-start.10 = (bf16[64,640]{1,0:T(8,128)(2,1)S(1)}, bf16[64,640]{1,0:T(8,128)(2,1)S(1)}, u32[]{:S(2)}, u32[]{:S(2)}) collective-permute-start(bf16[64,640]{1,0:T(8,128)(2,1)S(1)} %get-tuple-element.36), channel_id=1, source_target_pairs={{0,8},{8,16},{16,24},{24,32},{32,40},{40,48},{48,56},{56,64},{64,7... | collective-permute-start | bytes 245768 | tf_op jit(solution)/shard_map/ppermute | solution.py:410
  62.7 9.8 %collective-permute-start.9 = (bf16[64,640]{1,0:T(8,128)(2,1)S(1)}, bf16[64,640]{1,0:T(8,128)(2,1)S(1)}, u32[]{:S(2)}, u32[]{:S(2)}) collective-permute-start(bf16[64,640]{1,0:T(8,128)(2,1)S(1)} %get-tuple-element.35), channel_id=1, source_target_pairs={{8,0},{16,8},{24,16},{32,24},{40,32},{48,40},{56,48},{64,56},{72,6... | collective-permute-start | bytes 245768 | tf_op jit(solution)/shard_map/ppermute | solution.py:409

commit v8 on v7

--- a/solution.py
+++ b/solution.py
@@ -28,7 +28,7 @@
 WIDTH = 4 * LANE + 4 * (BAND - LANE + 2 * RANK)
 TILE = 256
 STEPS = NLON // 4 // TILE
-GROUP = 4
+GROUP = 10
 SMALL_BYTES = 16 * 2**20
 MIDDLE_BYTES = 40 * 2**20
 FETCH_BYTES = 44 * 2**20
@@ -130,19 +130,24 @@
     out_ref[...] = jnp.concatenate(rows, axis=0).astype(jnp.bfloat16)
 
 
-def fetch_kernel(order_ref, writer_ref, matrix_ref, legendre_ref, order_out, writer_out, matrix_out, held_out, sems):
+def hand_kernel(order_ref, writer_ref, matrix_ref, order_out, writer_out, matrix_out, sems):
     band = lax.axis_index("lat")
     variant = jnp.where(band == 0, 0, jnp.where(band == BANDS - 1, 2, 1))
     copies = [
-        pltpu.make_async_copy(legendre_ref.at[pl.ds(0, PART_SLOTS)], held_out, sems.at[0]),
-        pltpu.make_async_copy(order_ref, order_out, sems.at[1]),
-        pltpu.make_async_copy(writer_ref, writer_out, sems.at[2]),
-        pltpu.make_async_copy(matrix_ref.at[variant], matrix_out, sems.at[3]),
+        pltpu.make_async_copy(order_ref, order_out, sems.at[0]),
+        pltpu.make_async_copy(writer_ref, writer_out, sems.at[1]),
+        pltpu.make_async_copy(matrix_ref.at[variant], matrix_out, sems.at[2]),
     ]
     for copy in copies:
         copy.start()
     for copy in copies:
         copy.wait()
+
+
+def fetch_kernel(legendre_ref, held_out, sem):
+    copy = pltpu.make_async_copy(legendre_ref.at[pl.ds(0, PART_SLOTS)], held_out, sem)
+    copy.start()
+    copy.wait()
 
 
 def legendre_kernel(order_ref, writer_ref, *refs):
@@ -355,22 +360,32 @@
 
         below_z, above_z, across_z = [lax.ppermute(packed, "lat", along_z(step)) for step in (1, 3, 2)]
         firsts = [jnp.stack([packed, below_z]), jnp.stack([above_z, across_z])]
-        firsts, legendre = lax.optimization_barrier((firsts, legendre))
-        orders, writers, matrix, near = pl.pallas_call(
-            fetch_kernel,
+        small = pl.pallas_call(
+            hand_kernel,
             out_shape=[
                 jax.ShapeDtypeStruct((NWAVE,), jnp.int32),
                 jax.ShapeDtypeStruct((FIELDS,), jnp.int32),
                 bf16(BAND, 2 * LANE),
-                bf16(PART_SLOTS, BAND, NWAVE),
             ],
-            in_specs=[ANY] * 4,
-            out_specs=[ANY] * 3 + [VMEM],
-            scratch_shapes=[pltpu.SemaphoreType.DMA((4,))],
+            in_specs=[ANY] * 3,
+            out_specs=[ANY] * 3,
+            scratch_shapes=[pltpu.SemaphoreType.DMA((3,))],
+            compiler_params=FETCH,
+            cost_estimate=pl.CostEstimate(flops=0, bytes_accessed=6_000_000, transcendentals=0),
+            name="hand",
+        )(wave_order, writer_order, matrices)
+        firsts, legendre, small = lax.optimization_barrier((firsts, legendre, small))
+        orders, writers, matrix = small
+        near = pl.pallas_call(
+            fetch_kernel,
+            out_shape=bf16(PART_SLOTS, BAND, NWAVE),
+            in_specs=[ANY],
+            out_specs=VMEM,
+            scratch_shapes=[pltpu.SemaphoreType.DMA],
             compiler_params=FETCH,
             cost_estimate=pl.CostEstimate(flops=0, bytes_accessed=14_000_000, transcendentals=0),
             name="fetch",
-        )(wave_order, writer_order, matrices, legendre)
+        )(legendre)
         before = [lax.ppermute(values, "lat", along_x(1)) for values in firsts]
         after = [lax.ppermute(values, "lat", along_x(3)) for values in firsts]
         relayed, near = lax.optimization_barrier(((before[0], after[1]), near))

time: 79.4 us -> 78.4 us (0.987)
  the two profiles are of different devices: /device:TPU:1 before, /device:TPU:2 now
where the time goes in v8:
time: 78.4 us; the launch traced here: 77.4 us
  starting transfers between devices  23 us (29%)
  Pallas kernels  20.4 us (26%)
  waiting for transfers between devices  18.1 us (23%)
  blocking collectives  12.5 us (16%)
  local copies, waits for them, and re-layouts  2.31 us (3%)
  other arithmetic  0.95 us (1%)
    all_to_all x1, blocking collectives, on_device(): lax.all_to_all(tails, 'wave', split_axis=0, concat_axis=0, tiled=True)  12.5 us
    pallas_call x1, Pallas kernels, on_device(): pl.pallas_call(legendre_kernel, out_shape=[bf16(OWNERS, SLOTS, 4 * LANE),...  7.52 us
    pallas_call x1, Pallas kernels, on_device(): pl.pallas_call(synthesis_kernel, out_shape=bf16(2, BAND, NLON), in_specs=...  6.49 us
    ppermute x1, starting transfers between devices, on_device(): above = lax.ppermute(above, 'lat', neighbour(-1))  6.06 us
    ppermute x3, starting transfers between devices, on_device(): lax.ppermute(packed, 'lat', along_z(step))  5.3 us
    ppermute x3, waiting for transfers between devices, on_device(): lax.ppermute(packed, 'lat', along_z(step))  5.14 us
    all_to_all x1, starting transfers between devices, on_device(): lax.all_to_all(lifted, 'wave', split_axis=0, concat_axis=0, tiled=True)  3.54 us
    pallas_call x1, Pallas kernels, on_device(): pl.pallas_call(fetch_kernel, out_shape=bf16(PART_SLOTS, BAND, NWAVE), in_...  3.33 us
  transfers between devices with their start and end apart: 12, of which 10 were waited for; matrix products, arithmetic and copies ran while one was open for 0% of the time, Pallas kernels for 6%

profile of v8, /device:TPU:2, one launch (start us, length us, event | category | flops | bytes accessed | tf_op | source)
XLA Modules:
  0.0 77.4 jit_solution(9036609996258078230)
XLA Ops:
  0.0 1.7 %pack.1 = bf16[80,768]{1,0:T(8,128)(2,1)} custom-call(s32[640]{0:T(1024)} %order_ref.3, bf16[1,2,80,640]{3,2,1,0:T(8,128)(2,1)} %spectra_ref.1), custom_call_target="tpu_custom_call" | custom-call | tf_op jit(solution)/shard_map/pack/pallas_call | solution.py:348
  1.7 4.0 %collective-permute-start.1 = (bf16[80,768]{1,0:T(8,128)(2,1)}, bf16[80,768]{1,0:T(8,128)(2,1)S(1)}, u32[]{:S(2)}, u32[]{:S(2)}) collective-permute-start(bf16[80,768]{1,0:T(8,128)(2,1)} %pack.1), channel_id=1, source_target_pairs={{0,24},{8,0},{16,8},{24,16},{32,56},{40,32},{48,40},{56,48},{64,88... | collective-permute-start | bytes 368648 | tf_op jit(solution)/shard_map/ppermute | solution.py:361
  5.7 0.0 collective-permute-start.2
  5.7 1.3 %collective-permute-start = (bf16[80,768]{1,0:T(8,128)(2,1)}, bf16[80,768]{1,0:T(8,128)(2,1)S(1)}, u32[]{:S(2)}, u32[]{:S(2)}) collective-permute-start(bf16[80,768]{1,0:T(8,128)(2,1)} %pack.1), channel_id=1, source_target_pairs={{0,8},{8,16},{16,24},{24,0},{32,40},{40,48},{48,56},{56,32},{64,72... | collective-permute-start | bytes 368648 | tf_op jit(solution)/shard_map/ppermute | solution.py:361
  7.0 0.0 copy-start
  7.0 0.9 %copy-done = bf16[3,160,256]{2,1,0:T(8,128)(2,1)S(1)} copy-done((bf16[3,160,256]{2,1,0:T(8,128)(2,1)S(1)}, bf16[3,160,256]{2,1,0:T(8,128)(2,1)}, u32[]{:S(2)}) %copy-start) | copy-done | bytes 245784
  7.9 0.0 copy-start.1
  7.9 0.7 copy-done.1
  8.6 0.0 copy-start.3
  8.6 0.7 copy-done.3
  9.3 0.1 hand.1
  9.4 1.9 %collective-permute-done.1 = bf16[80,768]{1,0:T(8,128)(2,1)S(1)} collective-permute-done((bf16[80,768]{1,0:T(8,128)(2,1)}, bf16[80,768]{1,0:T(8,128)(2,1)S(1)}, u32[]{:S(2)}, u32[]{:S(2)}) %collective-permute-start.1) | collective-permute-done | bytes 122912 | tf_op jit(solution)/shard_map/ppermute | solution.py:361
  11.3 2.3 %collective-permute-done.2 = bf16[80,768]{1,0:T(8,128)(2,1)S(1)} collective-permute-done((bf16[80,768]{1,0:T(8,128)(2,1)}, bf16[80,768]{1,0:T(8,128)(2,1)S(1)}, u32[]{:S(2)}, u32[]{:S(2)}) %collective-permute-start.2) | collective-permute-done | bytes 122912 | tf_op jit(solution)/shard_map/ppermute | solution.py:361
  13.6 0.9 %collective-permute-done = bf16[80,768]{1,0:T(8,128)(2,1)S(1)} collective-permute-done((bf16[80,768]{1,0:T(8,128)(2,1)}, bf16[80,768]{1,0:T(8,128)(2,1)S(1)}, u32[]{:S(2)}, u32[]{:S(2)}) %collective-permute-start) | collective-permute-done | bytes 122912 | tf_op jit(solution)/shard_map/ppermute | solution.py:361
  14.6 0.9 %pad_maximum_fusion.refs_0_ = bf16[2,80,768]{2,1,0:T(8,128)(2,1)S(1)} fusion(bf16[1,80,768]{2,1,0:T(8,128)(2,1)S(1)} %bitcast.10, bf16[1,80,768]{2,1,0:T(8,128)(2,1)} %bitcast.8), kind=kLoop, calls=%fused_computation | loop fusion | flops 122880 | bytes 491520 | tf_op jit(solution)/shard_map/stack | solution.py:362
  15.5 1.6 %collective-permute-start.3 = (bf16[2,80,768]{2,1,0:T(8,128)(2,1)S(1)}, bf16[2,80,768]{2,1,0:T(8,128)(2,1)S(1)}, u32[]{:S(2)}, u32[]{:S(2)}) collective-permute-start(bf16[2,80,768]{2,1,0:T(8,128)(2,1)S(1)} %pad_maximum_fusion.refs_0_), channel_id=1, source_target_pairs={{0,32},{8,40},{16,48},{24,56},{32,64},{40,72},{48,80},{56,88},{64,... | collective-permute-start | bytes 737288 | tf_op jit(solution)/shard_map/ppermute | solution.py:389
  17.1 0.5 collective-permute-start.6
  17.6 1.5 %collective-permute-start.4 = (bf16[2,80,768]{2,1,0:T(8,128)(2,1)S(1)}, bf16[2,80,768]{2,1,0:T(8,128)(2,1)S(1)}, u32[]{:S(2)}, u32[]{:S(2)}) collective-permute-start(bf16[2,80,768]{2,1,0:T(8,128)(2,1)S(1)} %pad_maximum_fusion.1.refs_1_), channel_id=1, source_target_pairs={{0,32},{8,40},{16,48},{24,56},{32,64},{40,72},{48,80},{56,88},{64,... | collective-permute-start | bytes 737288 | tf_op jit(solution)/shard_map/ppermute | solution.py:389
  19.1 0.5 collective-permute-start.5
  19.6 3.3 %fetch.1.refs_8_ = bf16[40,160,640]{2,1,0:T(8,128)(2,1)S(1)} custom-call(bf16[80,160,640]{2,1,0:T(8,128)(2,1)} %refs_9_), custom_call_target="tpu_custom_call" | custom-call | bytes 14000000 | tf_op jit(solution)/shard_map/fetch/pallas_call | solution.py:379
  23.0 0.0 copy-start.2
  23.0 0.0 copy-start.4
  23.0 0.0 copy-start.5
  23.0 1.4 %collective-permute-done.3.refs_2_ = bf16[2,80,768]{2,1,0:T(8,128)(2,1)S(1)} collective-permute-done((bf16[2,80,768]{2,1,0:T(8,128)(2,1)S(1)}, bf16[2,80,768]{2,1,0:T(8,128)(2,1)S(1)}, u32[]{:S(2)}, u32[]{:S(2)}) %collective-permute-start.3) | collective-permute-done | bytes 245792 | tf_op jit(solution)/shard_map/ppermute | solution.py:389
  24.4 1.5 %collective-permute-done.6.refs_5_ = bf16[2,80,768]{2,1,0:T(8,128)(2,1)S(1)} collective-permute-done((bf16[2,80,768]{2,1,0:T(8,128)(2,1)S(1)}, bf16[2,80,768]{2,1,0:T(8,128)(2,1)S(1)}, u32[]{:S(2)}, u32[]{:S(2)}) %collective-permute-start.6) | collective-permute-done | bytes 245792 | tf_op jit(solution)/shard_map/ppermute | solution.py:390
  25.9 1.2 %collective-permute-start.7 = (bf16[2,80,768]{2,1,0:T(8,128)(2,1)S(1)}, bf16[2,80,768]{2,1,0:T(8,128)(2,1)S(1)}, u32[]{:S(2)}, u32[]{:S(2)}) collective-permute-start(bf16[2,80,768]{2,1,0:T(8,128)(2,1)S(1)} %collective-permute-done.3.refs_2_), channel_id=1, source_target_pairs={{0,32},{8,40},{16,48},{24,56},{32,64},{40,72},{48,80},{56,88},{64,... | collective-permute-start | bytes 737288 | tf_op jit(solution)/shard_map/ppermute | solution.py:392
  27.1 0.8 %collective-permute-start.8 = (bf16[2,80,768]{2,1,0:T(8,128)(2,1)S(1)}, bf16[2,80,768]{2,1,0:T(8,128)(2,1)S(1)}, u32[]{:S(2)}, u32[]{:S(2)}) collective-permute-start(bf16[2,80,768]{2,1,0:T(8,128)(2,1)S(1)} %collective-permute-done.6.refs_5_), channel_id=1, source_target_pairs={{0,96},{8,104},{16,112},{24,120},{32,0},{40,8},{48,16},{56,24},{64... | collective-permute-start | bytes 737288 | tf_op jit(solution)/shard_map/ppermute | solution.py:392
  28.0 1.7 %collective-permute-done.4.refs_3_ = bf16[2,80,768]{2,1,0:T(8,128)(2,1)S(1)} collective-permute-done((bf16[2,80,768]{2,1,0:T(8,128)(2,1)S(1)}, bf16[2,80,768]{2,1,0:T(8,128)(2,1)S(1)}, u32[]{:S(2)}, u32[]{:S(2)}) %collective-permute-start.4) | collective-permute-done | bytes 245792 | tf_op jit(solution)/shard_map/ppermute | solution.py:389
  29.7 1.5 %collective-permute-done.5.refs_4_ = bf16[2,80,768]{2,1,0:T(8,128)(2,1)S(1)} collective-permute-done((bf16[2,80,768]{2,1,0:T(8,128)(2,1)S(1)}, bf16[2,80,768]{2,1,0:T(8,128)(2,1)S(1)}, u32[]{:S(2)}, u32[]{:S(2)}) %collective-permute-start.5) | collective-permute-done | bytes 245792 | tf_op jit(solution)/shard_map/ppermute | solution.py:390
  31.2 2.4 %collective-permute-done.7.refs_6_ = bf16[2,80,768]{2,1,0:T(8,128)(2,1)S(1)} collective-permute-done((bf16[2,80,768]{2,1,0:T(8,128)(2,1)S(1)}, bf16[2,80,768]{2,1,0:T(8,128)(2,1)S(1)}, u32[]{:S(2)}, u32[]{:S(2)}) %collective-permute-start.7) | collective-permute-done | bytes 245792 | tf_op jit(solution)/shard_map/ppermute | solution.py:392
  33.6 1.2 %collective-permute-done.8.refs_7_ = bf16[2,80,768]{2,1,0:T(8,128)(2,1)S(1)} collective-permute-done((bf16[2,80,768]{2,1,0:T(8,128)(2,1)S(1)}, bf16[2,80,768]{2,1,0:T(8,128)(2,1)S(1)}, u32[]{:S(2)}, u32[]{:S(2)}) %collective-permute-start.8) | collective-permute-done | bytes 245792 | tf_op jit(solution)/shard_map/ppermute | solution.py:392
  34.8 7.5 %legendre.1 = (bf16[8,80,512]{2,1,0:T(8,128)(2,1)}, bf16[8,80,256]{2,1,0:T(8,128)(2,1)S(1)}) custom-call(s32[640]{0:T(1024)S(1)} %get-tuple-element.26.order_ref, s32[16]{0:T(128)S(1)} %get-tuple-element.27.writer_ref, bf16[2,80,768]{2,1,0:T(8,128)(2,1)S(1)} %pad_maximum_fusion.refs_0_, bf16[2,80,768]{2,1,0:T(8,128)(2,1)S(1)} %pad_maximum_fusion.1.refs_1_, ...), custom_call_target="tpu_custom_call" | custom-call | flops 800000000 | bytes 16000000 | tf_op jit(solution)/shard_map/legendre/pallas_call | solution.py:394
  42.4 12.5 %all_to_all.10 = bf16[8,80,256]{2,1,0:T(8,128)(2,1)S(1)} all-to-all(bf16[8,80,256]{2,1,0:T(8,128)(2,1)S(1)} %get-tuple-element.35), channel_id=1, replica_groups=mesh['lat'=16,'wave'=8] {'wave'}, dimensions={0} | all-to-all | bytes 655360 | tf_op jit(solution)/shard_map/all_to_all | solution.py:410
  54.9 3.5 %all-to-all-start.1 = ((bf16[8,80,512]{2,1,0:T(8,128)(2,1)}), bf16[8,80,512]{2,1,0:T(8,128)(2,1)S(1)}, u32[]{:S(2)}, u32[]{:S(2)}) async-start(bf16[8,80,512]{2,1,0:T(8,128)(2,1)} %get-tuple-element.37), calls=%async_computation.1 | async-start | bytes 1310720 | tf_op jit(solution)/shard_map/all_to_all | solution.py:411
  58.4 0.0 copy-done.2
  58.4 0.5 edges.1
  59.0 1.9 %collective-permute-start.10 = (bf16[64,640]{1,0:T(8,128)(2,1)S(1)}, bf16[64,640]{1,0:T(8,128)(2,1)S(1)}, u32[]{:S(2)}, u32[]{:S(2)}) collective-permute-start(bf16[64,640]{1,0:T(8,128)(2,1)S(1)} %get-tuple-element.40), channel_id=1, source_target_pairs={{0,8},{8,16},{16,24},{24,32},{32,40},{40,48},{48,56},{56,64},{64,7... | collective-permute-start | bytes 245768 | tf_op jit(solution)/shard_map/ppermute | solution.py:425
  60.9 6.1 %collective-permute-start.9 = (bf16[64,640]{1,0:T(8,128)(2,1)S(1)}, bf16[64,640]{1,0:T(8,128)(2,1)S(1)}, u32[]{:S(2)}, u32[]{:S(2)}) collective-permute-start(bf16[64,640]{1,0:T(8,128)(2,1)S(1)} %get-tuple-element.39), channel_id=1, source_target_pairs={{8,0},{16,8},{24,16},{32,24},{40,32},{48,40},{56,48},{64,56},{72,6... | collective-permute-start | bytes 245768 | tf_op jit(solution)/shard_map/ppermute | solution.py:424
  66.9 3.1 %all-to-all-done.1 = bf16[8,80,512]{2,1,0:T(8,128)(2,1)S(1)} async-done(((bf16[8,80,512]{2,1,0:T(8,128)(2,1)}), bf16[8,80,512]{2,1,0:T(8,128)(2,1)S(1)}, u32[]{:S(2)}, u32[]{:S(2)}) %all-to-all-start.1) | async-done | bytes 655392 | tf_op jit(solution)/shard_map/all_to_all | solution.py:411
  70.1 0.7 order.1.main_ref
  70.8 0.0 collective-permute-done.10.below_ref
  70.9 0.0 collective-permute-done.9.above_ref
  70.9 0.0 copy-done.4
  70.9 0.0 copy-done.5
  70.9 6.5 %synthesis.1 = bf16[2,160,5120]{2,1,0:T(8,128)(2,1)} custom-call(bf16[512,640]{1,0:T(8,128)(2,1)S(1)} %order.1.main_ref, bf16[128,640]{1,0:T(8,128)(2,1)S(1)} %get-tuple-element.38.rest_ref, bf16[64,640]{1,0:T(8,128)(2,1)S(1)} %collective-permute-done.9.above_ref, bf16[64,640]{1,0:T(8,128)(2,1)S(1)} %collective-permute-done.10.below_ref, ...), custom_call_target="tpu_custom_call" | custom-call | flops 2400000000 | bytes 11000000 | tf_op jit(solution)/shard_map/synthesis/pallas_call | solution.py:437
  (2 shorter events, 0.0 us)
Async XLA Ops:
  1.7 9.6 %collective-permute-start.1 = (bf16[80,768]{1,0:T(8,128)(2,1)}, bf16[80,768]{1,0:T(8,128)(2,1)S(1)}, u32[]{:S(2)}, u32[]{:S(2)}) collective-permute-start(bf16[80,768]{1,0:T(8,128)(2,1)} %pack.1), channel_id=1, source_target_pairs={{0,24},{8,0},{16,8},{24,16},{32,56},{40,32},{48,40},{56,48},{64,88... | collective-permute-start | bytes 368648 | tf_op jit(solution)/shard_map/ppermute | solution.py:361
  5.7 7.9 %collective-permute-start.2 = (bf16[80,768]{1,0:T(8,128)(2,1)}, bf16[80,768]{1,0:T(8,128)(2,1)S(1)}, u32[]{:S(2)}, u32[]{:S(2)}) collective-permute-start(bf16[80,768]{1,0:T(8,128)(2,1)} %pack.1), channel_id=1, source_target_pairs={{0,16},{8,24},{16,0},{24,8},{32,48},{40,56},{48,32},{56,40},{64,80... | collective-permute-start | bytes 368648 | tf_op jit(solution)/shard_map/ppermute | solution.py:361
  5.7 8.8 %collective-permute-start = (bf16[80,768]{1,0:T(8,128)(2,1)}, bf16[80,768]{1,0:T(8,128)(2,1)S(1)}, u32[]{:S(2)}, u32[]{:S(2)}) collective-permute-start(bf16[80,768]{1,0:T(8,128)(2,1)} %pack.1), channel_id=1, source_target_pairs={{0,8},{8,16},{16,24},{24,0},{32,40},{40,48},{48,56},{56,32},{64,72... | collective-permute-start | bytes 368648 | tf_op jit(solution)/shard_map/ppermute | solution.py:361
  7.0 0.9 %copy-start = (bf16[3,160,256]{2,1,0:T(8,128)(2,1)S(1)}, bf16[3,160,256]{2,1,0:T(8,128)(2,1)}, u32[]{:S(2)}) copy-start(bf16[3,160,256]{2,1,0:T(8,128)(2,1)} %constant.8.clone.matrix_ref) | copy-start | bytes 737284
  7.9 0.7 copy-start.1
  8.6 0.7 copy-start.3
  15.5 8.9 %collective-permute-start.3 = (bf16[2,80,768]{2,1,0:T(8,128)(2,1)S(1)}, bf16[2,80,768]{2,1,0:T(8,128)(2,1)S(1)}, u32[]{:S(2)}, u32[]{:S(2)}) collective-permute-start(bf16[2,80,768]{2,1,0:T(8,128)(2,1)S(1)} %pad_maximum_fusion.refs_0_), channel_id=1, source_target_pairs={{0,32},{8,40},{16,48},{24,56},{32,64},{40,72},{48,80},{56,88},{64,... | collective-permute-start | bytes 737288 | tf_op jit(solution)/shard_map/ppermute | solution.py:389
  17.1 8.9 %collective-permute-start.6 = (bf16[2,80,768]{2,1,0:T(8,128)(2,1)S(1)}, bf16[2,80,768]{2,1,0:T(8,128)(2,1)S(1)}, u32[]{:S(2)}, u32[]{:S(2)}) collective-permute-start(bf16[2,80,768]{2,1,0:T(8,128)(2,1)S(1)} %pad_maximum_fusion.1.refs_1_), channel_id=1, source_target_pairs={{0,96},{8,104},{16,112},{24,120},{32,0},{40,8},{48,16},{56,24},{64... | collective-permute-start | bytes 737288 | tf_op jit(solution)/shard_map/ppermute | solution.py:390
  17.6 12.1 %collective-permute-start.4 = (bf16[2,80,768]{2,1,0:T(8,128)(2,1)S(1)}, bf16[2,80,768]{2,1,0:T(8,128)(2,1)S(1)}, u32[]{:S(2)}, u32[]{:S(2)}) collective-permute-start(bf16[2,80,768]{2,1,0:T(8,128)(2,1)S(1)} %pad_maximum_fusion.1.refs_1_), channel_id=1, source_target_pairs={{0,32},{8,40},{16,48},{24,56},{32,64},{40,72},{48,80},{56,88},{64,... | collective-permute-start | bytes 737288 | tf_op jit(solution)/shard_map/ppermute | solution.py:389
  19.1 12.1 %collective-permute-start.5 = (bf16[2,80,768]{2,1,0:T(8,128)(2,1)S(1)}, bf16[2,80,768]{2,1,0:T(8,128)(2,1)S(1)}, u32[]{:S(2)}, u32[]{:S(2)}) collective-permute-start(bf16[2,80,768]{2,1,0:T(8,128)(2,1)S(1)} %pad_maximum_fusion.refs_0_), channel_id=1, source_target_pairs={{0,96},{8,104},{16,112},{24,120},{32,0},{40,8},{48,16},{56,24},{64... | collective-permute-start | bytes 737288 | tf_op jit(solution)/shard_map/ppermute | solution.py:390
  23.0 35.5 %copy-start.2 = (s32[640]{0:T(1024)S(1)}, s32[640]{0:T(1024)}, u32[]{:S(2)}) copy-start(s32[640]{0:T(1024)} %order_ref.3) | copy-start | bytes 7684
  23.0 47.9 %copy-start.4 = (bf16[2,640,128]{2,1,0:T(8,128)(2,1)S(1)}, bf16[2,640,128]{2,1,0:T(8,128)(2,1)}, u32[]{:S(2)}) copy-start(bf16[2,640,128]{2,1,0:T(8,128)(2,1)} %constant.10.clone.middle_ref) | copy-start | bytes 983044
  23.0 47.9 %copy-start.5 = (bf16[160,32]{1,0:T(8,128)(2,1)S(1)}, bf16[160,32]{1,0:T(8,128)(2,1)}, u32[]{:S(2)}) copy-start(bf16[160,32]{1,0:T(8,128)(2,1)} %constant.9.clone.expand_ref) | copy-start | bytes 30724
  25.9 7.7 %collective-permute-start.7 = (bf16[2,80,768]{2,1,0:T(8,128)(2,1)S(1)}, bf16[2,80,768]{2,1,0:T(8,128)(2,1)S(1)}, u32[]{:S(2)}, u32[]{:S(2)}) collective-permute-start(bf16[2,80,768]{2,1,0:T(8,128)(2,1)S(1)} %collective-permute-done.3.refs_2_), channel_id=1, source_target_pairs={{0,32},{8,40},{16,48},{24,56},{32,64},{40,72},{48,80},{56,88},{64,... | collective-permute-start | bytes 737288 | tf_op jit(solution)/shard_map/ppermute | solution.py:392
  27.1 7.7 %collective-permute-start.8 = (bf16[2,80,768]{2,1,0:T(8,128)(2,1)S(1)}, bf16[2,80,768]{2,1,0:T(8,128)(2,1)S(1)}, u32[]{:S(2)}, u32[]{:S(2)}) collective-permute-start(bf16[2,80,768]{2,1,0:T(8,128)(2,1)S(1)} %collective-permute-done.6.refs_5_), channel_id=1, source_target_pairs={{0,96},{8,104},{16,112},{24,120},{32,0},{40,8},{48,16},{56,24},{64... | collective-permute-start | bytes 737288 | tf_op jit(solution)/shard_map/ppermute | solution.py:392
  54.9 15.2 %all-to-all-start.1 = ((bf16[8,80,512]{2,1,0:T(8,128)(2,1)}), bf16[8,80,512]{2,1,0:T(8,128)(2,1)S(1)}, u32[]{:S(2)}, u32[]{:S(2)}) async-start(bf16[8,80,512]{2,1,0:T(8,128)(2,1)} %get-tuple-element.37), calls=%async_computation.1 | async-start | bytes 1310720 | tf_op jit(solution)/shard_map/all_to_all | solution.py:411
  59.0 11.9 %collective-permute-start.10 = (bf16[64,640]{1,0:T(8,128)(2,1)S(1)}, bf16[64,640]{1,0:T(8,128)(2,1)S(1)}, u32[]{:S(2)}, u32[]{:S(2)}) collective-permute-start(bf16[64,640]{1,0:T(8,128)(2,1)S(1)} %get-tuple-element.40), channel_id=1, source_target_pairs={{0,8},{8,16},{16,24},{24,32},{32,40},{40,48},{48,56},{56,64},{64,7... | collective-permute-start | bytes 245768 | tf_op jit(solution)/shard_map/ppermute | solution.py:425
  60.9 10.0 %collective-permute-start.9 = (bf16[64,640]{1,0:T(8,128)(2,1)S(1)}, bf16[64,640]{1,0:T(8,128)(2,1)S(1)}, u32[]{:S(2)}, u32[]{:S(2)}) collective-permute-start(bf16[64,640]{1,0:T(8,128)(2,1)S(1)} %get-tuple-element.39), channel_id=1, source_target_pairs={{8,0},{16,8},{24,16},{32,24},{40,32},{48,40},{56,48},{64,56},{72,6... | collective-permute-start | bytes 245768 | tf_op jit(solution)/shard_map/ppermute | solution.py:424

commit v9 on v8

--- a/solution.py
+++ b/solution.py
@@ -217,8 +217,8 @@
         picked = slice(index * chunk, (index + 1) * chunk)
         left = jnp.concatenate([rows[0, picked, :], rows[1, picked, : BAND - LANE]], axis=1).astype(jnp.bfloat16)
         sums = jnp.dot(left, matrix[...], preferred_element_type=jnp.float32)
-        results[0, picked, :] = sums[:, :LANE]
-        results[1, picked, :] = sums[:, LANE:]
+        out_ref[picked, :] = sums[:, :LANE].astype(jnp.bfloat16)
+        results[picked, :] = sums[:, LANE:]
 
     lane = lax.broadcasted_iota(jnp.int32, (SLOTS, LANE), 1)
     for owner in range(OWNERS):
@@ -227,17 +227,22 @@
             tails = []
             for part in range(2):
                 start = pl.multiple_of((2 * field + part) * SLOTS, 8)
-                place = (2 * member + part) * LANE
-                out_ref[owner, :, place : place + LANE] = results[0, pl.ds(start, SLOTS), :].astype(jnp.bfloat16)
-                tails.append(results[1, pl.ds(start, SLOTS), :])
+                tails.append(results[pl.ds(start, SLOTS), :])
             place = member * LANE
             tail_ref[owner, :, place : place + LANE] = jnp.where(lane < LANE // 2, *tails).astype(jnp.bfloat16)
 
 
-def edge_kernel(order_ref, waves_ref, chosen_ref, rest_ref, above_ref, below_ref):
+def sort_kernel(writer_ref, order_ref, rows_ref, out_ref, chosen_ref):
     row = lax.broadcasted_iota(jnp.int32, (NWAVE, NWAVE), 0)
     wave = jnp.where(row < NWAVE // 2, 2 * row, 2 * row + 1 - NWAVE)
     chosen_ref[...] = jnp.where(wave == order_ref[...], 1.0, 0.0).astype(jnp.bfloat16)
+    for owner in range(OWNERS):
+        for which in range(4):
+            start = pl.multiple_of((2 * writer_ref[2 * owner + which // 2] + which % 2) * SLOTS, 16)
+            out_ref[owner, :, which * LANE : (which + 1) * LANE] = rows_ref[pl.ds(start, SLOTS), :]
+
+
+def edge_kernel(chosen_ref, waves_ref, rest_ref, above_ref, below_ref):
     ordered = jnp.dot(chosen_ref[...], waves_ref[...], preferred_element_type=jnp.float32)
     turned = ordered.T.astype(jnp.bfloat16)
     rest = BAND - LANE
@@ -391,15 +396,15 @@
         relayed, near = lax.optimization_barrier(((before[0], after[1]), near))
         opposite = [lax.ppermute(relayed[0], "lat", along_x(1)), lax.ppermute(relayed[1], "lat", along_x(3))]
 
-        lifted, tails = pl.pallas_call(
+        in_order, tails = pl.pallas_call(
             legendre_kernel,
-            out_shape=[bf16(OWNERS, SLOTS, 4 * LANE), bf16(OWNERS, SLOTS, WIDTH - 4 * LANE)],
+            out_shape=[bf16(2 * FIELDS * SLOTS, LANE), bf16(OWNERS, SLOTS, WIDTH - 4 * LANE)],
             in_specs=[SMEM, SMEM] + [VMEM] * 8 + [VMEM, ANY, VMEM],
             out_specs=[VMEM] * 2,
             scratch_shapes=[
                 pltpu.VMEM((BLOCKS, 2 * FIELDS * PAIRS, LANE), jnp.float32),
                 pltpu.VMEM((2, 2 * FIELDS * SLOTS, LANE), jnp.float32),
-                pltpu.VMEM((2, 2 * FIELDS * SLOTS, LANE), jnp.float32),
+                pltpu.VMEM((2 * FIELDS * SLOTS, LANE), jnp.float32),
                 pltpu.VMEM((PART_SLOTS, BAND, NWAVE), jnp.bfloat16),
                 pltpu.SemaphoreType.DMA((2,)),
             ],
@@ -407,20 +412,29 @@
             cost_estimate=pl.CostEstimate(flops=800_000_000, bytes_accessed=16_000_000, transcendentals=0),
             name="legendre",
         )(orders, writers, *firsts, *before, *after, *opposite, near, legendre, matrix)
+        lifted, chosen = pl.pallas_call(
+            sort_kernel,
+            out_shape=[bf16(OWNERS, SLOTS, 4 * LANE), bf16(NWAVE, NWAVE)],
+            in_specs=[SMEM, VMEM, VMEM],
+            out_specs=[VMEM] * 2,
+            compiler_params=SMALL,
+            cost_estimate=pl.CostEstimate(flops=0, bytes_accessed=6_000_000, transcendentals=0),
+            name="sort",
+        )(writers, wave_order.reshape(1, NWAVE), in_order)
         edges = lax.all_to_all(tails, "wave", split_axis=0, concat_axis=0, tiled=True)
         waves = lax.all_to_all(lifted, "wave", split_axis=0, concat_axis=0, tiled=True)
 
         main, rest = 4 * LANE, 4 * (BAND - LANE)
-        chosen, tail, above, below = pl.pallas_call(
+        tail, above, below = pl.pallas_call(
             edge_kernel,
             grid=(1,),
-            out_shape=[bf16(NWAVE, NWAVE), bf16(rest, NWAVE), bf16(4 * RANK, NWAVE), bf16(4 * RANK, NWAVE)],
-            in_specs=[pl.BlockSpec((1, NWAVE), lambda i: (0, 0))]
+            out_shape=[bf16(rest, NWAVE), bf16(4 * RANK, NWAVE), bf16(4 * RANK, NWAVE)],
+            in_specs=[pl.BlockSpec((NWAVE, NWAVE), lambda i: (0, 0))]
             + [pl.BlockSpec((NWAVE, WIDTH - main), lambda i: (0, 0))],
-            out_specs=[VMEM] * 4,
+            out_specs=[VMEM] * 3,
             compiler_params=SMALL,
             name="edges",
-        )(wave_order.reshape(1, NWAVE), edges.reshape(NWAVE, WIDTH - main))
+        )(chosen, edges.reshape(NWAVE, WIDTH - main))
         above = lax.ppermute(above, "lat", neighbour(-1))
         below = lax.ppermute(below, "lat", neighbour(1))
         ordered = pl.pallas_call(

time: 78.4 us -> 78.5 us (level)
  blocking collectives: 12.5 us -> 0 us
  waiting for transfers between devices: 18.1 us -> 24.9 us
  starting transfers between devices: 23 us -> 27.4 us
  Pallas kernels: 20.4 us -> 21.7 us
    all_to_all x1 -> x0, blocking collectives: 12.5 us -> none  [on_device(): lax.all_to_all(tails, 'wave', split_axis=0, concat_axis=0, tiled=True)]
    all_to_all x0 -> x1, waiting for transfers between devices: none -> 6.69 us  [on_device(): lax.all_to_all(tails, 'wave', split_axis=0, concat_axis=0, tiled=True)]
    all_to_all x0 -> x1, starting transfers between devices: none -> 4.48 us  [on_device(): lax.all_to_all(tails, 'wave', split_axis=0, concat_axis=0, tiled=True)]
    pallas_call x2 -> x3, Pallas kernels: 8.02 us -> 9.36 us  [the longest x1 7.34 us: on_device(): pl.pallas_call(legendre_kernel, out_shape=[bf16(2 * FIELDS * SLOTS, LANE)...]
  transfers between devices with their start and end apart: 12 -> 13, of which waited for: 10 -> 11; matrix products, arithmetic and copies ran while one was open for 0% -> 0% of each run, Pallas kernels for 6% -> 8%
where the time goes in v9:
time: 78.5 us; the launch traced here: 77.4 us
  starting transfers between devices  27.4 us (35%)
  waiting for transfers between devices  24.9 us (32%)
  Pallas kernels  21.7 us (28%)
  local copies, waits for them, and re-layouts  2.31 us (3%)
  other arithmetic  0.95 us (1%)
    pallas_call x1, Pallas kernels, on_device(): pl.pallas_call(legendre_kernel, out_shape=[bf16(2 * FIELDS * SLOTS, LANE)...  7.34 us
    all_to_all x1, waiting for transfers between devices, on_device(): lax.all_to_all(tails, 'wave', split_axis=0, concat_axis=0, tiled=True)  6.69 us
    pallas_call x1, Pallas kernels, on_device(): pl.pallas_call(synthesis_kernel, out_shape=bf16(2, BAND, NLON), in_specs=...  6.51 us
    ppermute x1, starting transfers between devices, on_device(): above = lax.ppermute(above, 'lat', neighbour(-1))  6.03 us
    ppermute x3, starting transfers between devices, on_device(): lax.ppermute(packed, 'lat', along_z(step))  5.3 us
    ppermute x3, waiting for transfers between devices, on_device(): lax.ppermute(packed, 'lat', along_z(step))  5.14 us
    all_to_all x1, starting transfers between devices, on_device(): lax.all_to_all(tails, 'wave', split_axis=0, concat_axis=0, tiled=True)  4.48 us
    all_to_all x1, starting transfers between devices, on_device(): lax.all_to_all(lifted, 'wave', split_axis=0, concat_axis=0, tiled=True)  3.54 us
  transfers between devices with their start and end apart: 13, of which 11 were waited for; matrix products, arithmetic and copies ran while one was open for 0% of the time, Pallas kernels for 8%

profile of v9, /device:TPU:2, one launch (start us, length us, event | category | flops | bytes accessed | tf_op | source)
XLA Modules:
  0.0 77.4 jit_solution(1528052942223473225)
XLA Ops:
  0.0 1.7 %pack.1 = bf16[80,768]{1,0:T(8,128)(2,1)} custom-call(s32[640]{0:T(1024)} %order_ref.3, bf16[1,2,80,640]{3,2,1,0:T(8,128)(2,1)} %spectra_ref.1), custom_call_target="tpu_custom_call" | custom-call | tf_op jit(solution)/shard_map/pack/pallas_call | solution.py:353
  1.7 4.0 %collective-permute-start.1 = (bf16[80,768]{1,0:T(8,128)(2,1)}, bf16[80,768]{1,0:T(8,128)(2,1)S(1)}, u32[]{:S(2)}, u32[]{:S(2)}) collective-permute-start(bf16[80,768]{1,0:T(8,128)(2,1)} %pack.1), channel_id=1, source_target_pairs={{0,24},{8,0},{16,8},{24,16},{32,56},{40,32},{48,40},{56,48},{64,88... | collective-permute-start | bytes 368648 | tf_op jit(solution)/shard_map/ppermute | solution.py:366
  5.7 0.0 collective-permute-start.2
  5.7 1.3 %collective-permute-start = (bf16[80,768]{1,0:T(8,128)(2,1)}, bf16[80,768]{1,0:T(8,128)(2,1)S(1)}, u32[]{:S(2)}, u32[]{:S(2)}) collective-permute-start(bf16[80,768]{1,0:T(8,128)(2,1)} %pack.1), channel_id=1, source_target_pairs={{0,8},{8,16},{16,24},{24,0},{32,40},{40,48},{48,56},{56,32},{64,72... | collective-permute-start | bytes 368648 | tf_op jit(solution)/shard_map/ppermute | solution.py:366
  7.0 0.0 copy-start
  7.0 0.9 %copy-done = bf16[3,160,256]{2,1,0:T(8,128)(2,1)S(1)} copy-done((bf16[3,160,256]{2,1,0:T(8,128)(2,1)S(1)}, bf16[3,160,256]{2,1,0:T(8,128)(2,1)}, u32[]{:S(2)}) %copy-start) | copy-done | bytes 245784
  7.9 0.0 copy-start.1
  7.9 0.7 copy-done.1
  8.6 0.0 copy-start.3
  8.6 0.7 copy-done.3
  9.3 0.1 hand.1
  9.4 1.9 %collective-permute-done.1 = bf16[80,768]{1,0:T(8,128)(2,1)S(1)} collective-permute-done((bf16[80,768]{1,0:T(8,128)(2,1)}, bf16[80,768]{1,0:T(8,128)(2,1)S(1)}, u32[]{:S(2)}, u32[]{:S(2)}) %collective-permute-start.1) | collective-permute-done | bytes 122912 | tf_op jit(solution)/shard_map/ppermute | solution.py:366
  11.3 2.3 %collective-permute-done.2 = bf16[80,768]{1,0:T(8,128)(2,1)S(1)} collective-permute-done((bf16[80,768]{1,0:T(8,128)(2,1)}, bf16[80,768]{1,0:T(8,128)(2,1)S(1)}, u32[]{:S(2)}, u32[]{:S(2)}) %collective-permute-start.2) | collective-permute-done | bytes 122912 | tf_op jit(solution)/shard_map/ppermute | solution.py:366
  13.6 0.9 %collective-permute-done = bf16[80,768]{1,0:T(8,128)(2,1)S(1)} collective-permute-done((bf16[80,768]{1,0:T(8,128)(2,1)}, bf16[80,768]{1,0:T(8,128)(2,1)S(1)}, u32[]{:S(2)}, u32[]{:S(2)}) %collective-permute-start) | collective-permute-done | bytes 122912 | tf_op jit(solution)/shard_map/ppermute | solution.py:366
  14.6 0.9 %pad_maximum_fusion.refs_0_ = bf16[2,80,768]{2,1,0:T(8,128)(2,1)S(1)} fusion(bf16[1,80,768]{2,1,0:T(8,128)(2,1)S(1)} %bitcast.10, bf16[1,80,768]{2,1,0:T(8,128)(2,1)} %bitcast.8), kind=kLoop, calls=%fused_computation | loop fusion | flops 122880 | bytes 491520 | tf_op jit(solution)/shard_map/stack | solution.py:367
  15.5 1.6 %collective-permute-start.3 = (bf16[2,80,768]{2,1,0:T(8,128)(2,1)S(1)}, bf16[2,80,768]{2,1,0:T(8,128)(2,1)S(1)}, u32[]{:S(2)}, u32[]{:S(2)}) collective-permute-start(bf16[2,80,768]{2,1,0:T(8,128)(2,1)S(1)} %pad_maximum_fusion.refs_0_), channel_id=1, source_target_pairs={{0,32},{8,40},{16,48},{24,56},{32,64},{40,72},{48,80},{56,88},{64,... | collective-permute-start | bytes 737288 | tf_op jit(solution)/shard_map/ppermute | solution.py:394
  17.1 0.5 collective-permute-start.6
  17.6 1.5 %collective-permute-start.4 = (bf16[2,80,768]{2,1,0:T(8,128)(2,1)S(1)}, bf16[2,80,768]{2,1,0:T(8,128)(2,1)S(1)}, u32[]{:S(2)}, u32[]{:S(2)}) collective-permute-start(bf16[2,80,768]{2,1,0:T(8,128)(2,1)S(1)} %pad_maximum_fusion.1.refs_1_), channel_id=1, source_target_pairs={{0,32},{8,40},{16,48},{24,56},{32,64},{40,72},{48,80},{56,88},{64,... | collective-permute-start | bytes 737288 | tf_op jit(solution)/shard_map/ppermute | solution.py:394
  19.1 0.5 collective-permute-start.5
  19.6 3.3 %fetch.1.refs_8_ = bf16[40,160,640]{2,1,0:T(8,128)(2,1)S(1)} custom-call(bf16[80,160,640]{2,1,0:T(8,128)(2,1)} %refs_9_), custom_call_target="tpu_custom_call" | custom-call | bytes 14000000 | tf_op jit(solution)/shard_map/fetch/pallas_call | solution.py:384
  23.0 0.0 copy-start.2
  23.0 0.0 copy-start.4
  23.0 0.0 copy-start.5
  23.0 1.4 %collective-permute-done.3.refs_2_ = bf16[2,80,768]{2,1,0:T(8,128)(2,1)S(1)} collective-permute-done((bf16[2,80,768]{2,1,0:T(8,128)(2,1)S(1)}, bf16[2,80,768]{2,1,0:T(8,128)(2,1)S(1)}, u32[]{:S(2)}, u32[]{:S(2)}) %collective-permute-start.3) | collective-permute-done | bytes 245792 | tf_op jit(solution)/shard_map/ppermute | solution.py:394
  24.4 1.5 %collective-permute-done.6.refs_5_ = bf16[2,80,768]{2,1,0:T(8,128)(2,1)S(1)} collective-permute-done((bf16[2,80,768]{2,1,0:T(8,128)(2,1)S(1)}, bf16[2,80,768]{2,1,0:T(8,128)(2,1)S(1)}, u32[]{:S(2)}, u32[]{:S(2)}) %collective-permute-start.6) | collective-permute-done | bytes 245792 | tf_op jit(solution)/shard_map/ppermute | solution.py:395
  25.9 1.2 %collective-permute-start.7 = (bf16[2,80,768]{2,1,0:T(8,128)(2,1)S(1)}, bf16[2,80,768]{2,1,0:T(8,128)(2,1)S(1)}, u32[]{:S(2)}, u32[]{:S(2)}) collective-permute-start(bf16[2,80,768]{2,1,0:T(8,128)(2,1)S(1)} %collective-permute-done.3.refs_2_), channel_id=1, source_target_pairs={{0,32},{8,40},{16,48},{24,56},{32,64},{40,72},{48,80},{56,88},{64,... | collective-permute-start | bytes 737288 | tf_op jit(solution)/shard_map/ppermute | solution.py:397
  27.1 0.8 %collective-permute-start.8 = (bf16[2,80,768]{2,1,0:T(8,128)(2,1)S(1)}, bf16[2,80,768]{2,1,0:T(8,128)(2,1)S(1)}, u32[]{:S(2)}, u32[]{:S(2)}) collective-permute-start(bf16[2,80,768]{2,1,0:T(8,128)(2,1)S(1)} %collective-permute-done.6.refs_5_), channel_id=1, source_target_pairs={{0,96},{8,104},{16,112},{24,120},{32,0},{40,8},{48,16},{56,24},{64... | collective-permute-start | bytes 737288 | tf_op jit(solution)/shard_map/ppermute | solution.py:397
  28.0 1.7 %collective-permute-done.4.refs_3_ = bf16[2,80,768]{2,1,0:T(8,128)(2,1)S(1)} collective-permute-done((bf16[2,80,768]{2,1,0:T(8,128)(2,1)S(1)}, bf16[2,80,768]{2,1,0:T(8,128)(2,1)S(1)}, u32[]{:S(2)}, u32[]{:S(2)}) %collective-permute-start.4) | collective-permute-done | bytes 245792 | tf_op jit(solution)/shard_map/ppermute | solution.py:394
  29.7 1.5 %collective-permute-done.5.refs_4_ = bf16[2,80,768]{2,1,0:T(8,128)(2,1)S(1)} collective-permute-done((bf16[2,80,768]{2,1,0:T(8,128)(2,1)S(1)}, bf16[2,80,768]{2,1,0:T(8,128)(2,1)S(1)}, u32[]{:S(2)}, u32[]{:S(2)}) %collective-permute-start.5) | collective-permute-done | bytes 245792 | tf_op jit(solution)/shard_map/ppermute | solution.py:395
  31.2 2.4 %collective-permute-done.7.refs_6_ = bf16[2,80,768]{2,1,0:T(8,128)(2,1)S(1)} collective-permute-done((bf16[2,80,768]{2,1,0:T(8,128)(2,1)S(1)}, bf16[2,80,768]{2,1,0:T(8,128)(2,1)S(1)}, u32[]{:S(2)}, u32[]{:S(2)}) %collective-permute-start.7) | collective-permute-done | bytes 245792 | tf_op jit(solution)/shard_map/ppermute | solution.py:397
  33.6 1.2 %collective-permute-done.8.refs_7_ = bf16[2,80,768]{2,1,0:T(8,128)(2,1)S(1)} collective-permute-done((bf16[2,80,768]{2,1,0:T(8,128)(2,1)S(1)}, bf16[2,80,768]{2,1,0:T(8,128)(2,1)S(1)}, u32[]{:S(2)}, u32[]{:S(2)}) %collective-permute-start.8) | collective-permute-done | bytes 245792 | tf_op jit(solution)/shard_map/ppermute | solution.py:397
  34.8 7.3 %legendre.1 = (bf16[2560,128]{1,0:T(8,128)(2,1)S(1)}, bf16[8,80,256]{2,1,0:T(8,128)(2,1)}) custom-call(s32[640]{0:T(1024)S(1)} %get-tuple-element.28.order_ref, s32[16]{0:T(128)S(1)} %get-tuple-element.27.writer_ref, bf16[2,80,768]{2,1,0:T(8,128)(2,1)S(1)} %pad_maximum_fusion.refs_0_, bf16[2,80,768]{2,1,0:T(8,128)(2,1)S(1)} %pad_maximum_fusion.1.refs_1_, ...), custom_call_target="tpu_custom_call" | custom-call | flops 800000000 | bytes 16000000 | tf_op jit(solution)/shard_map/legendre/pallas_call | solution.py:399
  42.2 4.5 %all-to-all-start.1 = ((bf16[8,80,256]{2,1,0:T(8,128)(2,1)}), bf16[8,80,256]{2,1,0:T(8,128)(2,1)S(1)}, u32[]{:S(2)}, u32[]{:S(2)}) async-start(bf16[8,80,256]{2,1,0:T(8,128)(2,1)} %get-tuple-element.39), calls=%async_computation.1 | async-start | bytes 655360 | tf_op jit(solution)/shard_map/all_to_all | solution.py:424
  46.7 0.0 copy-done.2
  46.7 1.5 %sort.1 = (bf16[8,80,512]{2,1,0:T(8,128)(2,1)}, bf16[640,640]{1,0:T(8,128)(2,1)S(1)}) custom-call(s32[16]{0:T(128)S(1)} %get-tuple-element.27.writer_ref, s32[1,640]{1,0:T(1,128)S(1)} %reshape.9.order_ref, bf16[2560,128]{1,0:T(8,128)(2,1)S(1)} %get-tuple-element.36.rows_ref), custom_call_target="tpu_custom_call" | custom-call | bytes 6000000 | tf_op jit(solution)/shard_map/sort/pallas_call | solution.py:415
  48.2 6.7 %all-to-all-done.1 = bf16[8,80,256]{2,1,0:T(8,128)(2,1)S(1)} async-done(((bf16[8,80,256]{2,1,0:T(8,128)(2,1)}), bf16[8,80,256]{2,1,0:T(8,128)(2,1)S(1)}, u32[]{:S(2)}, u32[]{:S(2)}) %all-to-all-start.1) | async-done | bytes 327712 | tf_op jit(solution)/shard_map/all_to_all | solution.py:424
  54.9 3.5 %all-to-all-start = ((bf16[8,80,512]{2,1,0:T(8,128)(2,1)}), bf16[8,80,512]{2,1,0:T(8,128)(2,1)S(1)}, u32[]{:S(2)}, u32[]{:S(2)}) async-start(bf16[8,80,512]{2,1,0:T(8,128)(2,1)} %get-tuple-element.38), calls=%async_computation | async-start | bytes 1310720 | tf_op jit(solution)/shard_map/all_to_all | solution.py:425
  58.5 0.5 edges.1
  59.0 1.9 %collective-permute-start.10 = (bf16[64,640]{1,0:T(8,128)(2,1)S(1)}, bf16[64,640]{1,0:T(8,128)(2,1)S(1)}, u32[]{:S(2)}, u32[]{:S(2)}) collective-permute-start(bf16[64,640]{1,0:T(8,128)(2,1)S(1)} %get-tuple-element.42), channel_id=1, source_target_pairs={{0,8},{8,16},{16,24},{24,32},{32,40},{40,48},{48,56},{56,64},{64,7... | collective-permute-start | bytes 245768 | tf_op jit(solution)/shard_map/ppermute | solution.py:439
  60.9 6.0 %collective-permute-start.9 = (bf16[64,640]{1,0:T(8,128)(2,1)S(1)}, bf16[64,640]{1,0:T(8,128)(2,1)S(1)}, u32[]{:S(2)}, u32[]{:S(2)}) collective-permute-start(bf16[64,640]{1,0:T(8,128)(2,1)S(1)} %get-tuple-element.41), channel_id=1, source_target_pairs={{8,0},{16,8},{24,16},{32,24},{40,32},{48,40},{56,48},{64,56},{72,6... | collective-permute-start | bytes 245768 | tf_op jit(solution)/shard_map/ppermute | solution.py:438
  66.9 3.2 %all-to-all-done = bf16[8,80,512]{2,1,0:T(8,128)(2,1)S(1)} async-done(((bf16[8,80,512]{2,1,0:T(8,128)(2,1)}), bf16[8,80,512]{2,1,0:T(8,128)(2,1)S(1)}, u32[]{:S(2)}, u32[]{:S(2)}) %all-to-all-start) | async-done | bytes 655392 | tf_op jit(solution)/shard_map/all_to_all | solution.py:425
  70.1 0.7 order.1.main_ref
  70.9 0.0 collective-permute-done.10.below_ref
  70.9 0.0 collective-permute-done.9.above_ref
  70.9 0.0 copy-done.4
  70.9 0.0 copy-done.5
  70.9 6.5 %synthesis.1 = bf16[2,160,5120]{2,1,0:T(8,128)(2,1)} custom-call(bf16[512,640]{1,0:T(8,128)(2,1)S(1)} %order.1.main_ref, bf16[128,640]{1,0:T(8,128)(2,1)S(1)} %get-tuple-element.40.rest_ref, bf16[64,640]{1,0:T(8,128)(2,1)S(1)} %collective-permute-done.9.above_ref, bf16[64,640]{1,0:T(8,128)(2,1)S(1)} %collective-permute-done.10.below_ref, ...), custom_call_target="tpu_custom_call" | custom-call | flops 2400000000 | bytes 11000000 | tf_op jit(solution)/shard_map/synthesis/pallas_call | solution.py:451
  (2 shorter events, 0.0 us)
Async XLA Ops:
  1.7 9.6 %collective-permute-start.1 = (bf16[80,768]{1,0:T(8,128)(2,1)}, bf16[80,768]{1,0:T(8,128)(2,1)S(1)}, u32[]{:S(2)}, u32[]{:S(2)}) collective-permute-start(bf16[80,768]{1,0:T(8,128)(2,1)} %pack.1), channel_id=1, source_target_pairs={{0,24},{8,0},{16,8},{24,16},{32,56},{40,32},{48,40},{56,48},{64,88... | collective-permute-start | bytes 368648 | tf_op jit(solution)/shard_map/ppermute | solution.py:366
  5.7 7.9 %collective-permute-start.2 = (bf16[80,768]{1,0:T(8,128)(2,1)}, bf16[80,768]{1,0:T(8,128)(2,1)S(1)}, u32[]{:S(2)}, u32[]{:S(2)}) collective-permute-start(bf16[80,768]{1,0:T(8,128)(2,1)} %pack.1), channel_id=1, source_target_pairs={{0,16},{8,24},{16,0},{24,8},{32,48},{40,56},{48,32},{56,40},{64,80... | collective-permute-start | bytes 368648 | tf_op jit(solution)/shard_map/ppermute | solution.py:366
  5.7 8.8 %collective-permute-start = (bf16[80,768]{1,0:T(8,128)(2,1)}, bf16[80,768]{1,0:T(8,128)(2,1)S(1)}, u32[]{:S(2)}, u32[]{:S(2)}) collective-permute-start(bf16[80,768]{1,0:T(8,128)(2,1)} %pack.1), channel_id=1, source_target_pairs={{0,8},{8,16},{16,24},{24,0},{32,40},{40,48},{48,56},{56,32},{64,72... | collective-permute-start | bytes 368648 | tf_op jit(solution)/shard_map/ppermute | solution.py:366
  7.0 0.9 %copy-start = (bf16[3,160,256]{2,1,0:T(8,128)(2,1)S(1)}, bf16[3,160,256]{2,1,0:T(8,128)(2,1)}, u32[]{:S(2)}) copy-start(bf16[3,160,256]{2,1,0:T(8,128)(2,1)} %constant.8.clone.matrix_ref) | copy-start | bytes 737284
  7.9 0.7 copy-start.1
  8.6 0.7 copy-start.3
  15.5 8.9 %collective-permute-start.3 = (bf16[2,80,768]{2,1,0:T(8,128)(2,1)S(1)}, bf16[2,80,768]{2,1,0:T(8,128)(2,1)S(1)}, u32[]{:S(2)}, u32[]{:S(2)}) collective-permute-start(bf16[2,80,768]{2,1,0:T(8,128)(2,1)S(1)} %pad_maximum_fusion.refs_0_), channel_id=1, source_target_pairs={{0,32},{8,40},{16,48},{24,56},{32,64},{40,72},{48,80},{56,88},{64,... | collective-permute-start | bytes 737288 | tf_op jit(solution)/shard_map/ppermute | solution.py:394
  17.1 8.9 %collective-permute-start.6 = (bf16[2,80,768]{2,1,0:T(8,128)(2,1)S(1)}, bf16[2,80,768]{2,1,0:T(8,128)(2,1)S(1)}, u32[]{:S(2)}, u32[]{:S(2)}) collective-permute-start(bf16[2,80,768]{2,1,0:T(8,128)(2,1)S(1)} %pad_maximum_fusion.1.refs_1_), channel_id=1, source_target_pairs={{0,96},{8,104},{16,112},{24,120},{32,0},{40,8},{48,16},{56,24},{64... | collective-permute-start | bytes 737288 | tf_op jit(solution)/shard_map/ppermute | solution.py:395
  17.6 12.1 %collective-permute-start.4 = (bf16[2,80,768]{2,1,0:T(8,128)(2,1)S(1)}, bf16[2,80,768]{2,1,0:T(8,128)(2,1)S(1)}, u32[]{:S(2)}, u32[]{:S(2)}) collective-permute-start(bf16[2,80,768]{2,1,0:T(8,128)(2,1)S(1)} %pad_maximum_fusion.1.refs_1_), channel_id=1, source_target_pairs={{0,32},{8,40},{16,48},{24,56},{32,64},{40,72},{48,80},{56,88},{64,... | collective-permute-start | bytes 737288 | tf_op jit(solution)/shard_map/ppermute | solution.py:394
  19.1 12.1 %collective-permute-start.5 = (bf16[2,80,768]{2,1,0:T(8,128)(2,1)S(1)}, bf16[2,80,768]{2,1,0:T(8,128)(2,1)S(1)}, u32[]{:S(2)}, u32[]{:S(2)}) collective-permute-start(bf16[2,80,768]{2,1,0:T(8,128)(2,1)S(1)} %pad_maximum_fusion.refs_0_), channel_id=1, source_target_pairs={{0,96},{8,104},{16,112},{24,120},{32,0},{40,8},{48,16},{56,24},{64... | collective-permute-start | bytes 737288 | tf_op jit(solution)/shard_map/ppermute | solution.py:395
  23.0 23.7 %copy-start.2 = (s32[640]{0:T(1024)S(1)}, s32[640]{0:T(1024)}, u32[]{:S(2)}) copy-start(s32[640]{0:T(1024)} %order_ref.3) | copy-start | bytes 7684
  23.0 47.9 %copy-start.4 = (bf16[2,640,128]{2,1,0:T(8,128)(2,1)S(1)}, bf16[2,640,128]{2,1,0:T(8,128)(2,1)}, u32[]{:S(2)}) copy-start(bf16[2,640,128]{2,1,0:T(8,128)(2,1)} %constant.10.clone.middle_ref) | copy-start | bytes 983044
  23.0 47.9 %copy-start.5 = (bf16[160,32]{1,0:T(8,128)(2,1)S(1)}, bf16[160,32]{1,0:T(8,128)(2,1)}, u32[]{:S(2)}) copy-start(bf16[160,32]{1,0:T(8,128)(2,1)} %constant.9.clone.expand_ref) | copy-start | bytes 30724
  25.9 7.7 %collective-permute-start.7 = (bf16[2,80,768]{2,1,0:T(8,128)(2,1)S(1)}, bf16[2,80,768]{2,1,0:T(8,128)(2,1)S(1)}, u32[]{:S(2)}, u32[]{:S(2)}) collective-permute-start(bf16[2,80,768]{2,1,0:T(8,128)(2,1)S(1)} %collective-permute-done.3.refs_2_), channel_id=1, source_target_pairs={{0,32},{8,40},{16,48},{24,56},{32,64},{40,72},{48,80},{56,88},{64,... | collective-permute-start | bytes 737288 | tf_op jit(solution)/shard_map/ppermute | solution.py:397
  27.1 7.7 %collective-permute-start.8 = (bf16[2,80,768]{2,1,0:T(8,128)(2,1)S(1)}, bf16[2,80,768]{2,1,0:T(8,128)(2,1)S(1)}, u32[]{:S(2)}, u32[]{:S(2)}) collective-permute-start(bf16[2,80,768]{2,1,0:T(8,128)(2,1)S(1)} %collective-permute-done.6.refs_5_), channel_id=1, source_target_pairs={{0,96},{8,104},{16,112},{24,120},{32,0},{40,8},{48,16},{56,24},{64... | collective-permute-start | bytes 737288 | tf_op jit(solution)/shard_map/ppermute | solution.py:397
  42.2 12.7 %all-to-all-start.1 = ((bf16[8,80,256]{2,1,0:T(8,128)(2,1)}), bf16[8,80,256]{2,1,0:T(8,128)(2,1)S(1)}, u32[]{:S(2)}, u32[]{:S(2)}) async-start(bf16[8,80,256]{2,1,0:T(8,128)(2,1)} %get-tuple-element.39), calls=%async_computation.1 | async-start | bytes 655360 | tf_op jit(solution)/shard_map/all_to_all | solution.py:424
  54.9 15.2 %all-to-all-start = ((bf16[8,80,512]{2,1,0:T(8,128)(2,1)}), bf16[8,80,512]{2,1,0:T(8,128)(2,1)S(1)}, u32[]{:S(2)}, u32[]{:S(2)}) async-start(bf16[8,80,512]{2,1,0:T(8,128)(2,1)} %get-tuple-element.38), calls=%async_computation | async-start | bytes 1310720 | tf_op jit(solution)/shard_map/all_to_all | solution.py:425
  59.0 11.9 %collective-permute-start.10 = (bf16[64,640]{1,0:T(8,128)(2,1)S(1)}, bf16[64,640]{1,0:T(8,128)(2,1)S(1)}, u32[]{:S(2)}, u32[]{:S(2)}) collective-permute-start(bf16[64,640]{1,0:T(8,128)(2,1)S(1)} %get-tuple-element.42), channel_id=1, source_target_pairs={{0,8},{8,16},{16,24},{24,32},{32,40},{40,48},{48,56},{56,64},{64,7... | collective-permute-start | bytes 245768 | tf_op jit(solution)/shard_map/ppermute | solution.py:439
  60.9 10.0 %collective-permute-start.9 = (bf16[64,640]{1,0:T(8,128)(2,1)S(1)}, bf16[64,640]{1,0:T(8,128)(2,1)S(1)}, u32[]{:S(2)}, u32[]{:S(2)}) collective-permute-start(bf16[64,640]{1,0:T(8,128)(2,1)S(1)} %get-tuple-element.41), channel_id=1, source_target_pairs={{8,0},{16,8},{24,16},{32,24},{40,32},{48,40},{56,48},{64,56},{72,6... | collective-permute-start | bytes 245768 | tf_op jit(solution)/shard_map/ppermute | solution.py:438
